TPU v7x, 512 devices: a whole 4x4x16 slice. The times are simulated.
512 devices in a mesh: space: 64 (over y, z), mem: 8 (over x, core).
Axes of the slice: x: 4, y: 4, z: 16, core: 2. Of those that a mesh axis runs over, the one named last changes fastest.
Arguments:
- prior_state: bfloat16 [256, 786432], P('mem', 'space'), may hold values from -6 to 6
- block_counts: int32 [2, 64], P(None, 'space'), may hold values from 1 to 4, 128 in all within a row
- block_index: int32 [2, 256], P(None, 'space'), may hold values from 0 to 95
- gate_operator: float32 [2, 256, 32, 128], P(None, 'space'), may hold values from -0.5 to 0.5
- observed: float32 [2, 8192], P(None, 'space'), may hold values from -8 to 8
- obs_error: float32 [2, 8192], P(None, 'space'), may hold values from 0.25 to 4
- local_mask: int32 [2, 6144, 20], P(None, 'space'), may hold values 0 or 1
Outputs:
- analysis: bfloat16 [256, 786432], P('mem', 'space')
Inputs may be any that keep to these rules, and one draw needn't show every extreme that they name: `block_counts`: in each batch the counts over all tiles sum to twice the number of tiles, and some tile holds exactly 4.
All inputs are finite; a program needn't handle non-finite values. No bound on the sum of `block_counts` or of `local_mask` on one device may be relied on, other than what follows from the above.
Results may differ from a plain program's by a relative error of at most 0.0055.
Values may be sent and summed in bfloat16 or wider, within the bound.
No kernel may reach another device: no remote copies, remote signals or barrier semaphores. Data moves between devices by JAX's collectives and lax.ppermute only.
A program may use at most 64 MiB of HBM per device.

v0:
```python
import jax
import jax.numpy as jnp
from jax import lax
from jax.sharding import PartitionSpec as P

MEMBER_TOTAL = 256
BLK = 128
OB = 32
SB = 96
BATCHES = 2
SLOTS = 128


def passed_along(value, axis, steps):
    count = lax.axis_size(axis)
    leading, last = (max(0, -steps), min(count, count - steps))
    return lax.ppermute(value, axis, [(source, source + steps) for source in range(leading, last)])


def wide_rim(packed):
    pieces = []
    for offset in (2, 1, -1, -2):
        pieces.append(passed_along(packed, "space", offset))
    return jnp.concatenate([pieces[0], pieces[1], packed, pieces[2], pieces[3]], axis=2)


def per_device(
    prior_state, block_counts, block_index, gate_operator, observed, obs_error, local_mask
):
    largest_value = lax.Precision.HIGHEST
    mem_dev = prior_state.shape[0]
    groups = lax.axis_size("mem")
    local_blocks = SB // groups
    start_block = lax.axis_index("mem") * local_blocks
    slot_block = jnp.arange(SLOTS) // OB
    state_now = prior_state
    for batch_id in range(BATCHES):
        blocks = state_now.reshape(mem_dev, SB, BLK)
        picked = jnp.take(blocks, block_index[batch_id], axis=1).astype(jnp.float32)
        prior = jnp.einsum(
            "mcb,cob->mco", picked, gate_operator[batch_id], precision=largest_value
        ).reshape(mem_dev, SLOTS)
        mean_obs = lax.psum(jnp.sum(prior, 0), "mem") / MEMBER_TOTAL
        spread = prior - mean_obs
        variance = lax.psum(jnp.sum(spread * spread, 0), "mem") / (MEMBER_TOTAL - 1)
        error_now = obs_error[batch_id]
        gain_term = 1.0 / (variance + error_now)
        shrink = gain_term / (1.0 + jnp.sqrt(error_now * gain_term))
        live_slot = slot_block < block_counts[batch_id, 0]
        weights = jnp.where(
            live_slot[None, :], gain_term * (observed[batch_id] - mean_obs) - shrink * spread, 0.0
        )
        packed = jnp.stack([spread, weights])
        neighbour_blocks = wide_rim(lax.all_gather(packed, "mem", axis=1, tiled=True))
        state_cells = lax.all_to_all(state_now, "mem", split_axis=1, concat_axis=0, tiled=True)
        mask_rows = lax.dynamic_slice_in_dim(
            local_mask[batch_id], start_block, local_blocks, 0
        ).astype(jnp.float32)
        cell_values = state_cells.astype(jnp.float32).reshape(MEMBER_TOTAL, local_blocks, BLK)
        member_deviation = cell_values - jnp.mean(cell_values, 0)
        cross_covariance = jnp.einsum(
            "qfi,qx->fix", member_deviation, neighbour_blocks[0], precision=largest_value
        ) / (MEMBER_TOTAL - 1)
        spread_block_mask = jnp.repeat(mask_rows, OB, axis=1)
        increment = jnp.einsum(
            "vn,xdn->vxd",
            neighbour_blocks[1],
            cross_covariance * spread_block_mask[:, None, :],
            precision=largest_value,
        )
        state_now = lax.all_to_all(
            (cell_values + increment)
            .reshape(MEMBER_TOTAL, local_blocks * BLK)
            .astype(jnp.bfloat16),
            "mem",
            split_axis=0,
            concat_axis=1,
            tiled=True,
        )
    return state_now


def solution(mesh):
    placed = (
        P("mem", "space"),
        P(None, "space"),
        P(None, "space"),
        P(None, "space", None, None),
        P(None, "space"),
        P(None, "space"),
        P(None, "space", None),
    )
    return jax.shard_map(
        per_device, mesh=mesh, in_specs=placed, out_specs=P("mem", "space"), check_vma=False
    )
```

profile of v0, /device:TPU:24, one launch (start us, length us, event | category | flops | bytes accessed | tf_op | source)
XLA Modules:
  0.0 234.1 jit_solution(4241601156830848557)
XLA Ops:
  0.0 0.8 compare_and_fusion
  0.8 1.3 copy_bitcast_fusion
  3.0 14.6 %psum.28 = f32[128]{0:T(128)S(1)} all-reduce(f32[128]{0:T(128)S(1)} %reduce_sum.63), channel_id=1, replica_groups=mesh['space'=64,'mem'=8] {'mem'}, use_global_device_ids=true, to_apply=%region_1.3 | all-reduce | flops 128 | bytes 1024 | tf_op jit(solution)/shard_map/psum | solution.py:43
  17.9 12.4 %psum.29 = f32[128]{0:T(128)S(1)} all-reduce(f32[128]{0:T(128)S(1)} %reduce_sum.65), channel_id=1, replica_groups=mesh['space'=64,'mem'=8] {'mem'}, use_global_device_ids=true, to_apply=%region_3.5 | all-reduce | flops 128 | bytes 1024 | tf_op jit(solution)/shard_map/psum | solution.py:45
  31.8 12.8 %all_gather.6 = f32[2,256,128]{2,1,0:T(8,128)S(1)} all-gather(f32[2,32,128]{2,1,0:T(8,128)S(1)} %pad_maximum_fusion), channel_id=1, replica_groups=mesh['space'=64,'mem'=8] {'mem'}, dimensions={1}, use_global_device_ids=true | all-gather | bytes 294912 | tf_op jit(solution)/shard_map/all_gather | solution.py:54
  44.6 5.2 %collective-permute-start = (f32[2,256,128]{2,1,0:T(8,128)S(1)}, f32[2,256,128]{2,1,0:T(8,128)S(1)}, u32[]{:S(2)}, u32[]{:S(2)}) collective-permute-start(f32[2,256,128]{2,1,0:T(8,128)S(1)} %all_gather.6), channel_id=1, source_target_pairs={{0,16},{8,24},{16,32},{24,40},{32,48},{40,56},{48,64},{56,72},{64,... | collective-permute-start | bytes 786440 | tf_op jit(solution)/shard_map/ppermute | solution.py:17
  49.8 3.8 %collective-permute-start.1 = (f32[2,256,128]{2,1,0:T(8,128)S(1)}, f32[2,256,128]{2,1,0:T(8,128)S(1)}, u32[]{:S(2)}, u32[]{:S(2)}) collective-permute-start(f32[2,256,128]{2,1,0:T(8,128)S(1)} %all_gather.6), channel_id=1, source_target_pairs={{0,8},{8,16},{16,24},{24,32},{32,40},{40,48},{48,56},{56,64},{64,7... | collective-permute-start | bytes 786440 | tf_op jit(solution)/shard_map/ppermute | solution.py:17
  53.6 6.4 %collective-permute-start.2 = (f32[2,256,128]{2,1,0:T(8,128)S(1)}, f32[2,256,128]{2,1,0:T(8,128)S(1)}, u32[]{:S(2)}, u32[]{:S(2)}) collective-permute-start(f32[2,256,128]{2,1,0:T(8,128)S(1)} %all_gather.6), channel_id=1, source_target_pairs={{8,0},{16,8},{24,16},{32,24},{40,32},{48,40},{56,48},{64,56},{72,6... | collective-permute-start | bytes 786440 | tf_op jit(solution)/shard_map/ppermute | solution.py:17
  60.0 4.8 %collective-permute-start.3 = (f32[2,256,128]{2,1,0:T(8,128)S(1)}, f32[2,256,128]{2,1,0:T(8,128)S(1)}, u32[]{:S(2)}, u32[]{:S(2)}) collective-permute-start(f32[2,256,128]{2,1,0:T(8,128)S(1)} %all_gather.6), channel_id=1, source_target_pairs={{16,0},{24,8},{32,16},{40,24},{48,32},{56,40},{64,48},{72,56},{80,... | collective-permute-start | bytes 786440 | tf_op jit(solution)/shard_map/ppermute | solution.py:17
  64.9 0.9 copy.56
  65.8 3.5 %all-to-all-start = ((bf16[32,8,1536]{2,0,1:T(8,128)(2,1)}), bf16[32,8,1536]{2,0,1:T(8,128)(2,1)S(1)}, u32[]{:S(2)}, u32[]{:S(2)}) async-start(bf16[32,8,1536]{2,0,1:T(8,128)(2,1)} %bitcast.112), calls=%async_computation | async-start | bytes 1572864 | tf_op jit(solution)/shard_map/all_to_all | solution.py:55
  69.9 0.7 constant_dynamic-update-slice_fusion.4
  70.6 3.6 %collective-permute-done.1 = f32[2,256,128]{2,1,0:T(8,128)S(1)} collective-permute-done((f32[2,256,128]{2,1,0:T(8,128)S(1)}, f32[2,256,128]{2,1,0:T(8,128)S(1)}, u32[]{:S(2)}, u32[]{:S(2)}) %collective-permute-start.1) | collective-permute-done | bytes 262176 | tf_op jit(solution)/shard_map/ppermute | solution.py:17
  74.9 0.8 constant_dynamic-update-slice_fusion.2
  76.4 1.0 collective-permute-done.3
  77.5 0.8 constant_dynamic-update-slice_fusion
  78.2 4.2 %all-to-all-done = bf16[32,8,1536]{2,0,1:T(8,128)(2,1)S(1)} async-done(((bf16[32,8,1536]{2,0,1:T(8,128)(2,1)}), bf16[32,8,1536]{2,0,1:T(8,128)(2,1)S(1)}, u32[]{:S(2)}, u32[]{:S(2)}) %all-to-all-start) | async-done | bytes 786464 | tf_op jit(solution)/shard_map/all_to_all | solution.py:55
  82.6 1.4 fusion.6
  84.0 1.5 sub.136
  85.5 1.3 convert_bitcast_fusion.1
  86.8 2.7 %reshape.370 = f32[256,12,128]{2,1,0:T(8,128)} reshape(f32[8,32,1536]{2,1,0:T(8,128)} %convert_bitcast_fusion.1) | data formatting | bytes 3145728 | tf_op jit(solution)/shard_map/convert_element_type | solution.py:59
  89.5 5.9 %fusion.12 = f32[12,128,640]{2,1,0:T(8,128)S(1)} fusion(f32[256,12,128]{2,1,0:T(8,128)S(1)} %sub.136, f32[2,256,640]{2,1,0:T(8,128)} %constant_dynamic-update-slice_fusion), kind=kOutput, calls=%fused_computation.22 | convolution fusion | flops 3019898880 | bytes 6160384 | tf_op jit(solution)/shard_map/qfi,qx->fix/dot_general | solution.py:61
  95.4 5.6 %fusion.11 = bf16[256,12,128]{2,0,1:T(8,128)(2,1)S(1)} fusion(f32[256,12,128]{2,1,0:T(8,128)S(1)} %copy-done, f32[12,128,640]{2,1,0:T(8,128)S(1)} %fusion.12, f32[12,640]{1,0:T(8,128)S(1)} %mul.92, f32[2,256,640]{2,1,0:T(8,128)} %constant_dynamic-update-slice_fusion), kind=kOutput, calls=%fused_computation.21 | convolution fusion | flops 3021668352 | bytes 6977536 | tf_op jit(solution)/shard_map/vn,xdn->vxd/dot_general | solution.py:65
  101.6 1.4 convert_element_type.60
  103.0 4.4 %all-to-all-start.1 = ((bf16[8,32,1536]{2,1,0:T(8,128)(2,1)}), bf16[8,32,1536]{2,1,0:T(8,128)(2,1)}, u32[]{:S(2)}, u32[]{:S(2)}) async-start(bf16[8,32,1536]{2,1,0:T(8,128)(2,1)} %convert_element_type.60), calls=%async_computation.1 | async-start | bytes 1572864 | tf_op jit(solution)/shard_map/all_to_all | solution.py:71
  108.1 12.3 %all-to-all-done.1 = bf16[8,32,1536]{2,1,0:T(8,128)(2,1)} async-done(((bf16[8,32,1536]{2,1,0:T(8,128)(2,1)}), bf16[8,32,1536]{2,1,0:T(8,128)(2,1)}, u32[]{:S(2)}, u32[]{:S(2)}) %all-to-all-start.1) | async-done | bytes 786464 | tf_op jit(solution)/shard_map/all_to_all | solution.py:71
  120.4 1.6 copy.29
  121.9 0.9 reshape.368
  124.1 12.8 %psum.30 = f32[128]{0:T(128)S(1)} all-reduce(f32[128]{0:T(128)S(1)} %reduce_sum.68), channel_id=1, replica_groups=mesh['space'=64,'mem'=8] {'mem'}, use_global_device_ids=true, to_apply=%region_6.8 | all-reduce | flops 128 | bytes 1024 | tf_op jit(solution)/shard_map/psum | solution.py:43
  137.1 12.4 %psum.31 = f32[128]{0:T(128)S(1)} all-reduce(f32[128]{0:T(128)S(1)} %reduce_sum.70), channel_id=1, replica_groups=mesh['space'=64,'mem'=8] {'mem'}, use_global_device_ids=true, to_apply=%region_8.10 | all-reduce | flops 128 | bytes 1024 | tf_op jit(solution)/shard_map/psum | solution.py:45
  149.7 12.8 %all_gather.7 = f32[2,256,128]{2,1,0:T(8,128)S(1)} all-gather(f32[2,32,128]{2,1,0:T(8,128)S(1)} %pad_maximum_fusion.1), channel_id=1, replica_groups=mesh['space'=64,'mem'=8] {'mem'}, dimensions={1}, use_global_device_ids=true | all-gather | bytes 294912 | tf_op jit(solution)/shard_map/all_gather | solution.py:54
  162.5 2.0 collective-permute-start.4
  164.6 2.4 %collective-permute-start.5 = (f32[2,256,128]{2,1,0:T(8,128)S(1)}, f32[2,256,128]{2,1,0:T(8,128)S(1)}, u32[]{:S(2)}, u32[]{:S(2)}) collective-permute-start(f32[2,256,128]{2,1,0:T(8,128)S(1)} %all_gather.7), channel_id=1, source_target_pairs={{0,8},{8,16},{16,24},{24,32},{32,40},{40,48},{48,56},{56,64},{64,7... | collective-permute-start | bytes 786440 | tf_op jit(solution)/shard_map/ppermute | solution.py:17
  167.0 3.6 %all-to-all-start.2 = ((bf16[32,8,1536]{2,0,1:T(8,128)(2,1)}), bf16[32,8,1536]{2,0,1:T(8,128)(2,1)S(1)}, u32[]{:S(2)}, u32[]{:S(2)}) async-start(bf16[32,8,1536]{2,0,1:T(8,128)(2,1)} %bitcast.14), calls=%async_computation.2 | async-start | bytes 1572864 | tf_op jit(solution)/shard_map/all_to_all | solution.py:55
  170.8 5.5 %collective-permute-start.6 = (f32[2,256,128]{2,1,0:T(8,128)S(1)}, f32[2,256,128]{2,1,0:T(8,128)S(1)}, u32[]{:S(2)}, u32[]{:S(2)}) collective-permute-start(f32[2,256,128]{2,1,0:T(8,128)S(1)} %all_gather.7), channel_id=1, source_target_pairs={{8,0},{16,8},{24,16},{32,24},{40,32},{48,40},{56,48},{64,56},{72,6... | collective-permute-start | bytes 786440 | tf_op jit(solution)/shard_map/ppermute | solution.py:17
  176.3 4.8 %collective-permute-start.7 = (f32[2,256,128]{2,1,0:T(8,128)S(1)}, f32[2,256,128]{2,1,0:T(8,128)S(1)}, u32[]{:S(2)}, u32[]{:S(2)}) collective-permute-start(f32[2,256,128]{2,1,0:T(8,128)S(1)} %all_gather.7), channel_id=1, source_target_pairs={{16,0},{24,8},{32,16},{40,24},{48,32},{56,40},{64,48},{72,56},{80,... | collective-permute-start | bytes 786440 | tf_op jit(solution)/shard_map/ppermute | solution.py:17
  181.8 4.5 %collective-permute-done.5 = f32[2,256,128]{2,1,0:T(8,128)S(1)} collective-permute-done((f32[2,256,128]{2,1,0:T(8,128)S(1)}, f32[2,256,128]{2,1,0:T(8,128)S(1)}, u32[]{:S(2)}, u32[]{:S(2)}) %collective-permute-start.5) | collective-permute-done | bytes 262176 | tf_op jit(solution)/shard_map/ppermute | solution.py:17
  187.0 0.8 constant_dynamic-update-slice_fusion.7
  188.5 6.8 %collective-permute-done.7 = f32[2,256,128]{2,1,0:T(8,128)S(1)} collective-permute-done((f32[2,256,128]{2,1,0:T(8,128)S(1)}, f32[2,256,128]{2,1,0:T(8,128)S(1)}, u32[]{:S(2)}, u32[]{:S(2)}) %collective-permute-start.7) | collective-permute-done | bytes 262176 | tf_op jit(solution)/shard_map/ppermute | solution.py:17
  195.3 0.8 constant_dynamic-update-slice_fusion.5
  196.2 1.4 fusion.7
  197.6 1.5 sub.148
  199.1 1.3 convert_bitcast_fusion
  200.4 2.7 %reshape.371 = f32[256,12,128]{2,1,0:T(8,128)} reshape(f32[8,32,1536]{2,1,0:T(8,128)} %convert_bitcast_fusion) | data formatting | bytes 3145728 | tf_op jit(solution)/shard_map/convert_element_type | solution.py:59
  203.1 5.9 %fusion.9 = f32[12,128,640]{2,1,0:T(8,128)S(1)} fusion(f32[256,12,128]{2,1,0:T(8,128)S(1)} %sub.148, f32[2,256,640]{2,1,0:T(8,128)} %constant_dynamic-update-slice_fusion.5), kind=kOutput, calls=%fused_computation.18 | convolution fusion | flops 3019898880 | bytes 6160384 | tf_op jit(solution)/shard_map/qfi,qx->fix/dot_general | solution.py:61
  209.0 5.6 %fusion.8 = bf16[256,12,128]{2,0,1:T(8,128)(2,1)S(1)} fusion(f32[256,12,128]{2,1,0:T(8,128)S(1)} %copy-done.1, f32[12,128,640]{2,1,0:T(8,128)S(1)} %fusion.9, f32[12,640]{1,0:T(8,128)S(1)} %mul.102, f32[2,256,640]{2,1,0:T(8,128)} %constant_dynamic-update-slice_fusion.5), kind=kOutput, calls=%fused_computation.17 | convolution fusion | flops 3021668352 | bytes 6977536 | tf_op jit(solution)/shard_map/vn,xdn->vxd/dot_general | solution.py:65
  215.7 17.5 %all_to_all.52 = bf16[8,32,1536]{2,1,0:T(8,128)(2,1)S(1)} all-to-all(bf16[8,32,1536]{2,1,0:T(8,128)(2,1)S(1)} %convert_element_type.67), channel_id=1, replica_groups=mesh['space'=64,'mem'=8] {'mem'}, dimensions={0} | all-to-all | bytes 1572864 | tf_op jit(solution)/shard_map/all_to_all | solution.py:71
  233.2 0.9 copy.43
  (74 shorter events, 11.2 us)
Async XLA Ops:
  0.0 64.9 %copy-start.2 = (bf16[32,12288]{1,0:T(8,128)(2,1)S(1)}, bf16[32,12288]{1,0:T(8,128)(2,1)}, u32[]{:S(2)}) copy-start(bf16[32,12288]{1,0:T(8,128)(2,1)} %param.9) | copy-start | bytes 2359300
  0.0 2.7 %copy-start.3 = (f32[2,4,32,128]{3,2,1,0:T(8,128)S(1)}, f32[2,4,32,128]{3,2,1,0:T(8,128)}, u32[]{:S(2)}) copy-start(f32[2,4,32,128]{3,2,1,0:T(8,128)} %param.12) | copy-start | bytes 393220
  0.0 30.3 %copy-start.7 = (f32[2,128]{1,0:T(2,128)S(1)}, f32[2,128]{1,0:T(2,128)}, u32[]{:S(2)}) copy-start(f32[2,128]{1,0:T(2,128)} %param.13) | copy-start | bytes 3076
  0.0 30.3 %copy-start.5 = (f32[2,128]{1,0:T(2,128)S(1)}, f32[2,128]{1,0:T(2,128)}, u32[]{:S(2)}) copy-start(f32[2,128]{1,0:T(2,128)} %param.14) | copy-start | bytes 3076
  0.0 30.4 %copy-start.6 = (s32[2,1]{0,1:T(1,128)S(1)}, s32[2,1]{0,1:T(1,128)}, u32[]{:S(2)}) copy-start(s32[2,1]{0,1:T(1,128)} %param.10) | copy-start | bytes 28
  44.6 25.3 %collective-permute-start = (f32[2,256,128]{2,1,0:T(8,128)S(1)}, f32[2,256,128]{2,1,0:T(8,128)S(1)}, u32[]{:S(2)}, u32[]{:S(2)}) collective-permute-start(f32[2,256,128]{2,1,0:T(8,128)S(1)} %all_gather.6), channel_id=1, source_target_pairs={{0,16},{8,24},{16,32},{24,40},{32,48},{40,56},{48,64},{56,72},{64,... | collective-permute-start | bytes 786440 | tf_op jit(solution)/shard_map/ppermute | solution.py:17
  49.8 24.4 %collective-permute-start.1 = (f32[2,256,128]{2,1,0:T(8,128)S(1)}, f32[2,256,128]{2,1,0:T(8,128)S(1)}, u32[]{:S(2)}, u32[]{:S(2)}) collective-permute-start(f32[2,256,128]{2,1,0:T(8,128)S(1)} %all_gather.6), channel_id=1, source_target_pairs={{0,8},{8,16},{16,24},{24,32},{32,40},{40,48},{48,56},{56,64},{64,7... | collective-permute-start | bytes 786440 | tf_op jit(solution)/shard_map/ppermute | solution.py:17
  53.6 22.1 %collective-permute-start.2 = (f32[2,256,128]{2,1,0:T(8,128)S(1)}, f32[2,256,128]{2,1,0:T(8,128)S(1)}, u32[]{:S(2)}, u32[]{:S(2)}) collective-permute-start(f32[2,256,128]{2,1,0:T(8,128)S(1)} %all_gather.6), channel_id=1, source_target_pairs={{8,0},{16,8},{24,16},{32,24},{40,32},{48,40},{56,48},{64,56},{72,6... | collective-permute-start | bytes 786440 | tf_op jit(solution)/shard_map/ppermute | solution.py:17
  60.0 17.4 %collective-permute-start.3 = (f32[2,256,128]{2,1,0:T(8,128)S(1)}, f32[2,256,128]{2,1,0:T(8,128)S(1)}, u32[]{:S(2)}, u32[]{:S(2)}) collective-permute-start(f32[2,256,128]{2,1,0:T(8,128)S(1)} %all_gather.6), channel_id=1, source_target_pairs={{16,0},{24,8},{32,16},{40,24},{48,32},{56,40},{64,48},{72,56},{80,... | collective-permute-start | bytes 786440 | tf_op jit(solution)/shard_map/ppermute | solution.py:17
  64.9 4.5 %copy-start.4 = (s32[2,96,20]{1,0,2:T(2,128)S(1)}, s32[2,96,20]{1,0,2:T(2,128)}, u32[]{:S(2)}) copy-start(s32[2,96,20]{1,0,2:T(2,128)} %param.15) | copy-start | bytes 46084
  65.8 16.6 %all-to-all-start = ((bf16[32,8,1536]{2,0,1:T(8,128)(2,1)}), bf16[32,8,1536]{2,0,1:T(8,128)(2,1)S(1)}, u32[]{:S(2)}, u32[]{:S(2)}) async-start(bf16[32,8,1536]{2,0,1:T(8,128)(2,1)} %bitcast.112), calls=%async_computation | async-start | bytes 1572864 | tf_op jit(solution)/shard_map/all_to_all | solution.py:55
  89.5 5.9 %copy-start = (f32[256,12,128]{2,1,0:T(8,128)S(1)}, f32[256,12,128]{2,1,0:T(8,128)}, u32[]{:S(2)}) copy-start(f32[256,12,128]{2,1,0:T(8,128)} %reshape.370) | copy-start | bytes 4718596
  103.0 17.4 %all-to-all-start.1 = ((bf16[8,32,1536]{2,1,0:T(8,128)(2,1)}), bf16[8,32,1536]{2,1,0:T(8,128)(2,1)}, u32[]{:S(2)}, u32[]{:S(2)}) async-start(bf16[8,32,1536]{2,1,0:T(8,128)(2,1)} %convert_element_type.60), calls=%async_computation.1 | async-start | bytes 1572864 | tf_op jit(solution)/shard_map/all_to_all | solution.py:71
  162.5 18.6 %collective-permute-start.4 = (f32[2,256,128]{2,1,0:T(8,128)S(1)}, f32[2,256,128]{2,1,0:T(8,128)S(1)}, u32[]{:S(2)}, u32[]{:S(2)}) collective-permute-start(f32[2,256,128]{2,1,0:T(8,128)S(1)} %all_gather.7), channel_id=1, source_target_pairs={{0,16},{8,24},{16,32},{24,40},{32,48},{40,56},{48,64},{56,72},{64,... | collective-permute-start | bytes 786440 | tf_op jit(solution)/shard_map/ppermute | solution.py:17
  164.6 21.7 %collective-permute-start.5 = (f32[2,256,128]{2,1,0:T(8,128)S(1)}, f32[2,256,128]{2,1,0:T(8,128)S(1)}, u32[]{:S(2)}, u32[]{:S(2)}) collective-permute-start(f32[2,256,128]{2,1,0:T(8,128)S(1)} %all_gather.7), channel_id=1, source_target_pairs={{0,8},{8,16},{16,24},{24,32},{32,40},{40,48},{48,56},{56,64},{64,7... | collective-permute-start | bytes 786440 | tf_op jit(solution)/shard_map/ppermute | solution.py:17
  167.0 29.1 %all-to-all-start.2 = ((bf16[32,8,1536]{2,0,1:T(8,128)(2,1)}), bf16[32,8,1536]{2,0,1:T(8,128)(2,1)S(1)}, u32[]{:S(2)}, u32[]{:S(2)}) async-start(bf16[32,8,1536]{2,0,1:T(8,128)(2,1)} %bitcast.14), calls=%async_computation.2 | async-start | bytes 1572864 | tf_op jit(solution)/shard_map/all_to_all | solution.py:55
  170.8 17.0 %collective-permute-start.6 = (f32[2,256,128]{2,1,0:T(8,128)S(1)}, f32[2,256,128]{2,1,0:T(8,128)S(1)}, u32[]{:S(2)}, u32[]{:S(2)}) collective-permute-start(f32[2,256,128]{2,1,0:T(8,128)S(1)} %all_gather.7), channel_id=1, source_target_pairs={{8,0},{16,8},{24,16},{32,24},{40,32},{48,40},{56,48},{64,56},{72,6... | collective-permute-start | bytes 786440 | tf_op jit(solution)/shard_map/ppermute | solution.py:17
  176.3 19.0 %collective-permute-start.7 = (f32[2,256,128]{2,1,0:T(8,128)S(1)}, f32[2,256,128]{2,1,0:T(8,128)S(1)}, u32[]{:S(2)}, u32[]{:S(2)}) collective-permute-start(f32[2,256,128]{2,1,0:T(8,128)S(1)} %all_gather.7), channel_id=1, source_target_pairs={{16,0},{24,8},{32,16},{40,24},{48,32},{56,40},{64,48},{72,56},{80,... | collective-permute-start | bytes 786440 | tf_op jit(solution)/shard_map/ppermute | solution.py:17
  203.1 5.9 %copy-start.1 = (f32[256,12,128]{2,1,0:T(8,128)S(1)}, f32[256,12,128]{2,1,0:T(8,128)}, u32[]{:S(2)}) copy-start(f32[256,12,128]{2,1,0:T(8,128)} %reshape.371) | copy-start | bytes 4718596
where the time goes:
time: 236 us; the launch traced here: 234 us
  blocking collectives  95.4 us (40%)
  starting transfers between devices  46.4 us (20%)
  waiting for transfers between devices  32.4 us (14%)
  local copies, waits for them, and re-layouts  28.1 us (12%)
  matrix products  23.5 us (10%)
  other arithmetic  7.95 us (3%)
    ppermute x8, starting transfers between devices, passed_along(): lax.ppermute(value, axis, [(source, source + steps) for source in range(l...  34.9 us
    psum x2, blocking collectives, per_device(): mean_obs = lax.psum(jnp.sum(prior, 0), 'mem') / MEMBER_TOTAL  27.4 us
    all_gather x2, blocking collectives, per_device(): lax.all_gather(packed, 'mem', axis=1, tiled=True)  25.7 us
    psum x2, blocking collectives, per_device(): variance = lax.psum(jnp.sum(spread * spread, 0), 'mem') / (MEMBER_TOTAL - 1)  24.8 us
    all_to_all x1, blocking collectives, per_device(): lax.all_to_all((cell_values + increment).reshape(MEMBER_TOTAL, local_bloc...  17.5 us
    ppermute x8, waiting for transfers between devices, passed_along(): lax.ppermute(value, axis, [(source, source + steps) for source in range(l...  15.9 us
    all_to_all x1, waiting for transfers between devices, per_device(): lax.all_to_all((cell_values + increment).reshape(MEMBER_TOTAL, local_bloc...  12.3 us
    dot_general x2, matrix products, per_device(): jnp.einsum('qfi,qx->fix', member_deviation, neighbour_blocks[0], precisio...  11.8 us
  transfers between devices with their start and end apart: 11, of which 6 were waited for; matrix products, arithmetic and copies ran while one was open for 4% of the time, Pallas kernels for 0%

commit v1 on v0

v1 whole, which is shorter than its diff:
```python
import jax
import jax.numpy as jnp
from jax import lax
from jax.experimental import pallas as pl
from jax.experimental.pallas import tpu as pltpu
from jax.sharding import PartitionSpec as P

MEMBERS = 256
BLK = 128
OB = 32
CAPB = 4
SB = 96
SLOTS = 128
BATCHES = 2
ROWS = 48
PACK = 272
F32 = jnp.float32
BF16 = jnp.bfloat16


def two_parts(value):
    high = value.astype(BF16).astype(F32)
    return high, value - high


def dot(a, b, dims):
    return lax.dot_general(a, b, (dims, ((), ())), preferred_element_type=F32)


def observe_kernel(index_ref, gate_ref, state_ref, out_ref, moved_ref, picks, sems, move_sems):
    groups, mem_dev, width = moved_ref.shape
    copies = []
    for k in range(BATCHES):
        for c in range(CAPB):
            n = k * CAPB + c
            start = pl.multiple_of(index_ref[k, c] * BLK, BLK)
            copies.append(
                pltpu.make_async_copy(state_ref.at[:, pl.ds(start, BLK)], picks.at[n], sems.at[n])
            )
    moves = [
        pltpu.make_async_copy(
            state_ref.at[:, pl.ds(g * width, width)], moved_ref.at[g], move_sems.at[g]
        )
        for g in range(groups)
    ]
    for copy in copies + moves:
        copy.start()
    high, low = two_parts(gate_ref[...].reshape(BATCHES * CAPB * OB, BLK))
    for copy in copies:
        copy.wait()
    rows = picks[...].reshape(BATCHES * CAPB * mem_dev, BLK)
    each = dot(rows, high.astype(BF16), ((1,), (1,))) + dot(rows, low.astype(BF16), ((1,), (1,)))
    lane_block = lax.broadcasted_iota(jnp.int32, (mem_dev, BATCHES * SLOTS), 1) // OB
    prior = jnp.zeros((mem_dev, BATCHES * SLOTS), F32)
    for n in range(BATCHES * CAPB):
        prior = jnp.where(lane_block == n, each[n * mem_dev : (n + 1) * mem_dev], prior)
    mean = jnp.sum(prior, 0, keepdims=True) / mem_dev
    mean_high, mean_low = two_parts(mean)
    spare = ROWS - mem_dev
    row = lax.broadcasted_iota(jnp.int32, (spare, BATCHES * SLOTS), 0)
    tail = jnp.where(row == 0, mean_high, jnp.where(row == 1, mean_low, 0.0))
    block = jnp.concatenate([prior - mean, tail], 0).astype(BF16)
    for g in range(groups):
        out_ref[g] = block
    for move in moves:
        move.wait()


def observe(block_index, gate_operator, prior_state, groups):
    mem_dev, cells = prior_state.shape
    return pl.pallas_call(
        observe_kernel,
        in_specs=[
            pl.BlockSpec(memory_space=pltpu.SMEM),
            pl.BlockSpec(memory_space=pltpu.VMEM),
            pl.BlockSpec(memory_space=pl.ANY),
        ],
        out_specs=[pl.BlockSpec(memory_space=pltpu.VMEM), pl.BlockSpec(memory_space=pl.ANY)],
        out_shape=[
            jax.ShapeDtypeStruct((groups, ROWS, BATCHES * SLOTS), BF16),
            jax.ShapeDtypeStruct((groups, mem_dev, cells // groups), BF16),
        ],
        scratch_shapes=[
            pltpu.VMEM((BATCHES * CAPB, mem_dev, BLK), BF16),
            pltpu.SemaphoreType.DMA((BATCHES * CAPB,)),
            pltpu.SemaphoreType.DMA((groups,)),
        ],
        name="observe",
    )(block_index, gate_operator, prior_state)


def members_of(shared_ref, batch_id):
    groups = shared_ref.shape[0]
    mem_dev = MEMBERS // groups
    lanes = slice(batch_id * SLOTS, (batch_id + 1) * SLOTS)
    parts = []
    for g in range(groups):
        block = shared_ref[g, :, lanes].astype(F32)
        parts.append(block[:mem_dev] + (block[mem_dev : mem_dev + 1] + block[mem_dev + 1 : mem_dev + 2]))
    return jnp.concatenate(parts, 0)


def store_packed(out_ref, prior, observed, error_now, live_count):
    mean_obs = jnp.sum(prior, 0, keepdims=True) / MEMBERS
    spread = prior - mean_obs
    variance = jnp.sum(spread * spread, 0, keepdims=True) / (MEMBERS - 1)
    gain = 1.0 / (variance + error_now)
    shrink = gain / (1.0 + jnp.sqrt(error_now * gain))
    live = lax.broadcasted_iota(jnp.int32, (1, SLOTS), 1) // OB < live_count
    level = jnp.where(live, gain * (observed - mean_obs), 0.0)
    slope = jnp.where(live, shrink, 0.0)
    level_high, level_low = two_parts(level)
    slope_high, slope_low = two_parts(slope)
    row = lax.broadcasted_iota(jnp.int32, (PACK - MEMBERS, SLOTS), 0)
    tail = jnp.where(
        row == 0,
        level_high,
        jnp.where(row == 1, level_low, jnp.where(row == 2, slope_high, jnp.where(row == 3, slope_low, 0.0))),
    )
    out_ref[:MEMBERS] = spread.astype(BF16)
    out_ref[MEMBERS:] = tail.astype(BF16)


def first_pack_kernel(counts_ref, shared_ref, observed_ref, error_ref, out_ref):
    store_packed(
        out_ref, members_of(shared_ref, 0), observed_ref[0:1], error_ref[0:1], counts_ref[0, 0]
    )


def window(own_ref, around_ref):
    return [
        (0, own_ref[...]),
        (-1, around_ref[0, 0]),
        (-2, around_ref[0, 1]),
        (1, around_ref[1, 0]),
        (2, around_ref[1, 1]),
    ]


def weights_of(pack):
    tail = pack[MEMBERS:].astype(F32)
    level = tail[0:1] + tail[1:2]
    slope = tail[2:3] + tail[3:4]
    return (level - slope * pack[:MEMBERS].astype(F32)).astype(BF16)


def turned(pack):
    return jnp.transpose(pack[:MEMBERS].astype(F32)).astype(BF16)


def second_pack_kernel(
    counts_ref, index_ref, mask_ref, shared_ref, own_ref, around_ref, observed_ref, error_ref, out_ref
):
    prior = members_of(shared_ref, 1)
    deviation = (prior - jnp.sum(prior, 0, keepdims=True) / MEMBERS).astype(BF16)
    lane_block = lax.broadcasted_iota(jnp.int32, (1, SLOTS), 1) // OB
    total = prior
    for offset, pack in window(own_ref, around_ref):
        covariance = dot(turned(pack), deviation, ((1,), (0,)))
        kept = []
        for c in range(CAPB):
            column = (offset + 2) * CAPB + c
            keep = jnp.zeros((1, SLOTS), F32)
            for b in range(CAPB):
                flag = mask_ref[0, index_ref[1, b], column].astype(F32) * (1.0 / (MEMBERS - 1))
                keep = jnp.where(lane_block == b, flag, keep)
            kept.append(covariance[c * OB : (c + 1) * OB] * keep)
        kept = jnp.concatenate(kept, 0).astype(BF16)
        total = total + dot(weights_of(pack), kept, ((1,), (0,)))
    store_packed(out_ref, total, observed_ref[1:2], error_ref[1:2], counts_ref[1, 0])


def update_kernel(batch_id, place_ref, mask_ref, own_ref, around_ref, state_ref, out_ref, turned_ref, weights_ref):
    tiles = window(own_ref, around_ref)
    for n, (_, pack) in enumerate(tiles):
        turned_ref[n * SLOTS : (n + 1) * SLOTS] = turned(pack)
        weights_ref[:, n * SLOTS : (n + 1) * SLOTS] = weights_of(pack)
    cells = state_ref.shape[1]
    first = place_ref[0] * (cells // BLK)
    step = 2 * BLK
    for at in range(0, cells, step):
        values = state_ref[:, at : at + step].astype(F32)
        mean = jnp.sum(values, 0, keepdims=True) / MEMBERS
        covariance = dot(turned_ref[...], (values - mean).astype(BF16), ((1,), (0,)))
        rows = []
        for n, (offset, _) in enumerate(tiles):
            for c in range(CAPB):
                row = covariance[n * SLOTS + c * OB : n * SLOTS + (c + 1) * OB]
                halves = []
                for h in range(2):
                    block = first + (at // BLK + h)
                    flag = mask_ref[batch_id, block, (offset + 2) * CAPB + c].astype(F32) * (
                        1.0 / (MEMBERS - 1)
                    )
                    halves.append(row[:, h * BLK : (h + 1) * BLK] * flag)
                rows.append(jnp.concatenate(halves, 1))
        kept = jnp.concatenate(rows, 0).astype(BF16)
        increment = dot(weights_ref[...], kept, ((1,), (0,)))
        out_ref[:, at : at + step] = (values + increment).astype(BF16)


VM = pl.BlockSpec(memory_space=pltpu.VMEM)
SM = pl.BlockSpec(memory_space=pltpu.SMEM)


def first_pack(counts, shared, observed, errors):
    return pl.pallas_call(
        first_pack_kernel,
        in_specs=[SM, VM, VM, VM],
        out_specs=VM,
        out_shape=jax.ShapeDtypeStruct((PACK, SLOTS), BF16),
        name="first_pack",
    )(counts, shared, observed, errors)


def second_pack(counts, index, mask, shared, own, around, observed, errors):
    return pl.pallas_call(
        second_pack_kernel,
        in_specs=[SM, SM, SM, VM, VM, VM, VM, VM],
        out_specs=VM,
        out_shape=jax.ShapeDtypeStruct((PACK, SLOTS), BF16),
        name="second_pack",
    )(counts, index, mask, shared, own, around, observed, errors)


def update(batch_id, place, mask, own, around, state):
    return pl.pallas_call(
        lambda *refs: update_kernel(batch_id, *refs),
        in_specs=[SM, SM, VM, VM, VM],
        out_specs=VM,
        out_shape=jax.ShapeDtypeStruct(state.shape, BF16),
        scratch_shapes=[pltpu.VMEM((5 * SLOTS, MEMBERS), BF16), pltpu.VMEM((MEMBERS, 5 * SLOTS), BF16)],
        compiler_params=pltpu.CompilerParams(vmem_limit_bytes=32 * 1024 * 1024),
        name="update",
    )(place, mask, own, around, state)


def shared_around(pack):
    tiles, groups = lax.axis_size("space"), lax.axis_size("mem")
    received = []
    for offset in (1, 2):
        pairs = []
        for tile in range(tiles):
            for m in range(groups):
                target = tile + offset if m % 2 == 0 else tile - offset
                if 0 <= target < tiles:
                    pairs.append((tile * groups + m, target * groups + m))
        received.append(lax.ppermute(pack, ("space", "mem"), pairs))
    chips = [[2 * chip, 2 * chip + 1] for chip in range(groups // 2)]
    return lax.all_gather(jnp.stack(received), "mem", axis=0, axis_index_groups=chips)


def per_device(prior_state, block_counts, block_index, gate_operator, observed, obs_error, local_mask):
    groups = lax.axis_size("mem")
    mem_dev, cells = prior_state.shape
    place = lax.axis_index("mem").astype(jnp.int32).reshape(1)
    own_block, moved = observe(block_index, gate_operator, prior_state, groups)
    shared = lax.all_to_all(own_block, "mem", split_axis=0, concat_axis=0, tiled=True)
    state = lax.all_to_all(moved, "mem", split_axis=0, concat_axis=0, tiled=True)
    state = state.reshape(MEMBERS, cells // groups)
    pack = first_pack(block_counts, shared, observed, obs_error)
    around = shared_around(pack)
    next_pack = second_pack(
        block_counts, block_index, local_mask, shared, pack, around, observed, obs_error
    )
    state = update(0, place, local_mask, pack, around, state)
    next_around = shared_around(next_pack)
    state = update(1, place, local_mask, next_pack, next_around, state)
    parts = lax.all_to_all(
        state.reshape(groups, mem_dev, cells // groups), "mem", split_axis=0, concat_axis=0, tiled=True
    )
    return parts.transpose(1, 0, 2).reshape(mem_dev, cells)


def solution(mesh):
    placed = (
        P("mem", "space"),
        P(None, "space"),
        P(None, "space"),
        P(None, "space", None, None),
        P(None, "space"),
        P(None, "space"),
        P(None, "space", None),
    )
    return jax.shard_map(
        per_device, mesh=mesh, in_specs=placed, out_specs=P("mem", "space"), check_vma=False
    )
```

time: 236 us -> 106 us (0.45)
  blocking collectives: 95.4 us -> 34.1 us
  Pallas kernels: 0 us -> 39.3 us
  starting transfers between devices: 46.4 us -> 17.5 us
  local copies, waits for them, and re-layouts: 28.1 us -> 2.36 us
  matrix products: 23.5 us -> 0 us
  waiting for transfers between devices: 32.4 us -> 12.3 us
  other arithmetic: 7.95 us -> 0.03 us
    psum x4 -> x0, blocking collectives: 52.2 us -> none  [the longest x2 27.4 us: per_device(): mean_obs = lax.psum(jnp.sum(prior, 0), 'mem') / MEMBER_TOTAL]
    pallas_call x0 -> x5, Pallas kernels: none -> 39.3 us  [the longest x1 26.7 us: observe(): pl.pallas_call(observe_kernel, in_specs=[pl.BlockSpec(memory_space=pltpu....]
    dot_general x6 -> x0, matrix products: 23.5 us -> none  [the longest x2 11.8 us: per_device(): jnp.einsum('qfi,qx->fix', member_deviation, neighbour_blocks[0], precisio...]
    ppermute x8 -> x4, starting transfers between devices: 34.9 us -> 13.8 us  [shared_around(): received.append(lax.ppermute(pack, ('space', 'mem'), pairs))]
    all_gather x2, blocking collectives: 25.7 us -> 5.33 us  [shared_around(): lax.all_gather(jnp.stack(received), 'mem', axis=0, axis_index_groups=chips)]
    all_to_all x3 -> x1, waiting for transfers between devices: 16.5 us -> 0.01 us  [per_device(): lax.all_to_all(moved, 'mem', split_axis=0, concat_axis=0, tiled=True)]
    all_to_all x1 -> x2, blocking collectives: 17.5 us -> 28.8 us  [the longest x1 17.5 us: per_device(): lax.all_to_all(state.reshape(groups, mem_dev, cells // groups), 'mem', sp...]
    convert_element_type x6 -> x0, local copies, waits for them, and re-layouts: 8.41 us -> none  [the longest x2 5.39 us: per_device(): state_cells.astype(jnp.float32).reshape(MEMBER_TOTAL, local_blocks, BLK)]
  transfers between devices with their start and end apart: 11 -> 5, of which waited for: 6 -> 4; matrix products, arithmetic and copies ran while one was open for 4% -> 1% of each run, Pallas kernels for 0% -> 5%
where the time goes in v1:
time: 106 us
  Pallas kernels  39.3 us (37%)
  blocking collectives  34.1 us (32%)
  starting transfers between devices  17.5 us (17%)
  waiting for transfers between devices  12.3 us (12%)
  local copies, waits for them, and re-layouts  2.36 us (2%)
    pallas_call x1, Pallas kernels, observe(): pl.pallas_call(observe_kernel, in_specs=[pl.BlockSpec(memory_space=pltpu....  26.7 us
    all_to_all x1, blocking collectives, per_device(): lax.all_to_all(state.reshape(groups, mem_dev, cells // groups), 'mem', sp...  17.5 us
    ppermute x4, starting transfers between devices, shared_around(): received.append(lax.ppermute(pack, ('space', 'mem'), pairs))  13.8 us
    ppermute x4, waiting for transfers between devices, shared_around(): received.append(lax.ppermute(pack, ('space', 'mem'), pairs))  12.3 us
    all_to_all x1, blocking collectives, per_device(): lax.all_to_all(own_block, 'mem', split_axis=0, concat_axis=0, tiled=True)  11.3 us
    pallas_call x2, Pallas kernels, update(): pl.pallas_call(lambda *refs: update_kernel(batch_id, *refs), in_specs=[SM...  7.22 us
    all_gather x2, blocking collectives, shared_around(): lax.all_gather(jnp.stack(received), 'mem', axis=0, axis_index_groups=chips)  5.33 us
    pallas_call x1, Pallas kernels, second_pack(): pl.pallas_call(second_pack_kernel, in_specs=[SM, SM, SM, VM, VM, VM, VM,...  3.69 us
  transfers between devices with their start and end apart: 5, of which 4 were waited for; matrix products, arithmetic and copies ran while one was open for 1% of the time, Pallas kernels for 5%

profile of v1, /device:TPU:24, one launch (start us, length us, event | category | flops | bytes accessed | tf_op | source)
XLA Modules:
  0.0 105.7 jit_solution(13625296289439982140)
XLA Ops:
  0.0 26.7 %observe.1 = (bf16[8,48,256]{2,1,0:T(8,128)(2,1)}, bf16[8,32,1536]{2,1,0:T(8,128)(2,1)}) custom-call(s32[2,4]{1,0:T(2,128)} %index_ref.3, f32[2,4,32,128]{3,2,1,0:T(8,128)} %gate_ref.1, bf16[32,12288]{1,0:T(8,128)(2,1)} %state_ref.1), custom_call_target="tpu_custom_call" | custom-call | tf_op jit(solution)/shard_map/observe/pallas_call | solution.py:71
  26.7 11.3 %all_to_all.15.shared_ref = bf16[8,48,256]{2,1,0:T(8,128)(2,1)} all-to-all(bf16[8,48,256]{2,1,0:T(8,128)(2,1)} %get-tuple-element.7), channel_id=1, replica_groups=mesh['space'=64,'mem'=8] {'mem'}, dimensions={0} | all-to-all | bytes 393216 | tf_op jit(solution)/shard_map/all_to_all | solution.py:258
  37.9 0.0 copy-start.5
  37.9 3.7 %all-to-all-start.1 = ((bf16[8,32,1536]{2,1,0:T(8,128)(2,1)}), bf16[8,32,1536]{2,1,0:T(8,128)(2,1)S(1)}, u32[]{:S(2)}, u32[]{:S(2)}) async-start(bf16[8,32,1536]{2,1,0:T(8,128)(2,1)} %get-tuple-element.8), calls=%async_computation.1 | async-start | bytes 1572864 | tf_op jit(solution)/shard_map/all_to_all | solution.py:259
  41.6 0.0 copy-done.5
  41.6 0.7 copy.15.counts_ref
  42.3 0.0 copy-start.4
  42.3 1.7 %first_pack.1.own_ref.refs_2_ = bf16[272,128]{1,0:T(8,128)(2,1)} custom-call(s32[2,1]{1,0:T(2,128)} %copy.15.counts_ref, bf16[8,48,256]{2,1,0:T(8,128)(2,1)} %all_to_all.15.shared_ref, f32[2,128]{1,0:T(2,128)} %observed_ref.3, f32[2,128]{1,0:T(2,128)} %error_ref.3), custom_call_target="tpu_custom_call" | custom-call | tf_op jit(solution)/shard_map/first_pack/pallas_call | solution.py:207
  44.0 5.2 %collective-permute-start.1 = (bf16[272,128]{1,0:T(8,128)(2,1)}, bf16[272,128]{1,0:T(8,128)(2,1)S(1)}, u32[]{:S(2)}, u32[]{:S(2)}) collective-permute-start(bf16[272,128]{1,0:T(8,128)(2,1)} %first_pack.1.own_ref.refs_2_), channel_id=1, source_target_pairs={{0,16},{2,18},{4,20},{6,22},{8,24},{10,26},{12,28},{14,30},{16,32}... | collective-permute-start | bytes 208904 | tf_op jit(solution)/shard_map/ppermute | solution.py:248
  49.2 3.8 %collective-permute-start = (bf16[272,128]{1,0:T(8,128)(2,1)}, bf16[272,128]{1,0:T(8,128)(2,1)S(1)}, u32[]{:S(2)}, u32[]{:S(2)}) collective-permute-start(bf16[272,128]{1,0:T(8,128)(2,1)} %first_pack.1.own_ref.refs_2_), channel_id=1, source_target_pairs={{0,8},{2,10},{4,12},{6,14},{8,16},{9,1},{10,18},{11,3},{12,20},{13... | collective-permute-start | bytes 208904 | tf_op jit(solution)/shard_map/ppermute | solution.py:248
  53.0 0.0 copy-done.4
  53.0 0.7 copy.18.mask_ref.refs_1_
  53.8 4.9 %collective-permute-done.1 = bf16[272,128]{1,0:T(8,128)(2,1)S(1)} collective-permute-done((bf16[272,128]{1,0:T(8,128)(2,1)}, bf16[272,128]{1,0:T(8,128)(2,1)S(1)}, u32[]{:S(2)}, u32[]{:S(2)}) %collective-permute-start.1) | collective-permute-done | bytes 69664 | tf_op jit(solution)/shard_map/ppermute | solution.py:248
  58.6 1.4 %collective-permute-done = bf16[272,128]{1,0:T(8,128)(2,1)S(1)} collective-permute-done((bf16[272,128]{1,0:T(8,128)(2,1)}, bf16[272,128]{1,0:T(8,128)(2,1)S(1)}, u32[]{:S(2)}, u32[]{:S(2)}) %collective-permute-start) | collective-permute-done | bytes 69664 | tf_op jit(solution)/shard_map/ppermute | solution.py:248
  60.0 3.2 %all-gather = bf16[4,272,128]{2,1,0:T(8,128)(2,1)} all-gather(bf16[2,272,128]{2,1,0:T(8,128)(2,1)S(1)} %pad_maximum_fusion), channel_id=2, replica_groups={{0,1},{2,3},{4,5},{6,7},{8,9},{10,11},{12,13},{14,15},{16,17},{18,19},{..., dimensions={0}, use_global_device_ids=true | all-gather | bytes 417792 | tf_op jit(solution)/shard_map/all_gather | solution.py:250
  63.2 3.7 %second_pack.1.refs_2_ = bf16[272,128]{1,0:T(8,128)(2,1)} custom-call(s32[2,1]{1,0:T(2,128)} %copy.15.counts_ref, s32[2,4]{1,0:T(2,128)} %index_ref.3, s32[2,96,20]{2,1,0:T(8,128)} %copy.18.mask_ref.refs_1_, bf16[8,48,256]{2,1,0:T(8,128)(2,1)} %all_to_all.15.shared_ref, bf16[272,128]{1,0:T(8,128)(2,1)} %first_pack.1.own_ref.refs_2_, ...), custom_call_target="tpu_custom_call" | custom-call | tf_op jit(solution)/shard_map/second_pack/pallas_call | solution.py:217
  66.9 2.4 %collective-permute-start.3 = (bf16[272,128]{1,0:T(8,128)(2,1)}, bf16[272,128]{1,0:T(8,128)(2,1)S(1)}, u32[]{:S(2)}, u32[]{:S(2)}) collective-permute-start(bf16[272,128]{1,0:T(8,128)(2,1)} %second_pack.1.refs_2_), channel_id=1, source_target_pairs={{0,16},{2,18},{4,20},{6,22},{8,24},{10,26},{12,28},{14,30},{16,32}... | collective-permute-start | bytes 208904 | tf_op jit(solution)/shard_map/ppermute | solution.py:248
  69.3 2.4 %collective-permute-start.2 = (bf16[272,128]{1,0:T(8,128)(2,1)}, bf16[272,128]{1,0:T(8,128)(2,1)S(1)}, u32[]{:S(2)}, u32[]{:S(2)}) collective-permute-start(bf16[272,128]{1,0:T(8,128)(2,1)} %second_pack.1.refs_2_), channel_id=1, source_target_pairs={{0,8},{2,10},{4,12},{6,14},{8,16},{9,1},{10,18},{11,3},{12,20},{13... | collective-permute-start | bytes 208904 | tf_op jit(solution)/shard_map/ppermute | solution.py:248
  71.7 4.7 %collective-permute-done.3 = bf16[272,128]{1,0:T(8,128)(2,1)S(1)} collective-permute-done((bf16[272,128]{1,0:T(8,128)(2,1)}, bf16[272,128]{1,0:T(8,128)(2,1)S(1)}, u32[]{:S(2)}, u32[]{:S(2)}) %collective-permute-start.3) | collective-permute-done | bytes 69664 | tf_op jit(solution)/shard_map/ppermute | solution.py:248
  76.4 1.4 %collective-permute-done.2 = bf16[272,128]{1,0:T(8,128)(2,1)S(1)} collective-permute-done((bf16[272,128]{1,0:T(8,128)(2,1)}, bf16[272,128]{1,0:T(8,128)(2,1)S(1)}, u32[]{:S(2)}, u32[]{:S(2)}) %collective-permute-start.2) | collective-permute-done | bytes 69664 | tf_op jit(solution)/shard_map/ppermute | solution.py:248
  77.8 0.0 copy-start.2
  77.8 0.0 copy-start
  77.9 0.0 copy-start.1
  77.9 2.1 %all-gather.1 = bf16[4,272,128]{2,1,0:T(8,128)(2,1)S(1)} all-gather(bf16[2,272,128]{2,1,0:T(8,128)(2,1)S(1)} %pad_maximum_fusion.1), channel_id=3, replica_groups={{0,1},{2,3},{4,5},{6,7},{8,9},{10,11},{12,13},{14,15},{16,17},{18,19},{..., dimensions={0}, use_global_device_ids=true | all-gather | bytes 417792 | tf_op jit(solution)/shard_map/all_gather | solution.py:250
  80.0 0.0 all-to-all-done.1
  80.0 0.0 copy-done.2
  80.0 0.0 copy-done
  80.0 0.0 copy-done.1
  80.0 0.0 copy-start.3
  80.0 3.6 %update.2.refs_4_ = bf16[256,1536]{1,0:T(8,128)(2,1)S(1)} custom-call(s32[1]{0:T(128)} %bitcast.refs_0_, s32[2,96,20]{2,1,0:T(8,128)S(1)} %copy-done.1, bf16[272,128]{1,0:T(8,128)(2,1)S(1)} %copy-done.2, bf16[2,2,272,128]{3,2,1,0:T(8,128)(2,1)S(1)} %bitcast.15, bf16[256,1536]{1,0:T(8,128)(2,1)S(1)} %bitcast.12), custom_call_target="tpu_custom_call" | custom-call | tf_op jit(solution)/shard_map/update/pallas_call | solution.py:227
  83.7 0.0 copy-done.3
  83.7 3.6 %update.3 = bf16[256,1536]{1,0:T(8,128)(2,1)S(1)} custom-call(s32[1]{0:T(128)} %bitcast.refs_0_, s32[2,96,20]{2,1,0:T(8,128)S(1)} %copy-done.1, bf16[272,128]{1,0:T(8,128)(2,1)S(1)} %copy-done.3, bf16[2,2,272,128]{3,2,1,0:T(8,128)(2,1)S(1)} %bitcast.16, bf16[256,1536]{1,0:T(8,128)(2,1)S(1)} %update.2.refs_4_), custom_call_target="tpu_custom_call" | custom-call | tf_op jit(solution)/shard_map/update/pallas_call | solution.py:227
  87.3 17.5 %all_to_all.16 = bf16[8,32,1536]{2,1,0:T(8,128)(2,1)S(1)} all-to-all(bf16[8,32,1536]{2,1,0:T(8,128)(2,1)S(1)} %bitcast.13), channel_id=1, replica_groups=mesh['space'=64,'mem'=8] {'mem'}, dimensions={0} | all-to-all | bytes 1572864 | tf_op jit(solution)/shard_map/all_to_all | solution.py:269
  104.8 0.9 copy.20
  (2 shorter events, 0.0 us)
Async XLA Ops:
  37.9 3.7 %copy-start.5 = (s32[2,1]{0,1:T(1,128)S(1)}, s32[2,1]{0,1:T(1,128)}, u32[]{:S(2)}) copy-start(s32[2,1]{0,1:T(1,128)} %param.8) | copy-start | bytes 28
  37.9 42.1 %all-to-all-start.1 = ((bf16[8,32,1536]{2,1,0:T(8,128)(2,1)}), bf16[8,32,1536]{2,1,0:T(8,128)(2,1)S(1)}, u32[]{:S(2)}, u32[]{:S(2)}) async-start(bf16[8,32,1536]{2,1,0:T(8,128)(2,1)} %get-tuple-element.8), calls=%async_computation.1 | async-start | bytes 1572864 | tf_op jit(solution)/shard_map/all_to_all | solution.py:259
  42.3 10.7 %copy-start.4 = (s32[2,96,20]{1,0,2:T(2,128)S(1)}, s32[2,96,20]{1,0,2:T(2,128)}, u32[]{:S(2)}) copy-start(s32[2,96,20]{1,0,2:T(2,128)} %param.13) | copy-start | bytes 46084
  44.0 14.6 %collective-permute-start.1 = (bf16[272,128]{1,0:T(8,128)(2,1)}, bf16[272,128]{1,0:T(8,128)(2,1)S(1)}, u32[]{:S(2)}, u32[]{:S(2)}) collective-permute-start(bf16[272,128]{1,0:T(8,128)(2,1)} %first_pack.1.own_ref.refs_2_), channel_id=1, source_target_pairs={{0,16},{2,18},{4,20},{6,22},{8,24},{10,26},{12,28},{14,30},{16,32}... | collective-permute-start | bytes 208904 | tf_op jit(solution)/shard_map/ppermute | solution.py:248
  49.2 10.8 %collective-permute-start = (bf16[272,128]{1,0:T(8,128)(2,1)}, bf16[272,128]{1,0:T(8,128)(2,1)S(1)}, u32[]{:S(2)}, u32[]{:S(2)}) collective-permute-start(bf16[272,128]{1,0:T(8,128)(2,1)} %first_pack.1.own_ref.refs_2_), channel_id=1, source_target_pairs={{0,8},{2,10},{4,12},{6,14},{8,16},{9,1},{10,18},{11,3},{12,20},{13... | collective-permute-start | bytes 208904 | tf_op jit(solution)/shard_map/ppermute | solution.py:248
  66.9 9.5 %collective-permute-start.3 = (bf16[272,128]{1,0:T(8,128)(2,1)}, bf16[272,128]{1,0:T(8,128)(2,1)S(1)}, u32[]{:S(2)}, u32[]{:S(2)}) collective-permute-start(bf16[272,128]{1,0:T(8,128)(2,1)} %second_pack.1.refs_2_), channel_id=1, source_target_pairs={{0,16},{2,18},{4,20},{6,22},{8,24},{10,26},{12,28},{14,30},{16,32}... | collective-permute-start | bytes 208904 | tf_op jit(solution)/shard_map/ppermute | solution.py:248
  69.3 8.5 %collective-permute-start.2 = (bf16[272,128]{1,0:T(8,128)(2,1)}, bf16[272,128]{1,0:T(8,128)(2,1)S(1)}, u32[]{:S(2)}, u32[]{:S(2)}) collective-permute-start(bf16[272,128]{1,0:T(8,128)(2,1)} %second_pack.1.refs_2_), channel_id=1, source_target_pairs={{0,8},{2,10},{4,12},{6,14},{8,16},{9,1},{10,18},{11,3},{12,20},{13... | collective-permute-start | bytes 208904 | tf_op jit(solution)/shard_map/ppermute | solution.py:248
  77.8 2.2 %copy-start.2 = (bf16[272,128]{1,0:T(8,128)(2,1)S(1)}, bf16[272,128]{1,0:T(8,128)(2,1)}, u32[]{:S(2)}) copy-start(bf16[272,128]{1,0:T(8,128)(2,1)} %first_pack.1.own_ref.refs_2_) | copy-start | bytes 208900
  77.8 2.2 %copy-start = (bf16[4,272,128]{2,1,0:T(8,128)(2,1)S(1)}, bf16[4,272,128]{2,1,0:T(8,128)(2,1)}, u32[]{:S(2)}) copy-start(bf16[4,272,128]{2,1,0:T(8,128)(2,1)} %all-gather) | copy-start | bytes 835588
  77.9 2.2 %copy-start.1 = (s32[2,96,20]{2,1,0:T(8,128)S(1)}, s32[2,96,20]{2,1,0:T(8,128)}, u32[]{:S(2)}) copy-start(s32[2,96,20]{2,1,0:T(8,128)} %copy.18.mask_ref.refs_1_) | copy-start | bytes 46084
  80.0 3.6 %copy-start.3 = (bf16[272,128]{1,0:T(8,128)(2,1)S(1)}, bf16[272,128]{1,0:T(8,128)(2,1)}, u32[]{:S(2)}) copy-start(bf16[272,128]{1,0:T(8,128)(2,1)} %second_pack.1.refs_2_) | copy-start | bytes 208900

commit v2 on v1

v2 whole, which is shorter than its diff:
```python
import jax
import jax.numpy as jnp
from jax import lax
from jax.experimental import pallas as pl
from jax.experimental.pallas import tpu as pltpu
from jax.sharding import PartitionSpec as P

MEMBERS = 256
BLK = 128
OB = 32
CAPB = 4
SB = 96
SLOTS = 128
BATCHES = 2
ROWS = 48
PACK = 272
F32 = jnp.float32
BF16 = jnp.bfloat16


def two_parts(value):
    high = value.astype(BF16).astype(F32)
    return high, value - high


def dot(a, b, dims):
    return lax.dot_general(a, b, (dims, ((), ())), preferred_element_type=F32)


def observe_kernel(index_ref, gate_ref, state_ref, out_ref, moved_ref):
    groups, mem_dev, width = moved_ref.shape
    high, low = two_parts(gate_ref[...].reshape(BATCHES * CAPB * OB, BLK))
    picks = []
    for k in range(BATCHES):
        for c in range(CAPB):
            start = pl.multiple_of(index_ref[k, c] * BLK, BLK)
            picks.append(state_ref[:, pl.ds(start, BLK)])
    rows = jnp.concatenate(picks, 0)
    each = dot(rows, high.astype(BF16), ((1,), (1,))) + dot(rows, low.astype(BF16), ((1,), (1,)))
    lane_block = lax.broadcasted_iota(jnp.int32, (mem_dev, BATCHES * SLOTS), 1) // OB
    prior = jnp.zeros((mem_dev, BATCHES * SLOTS), F32)
    for n in range(BATCHES * CAPB):
        prior = jnp.where(lane_block == n, each[n * mem_dev : (n + 1) * mem_dev], prior)
    mean = jnp.sum(prior, 0, keepdims=True) / mem_dev
    mean_high, mean_low = two_parts(mean)
    spare = ROWS - mem_dev
    row = lax.broadcasted_iota(jnp.int32, (spare, BATCHES * SLOTS), 0)
    tail = jnp.where(row == 0, mean_high, jnp.where(row == 1, mean_low, 0.0))
    block = jnp.concatenate([prior - mean, tail], 0).astype(BF16)
    for g in range(groups):
        out_ref[g] = block
        moved_ref[g] = state_ref[:, g * width : (g + 1) * width]


def members_of(shared_ref, batch_id):
    groups = shared_ref.shape[0]
    mem_dev = MEMBERS // groups
    lanes = slice(batch_id * SLOTS, (batch_id + 1) * SLOTS)
    parts = []
    for g in range(groups):
        block = shared_ref[g, :, lanes].astype(F32)
        parts.append(block[:mem_dev] + (block[mem_dev : mem_dev + 1] + block[mem_dev + 1 : mem_dev + 2]))
    return jnp.concatenate(parts, 0)


def store_packed(out_ref, prior, observed, error_now, live_count):
    mean_obs = jnp.sum(prior, 0, keepdims=True) / MEMBERS
    spread = prior - mean_obs
    variance = jnp.sum(spread * spread, 0, keepdims=True) / (MEMBERS - 1)
    gain = 1.0 / (variance + error_now)
    shrink = gain / (1.0 + jnp.sqrt(error_now * gain))
    live = lax.broadcasted_iota(jnp.int32, (1, SLOTS), 1) // OB < live_count
    scale = jnp.sqrt(shrink / (MEMBERS - 1))
    level = jnp.where(live, gain * (observed - mean_obs) / (scale * (MEMBERS - 1)), 0.0)
    scaled = (spread * jnp.where(live, scale, 0.0)).astype(BF16)
    total = jnp.sum(scaled.astype(F32), 0, keepdims=True)
    level_high, level_low = two_parts(level)
    total_high, total_low = two_parts(total)
    row = lax.broadcasted_iota(jnp.int32, (PACK - MEMBERS, SLOTS), 0)
    tail = jnp.where(
        row == 0,
        level_high,
        jnp.where(row == 1, level_low, jnp.where(row == 2, total_high, jnp.where(row == 3, total_low, 0.0))),
    )
    out_ref[:MEMBERS] = scaled
    out_ref[MEMBERS:] = tail.astype(BF16)


def first_pack_kernel(counts_ref, shared_ref, observed_ref, error_ref, out_ref):
    store_packed(
        out_ref, members_of(shared_ref, 0), observed_ref[0:1], error_ref[0:1], counts_ref[0:1, 0:1]
    )


def window(own_ref, around_ref):
    return [
        (0, own_ref),
        (-1, around_ref.at[0, 0]),
        (-2, around_ref.at[0, 1]),
        (1, around_ref.at[1, 0]),
        (2, around_ref.at[1, 1]),
    ]


def turned(pack):
    return jnp.transpose(pack[:MEMBERS].astype(F32)).astype(BF16)


def column_of(pack, row):
    value = pack[row : row + 1].astype(F32) + pack[row + 1 : row + 2].astype(F32)
    return jnp.transpose(jnp.broadcast_to(value, (SLOTS, SLOTS)))


def applied(change):
    return (change[MEMBERS : MEMBERS + 1] + change[MEMBERS + 1 : MEMBERS + 2]) - change[:MEMBERS]


def second_pack_kernel(
    counts_ref, index_ref, mask_ref, shared_ref, own_ref, around_ref, observed_ref, error_ref, out_ref
):
    prior = members_of(shared_ref, 1)
    high, low = two_parts(prior - jnp.sum(prior, 0, keepdims=True) / MEMBERS)
    deviation = jnp.concatenate([high, low], 1).astype(BF16)
    lane_block = lax.broadcasted_iota(jnp.int32, (1, SLOTS), 1) // OB
    change = jnp.zeros((PACK, 2 * SLOTS), F32)
    for offset, pack_ref in window(own_ref, around_ref):
        pack = pack_ref[...]
        covariance = dot(turned(pack), deviation, ((1,), (0,)))
        covariance = covariance[:, :SLOTS] + covariance[:, SLOTS:]
        kept = []
        for c in range(CAPB):
            column = (offset + 2) * CAPB + c
            keep = jnp.zeros((1, SLOTS), F32)
            for b in range(CAPB):
                flag = mask_ref[0, index_ref[1, b], column].astype(F32)
                keep = jnp.where(lane_block == b, flag, keep)
            kept.append(covariance[c * OB : (c + 1) * OB] * keep)
        high, low = two_parts(jnp.concatenate(kept, 0))
        change = change + dot(pack, jnp.concatenate([high, low], 1).astype(BF16), ((1,), (0,)))
    prior = prior + applied(change[:, :SLOTS] + change[:, SLOTS:])
    store_packed(out_ref, prior, observed_ref[1:2], error_ref[1:2], counts_ref[1:2, 0:1])


def update_kernel(
    batch_id, place_ref, mask_ref, own_ref, around_ref, state_ref, out_ref,
    turned_ref, packs_ref, total_ref, kept_ref,
):
    tiles = window(own_ref, around_ref)
    for n, (_, pack_ref) in enumerate(tiles):
        span = slice(n * SLOTS, (n + 1) * SLOTS)
        pack = pack_ref[...]
        turned_ref[span] = turned(pack)
        packs_ref[:, 2 * n * SLOTS : (2 * n + 1) * SLOTS] = pack
        packs_ref[:, (2 * n + 1) * SLOTS : (2 * n + 2) * SLOTS] = pack
        total_ref[span] = column_of(pack, MEMBERS + 2)
    cells = state_ref.shape[1]
    first = place_ref[0] * (cells // BLK)
    step = 2 * BLK
    for at in range(0, cells, step):
        buffer = at // step % 2
        values = state_ref[:, at : at + step]
        mean = jnp.sum(values.astype(F32), 0, keepdims=True) / MEMBERS
        covariance = dot(turned_ref[...], values, ((1,), (0,)))
        for n, (offset, _) in enumerate(tiles):
            for c in range(CAPB):
                span = slice(n * SLOTS + c * OB, n * SLOTS + (c + 1) * OB)
                total = total_ref[span]
                row = 2 * n * SLOTS + c * OB
                for h in range(2):
                    lanes = slice(h * BLK, (h + 1) * BLK)
                    block = first + (at // BLK + h)
                    flag = mask_ref[batch_id, block, (offset + 2) * CAPB + c].astype(F32)
                    kept = (covariance[span, lanes] - total * mean[:, lanes]) * flag
                    high, low = two_parts(kept)
                    kept_ref[buffer, row : row + OB, lanes] = high.astype(BF16)
                    kept_ref[buffer, row + SLOTS : row + SLOTS + OB, lanes] = low.astype(BF16)
        change = dot(packs_ref[...], kept_ref[buffer], ((1,), (0,)))
        out_ref[:, at : at + step] = (values.astype(F32) + applied(change)).astype(BF16)


PARAMS = pltpu.CompilerParams(vmem_limit_bytes=32 * 1024 * 1024)
VM = pl.BlockSpec(memory_space=pltpu.VMEM)
SM = pl.BlockSpec(memory_space=pltpu.SMEM)


def observe(block_index, gate_operator, prior_state, groups):
    mem_dev, cells = prior_state.shape
    return pl.pallas_call(
        observe_kernel,
        in_specs=[SM, VM, VM],
        out_specs=[VM, VM],
        out_shape=[
            jax.ShapeDtypeStruct((groups, ROWS, BATCHES * SLOTS), BF16),
            jax.ShapeDtypeStruct((groups, mem_dev, cells // groups), BF16),
        ],
        compiler_params=PARAMS,
        name="observe",
    )(block_index, gate_operator, prior_state)


def first_pack(counts, shared, observed, errors):
    return pl.pallas_call(
        first_pack_kernel,
        in_specs=[VM, VM, VM, VM],
        out_specs=VM,
        out_shape=jax.ShapeDtypeStruct((PACK, SLOTS), BF16),
        compiler_params=PARAMS,
        name="first_pack",
    )(counts, shared, observed, errors)


def second_pack(counts, index, mask, shared, own, around, observed, errors):
    return pl.pallas_call(
        second_pack_kernel,
        in_specs=[VM, SM, SM, VM, VM, VM, VM, VM],
        out_specs=VM,
        out_shape=jax.ShapeDtypeStruct((PACK, SLOTS), BF16),
        compiler_params=PARAMS,
        name="second_pack",
    )(counts, index, mask, shared, own, around, observed, errors)


def update(batch_id, place, mask, own, around, state):
    return pl.pallas_call(
        lambda *refs: update_kernel(batch_id, *refs),
        in_specs=[SM, SM, VM, VM, VM],
        out_specs=VM,
        out_shape=jax.ShapeDtypeStruct(state.shape, BF16),
        scratch_shapes=[
            pltpu.VMEM((5 * SLOTS, MEMBERS), BF16),
            pltpu.VMEM((PACK, 10 * SLOTS), BF16),
            pltpu.VMEM((5 * SLOTS, BLK), F32),
            pltpu.VMEM((2, 10 * SLOTS, 2 * BLK), BF16),
        ],
        compiler_params=PARAMS,
        name="update",
    )(place, mask, own, around, state)


def passed_around(pack):
    tiles, groups = lax.axis_size("space"), lax.axis_size("mem")
    received = []
    for offset in (1, 2):
        pairs = []
        for tile in range(tiles):
            for m in range(groups):
                target = tile + offset if m % 2 == 0 else tile - offset
                if 0 <= target < tiles:
                    pairs.append((tile * groups + m, target * groups + m))
        received.append(lax.ppermute(pack, ("space", "mem"), pairs))
    return jnp.stack(received)


def chip_shared(received):
    groups = lax.axis_size("mem")
    chips = [[2 * chip, 2 * chip + 1] for chip in range(groups // 2)]
    return lax.all_gather(received, "mem", axis=0, axis_index_groups=chips)


def per_device(prior_state, block_counts, block_index, gate_operator, observed, obs_error, local_mask):
    groups = lax.axis_size("mem")
    mem_dev, cells = prior_state.shape
    place = lax.axis_index("mem").astype(jnp.int32).reshape(1)
    own_block, moved = observe(block_index, gate_operator, prior_state, groups)
    shared = lax.all_to_all(own_block, "mem", split_axis=0, concat_axis=0, tiled=True)
    pack = first_pack(block_counts, shared, observed, obs_error)
    received = passed_around(pack)
    moved, pack = lax.optimization_barrier((moved, pack))
    state = lax.all_to_all(moved, "mem", split_axis=0, concat_axis=0, tiled=True)
    state = state.reshape(MEMBERS, cells // groups)
    around = chip_shared(received)
    around, state = lax.optimization_barrier((around, state))
    next_pack = second_pack(
        block_counts, block_index, local_mask, shared, pack, around, observed, obs_error
    )
    received = passed_around(next_pack)
    state = update(0, place, local_mask, pack, around, state)
    received, state = lax.optimization_barrier((received, state))
    next_around = chip_shared(received)
    state = update(1, place, local_mask, next_pack, next_around, state)
    parts = lax.all_to_all(
        state.reshape(groups, mem_dev, cells // groups), "mem", split_axis=0, concat_axis=0, tiled=True
    )
    return parts.transpose(1, 0, 2).reshape(mem_dev, cells)


def solution(mesh):
    placed = (
        P("mem", "space"),
        P(None, "space"),
        P(None, "space"),
        P(None, "space", None, None),
        P(None, "space"),
        P(None, "space"),
        P(None, "space", None),
    )
    return jax.shard_map(
        per_device, mesh=mesh, in_specs=placed, out_specs=P("mem", "space"), check_vma=False
    )
```

time: 106 us -> 80.2 us (0.76)
  Pallas kernels: 39.3 us -> 14.8 us
  blocking collectives: 34.1 us -> 24 us
  starting transfers between devices: 17.5 us -> 21.8 us
  local copies, waits for them, and re-layouts: 2.36 us -> 4.56 us
  waiting for transfers between devices: 12.3 us -> 14.3 us
    pallas_call x3, Pallas kernels: 32.1 us -> 5.08 us  [the longest x1 3.21 us: second_pack(): pl.pallas_call(second_pack_kernel, in_specs=[VM, SM, SM, VM, VM, VM, VM,...]
    all_to_all x1 -> x0, blocking collectives: 11.3 us -> none  [per_device(): lax.all_to_all(own_block, 'mem', split_axis=0, concat_axis=0, tiled=True)]
    all_to_all x0 -> x1, waiting for transfers between devices: none -> 6.73 us  [per_device(): lax.all_to_all(own_block, 'mem', split_axis=0, concat_axis=0, tiled=True)]
    ppermute x4, waiting for transfers between devices: 12.3 us -> 7.6 us  [passed_around(): received.append(lax.ppermute(pack, ('space', 'mem'), pairs))]
    all_to_all x0 -> x1, starting transfers between devices: none -> 4.43 us  [per_device(): lax.all_to_all(own_block, 'mem', split_axis=0, concat_axis=0, tiled=True)]
    pallas_call x2, Pallas kernels: 7.22 us -> 9.73 us  [update(): pl.pallas_call(lambda *refs: update_kernel(batch_id, *refs), in_specs=[SM...]
    unnamed x14 -> x18, local copies, waits for them, and re-layouts: 1.41 us -> 3.61 us
    all_gather x2, blocking collectives: 5.33 us -> 7.15 us  [chip_shared(): return lax.all_gather(received, 'mem', axis=0, axis_index_groups=chips)]
  transfers between devices with their start and end apart: 5 -> 6, of which waited for: 4 -> 4; matrix products, arithmetic and copies ran while one was open for 1% -> 0% of each run, Pallas kernels for 5% -> 6%
where the time goes in v2:
time: 80.2 us; the launch traced here: 79.7 us
  blocking collectives  24 us (30%)
  starting transfers between devices  21.8 us (27%)
  Pallas kernels  14.8 us (18%)
  waiting for transfers between devices  14.3 us (18%)
  local copies, waits for them, and re-layouts  4.56 us (6%)
    all_to_all x1, blocking collectives, per_device(): lax.all_to_all(state.reshape(groups, mem_dev, cells // groups), 'mem', sp...  16.9 us
    ppermute x4, starting transfers between devices, passed_around(): received.append(lax.ppermute(pack, ('space', 'mem'), pairs))  13.9 us
    pallas_call x2, Pallas kernels, update(): pl.pallas_call(lambda *refs: update_kernel(batch_id, *refs), in_specs=[SM...  9.73 us
    ppermute x4, waiting for transfers between devices, passed_around(): received.append(lax.ppermute(pack, ('space', 'mem'), pairs))  7.6 us
    all_gather x2, blocking collectives, chip_shared(): return lax.all_gather(received, 'mem', axis=0, axis_index_groups=chips)  7.15 us
    all_to_all x1, waiting for transfers between devices, per_device(): lax.all_to_all(own_block, 'mem', split_axis=0, concat_axis=0, tiled=True)  6.73 us
    all_to_all x1, starting transfers between devices, per_device(): lax.all_to_all(own_block, 'mem', split_axis=0, concat_axis=0, tiled=True)  4.43 us
    unnamed x18, local copies, waits for them, and re-layouts  3.61 us
  transfers between devices with their start and end apart: 6, of which 4 were waited for; matrix products, arithmetic and copies ran while one was open for 0% of the time, Pallas kernels for 6%

profile of v2, /device:TPU:24, one launch (start us, length us, event | category | flops | bytes accessed | tf_op | source)
XLA Modules:
  0.0 79.7 jit_solution(15981695161023548767)
XLA Ops:
  0.0 0.0 copy-start
  0.0 1.1 %copy-done = bf16[32,12288]{1,0:T(8,128)(2,1)S(1)} copy-done((bf16[32,12288]{1,0:T(8,128)(2,1)S(1)}, bf16[32,12288]{1,0:T(8,128)(2,1)}, u32[]{:S(2)}) %copy-start) | copy-done | bytes 786456
  1.1 0.0 copy-start.1
  1.1 0.9 %copy-done.1 = f32[2,4,32,128]{3,2,1,0:T(8,128)S(1)} copy-done((f32[2,4,32,128]{3,2,1,0:T(8,128)S(1)}, f32[2,4,32,128]{3,2,1,0:T(8,128)}, u32[]{:S(2)}) %copy-start.1) | copy-done | bytes 131096
  2.0 0.0 copy-start.4
  2.0 0.7 copy-done.4
  2.7 1.7 %observe.1 = (bf16[8,48,256]{2,1,0:T(8,128)(2,1)}, bf16[8,32,1536]{2,1,0:T(8,128)(2,1)}) custom-call(s32[2,4]{1,0:T(2,128)S(1)} %copy-done.4, f32[2,4,32,128]{3,2,1,0:T(8,128)S(1)} %copy-done.1, bf16[32,12288]{1,0:T(8,128)(2,1)S(1)} %copy-done), custom_call_target="tpu_custom_call" | custom-call | tf_op jit(solution)/shard_map/observe/pallas_call | solution.py:188
  4.4 0.0 copy-start.7
  4.4 0.0 copy-start.3
  4.4 4.4 %all-to-all-start = ((bf16[8,48,256]{2,1,0:T(8,128)(2,1)}), bf16[8,48,256]{2,1,0:T(8,128)(2,1)S(1)}, u32[]{:S(2)}, u32[]{:S(2)}) async-start(bf16[8,48,256]{2,1,0:T(8,128)(2,1)} %get-tuple-element.13), calls=%async_computation | async-start | bytes 393216 | tf_op jit(solution)/shard_map/all_to_all | solution.py:265
  8.9 0.0 copy-done.7
  8.9 0.0 copy-start.2
  8.9 0.1 copy.15.counts_ref
  9.0 6.7 %all-to-all-done.shared_ref = bf16[8,48,256]{2,1,0:T(8,128)(2,1)S(1)} async-done(((bf16[8,48,256]{2,1,0:T(8,128)(2,1)}), bf16[8,48,256]{2,1,0:T(8,128)(2,1)S(1)}, u32[]{:S(2)}, u32[]{:S(2)}) %all-to-all-start) | async-done | bytes 196640 | tf_op jit(solution)/shard_map/all_to_all | solution.py:265
  15.7 0.0 copy-done.3
  15.7 0.0 copy-done.2
  15.7 0.2 first_pack.1.own_ref.refs_2_
  15.9 0.0 copy-start.6
  15.9 3.6 %all-to-all-start.1 = ((bf16[8,32,1536]{2,1,0:T(8,128)(2,1)}), bf16[8,32,1536]{2,1,0:T(8,128)(2,1)S(1)}, u32[]{:S(2)}, u32[]{:S(2)}) async-start(bf16[8,32,1536]{2,1,0:T(8,128)(2,1)} %get-tuple-element.16), calls=%async_computation.1 | async-start | bytes 1572864 | tf_op jit(solution)/shard_map/all_to_all | solution.py:269
  19.4 5.2 %collective-permute-start.1 = (bf16[272,128]{1,0:T(8,128)(2,1)S(1)}, bf16[272,128]{1,0:T(8,128)(2,1)S(1)}, u32[]{:S(2)}, u32[]{:S(2)}) collective-permute-start(bf16[272,128]{1,0:T(8,128)(2,1)S(1)} %first_pack.1.own_ref.refs_2_), channel_id=1, source_target_pairs={{0,16},{2,18},{4,20},{6,22},{8,24},{10,26},{12,28},{14,30},{16,32}... | collective-permute-start | bytes 208904 | tf_op jit(solution)/shard_map/ppermute | solution.py:250
  24.6 3.8 %collective-permute-start = (bf16[272,128]{1,0:T(8,128)(2,1)S(1)}, bf16[272,128]{1,0:T(8,128)(2,1)S(1)}, u32[]{:S(2)}, u32[]{:S(2)}) collective-permute-start(bf16[272,128]{1,0:T(8,128)(2,1)S(1)} %first_pack.1.own_ref.refs_2_), channel_id=1, source_target_pairs={{0,8},{2,10},{4,12},{6,14},{8,16},{9,1},{10,18},{11,3},{12,20},{13... | collective-permute-start | bytes 208904 | tf_op jit(solution)/shard_map/ppermute | solution.py:250
  28.5 0.0 copy-done.6
  28.5 0.1 copy.18.mask_ref.refs_1_
  28.6 5.3 %collective-permute-done.1 = bf16[272,128]{1,0:T(8,128)(2,1)S(1)} collective-permute-done((bf16[272,128]{1,0:T(8,128)(2,1)S(1)}, bf16[272,128]{1,0:T(8,128)(2,1)S(1)}, u32[]{:S(2)}, u32[]{:S(2)}) %collective-permute-start.1) | collective-permute-done | bytes 69664 | tf_op jit(solution)/shard_map/ppermute | solution.py:250
  33.9 1.4 %collective-permute-done = bf16[272,128]{1,0:T(8,128)(2,1)S(1)} collective-permute-done((bf16[272,128]{1,0:T(8,128)(2,1)S(1)}, bf16[272,128]{1,0:T(8,128)(2,1)S(1)}, u32[]{:S(2)}, u32[]{:S(2)}) %collective-permute-start) | collective-permute-done | bytes 69664 | tf_op jit(solution)/shard_map/ppermute | solution.py:250
  35.3 3.1 %all-gather = bf16[4,272,128]{2,1,0:T(8,128)(2,1)S(1)} all-gather(bf16[2,272,128]{2,1,0:T(8,128)(2,1)S(1)} %pad_maximum_fusion), channel_id=2, replica_groups={{0,1},{2,3},{4,5},{6,7},{8,9},{10,11},{12,13},{14,15},{16,17},{18,19},{..., dimensions={0}, use_global_device_ids=true | all-gather | bytes 417792 | tf_op jit(solution)/shard_map/all_gather | solution.py:257
  38.3 0.0 all-to-all-done.1
  38.3 0.0 copy-start.5
  38.3 0.7 copy-done.5
  39.0 3.2 %second_pack.1.refs_2_ = bf16[272,128]{1,0:T(8,128)(2,1)S(1)} custom-call(s32[2,1]{1,0:T(2,128)S(1)} %copy.15.counts_ref, s32[2,4]{1,0:T(2,128)S(1)} %copy-done.5, s32[2,96,20]{2,1,0:T(8,128)S(1)} %copy.18.mask_ref.refs_1_, bf16[8,48,256]{2,1,0:T(8,128)(2,1)S(1)} %all-to-all-done.shared_ref, bf16[272,128]{1,0:T(8,128)(2,1)S(1)} %first_pack.1.own_ref.refs_2_, ...), custom_call_target="tpu_custom_call" | custom-call | tf_op jit(solution)/shard_map/second_pack/pallas_call | solution.py:213
  42.2 2.3 %collective-permute-start.3 = (bf16[272,128]{1,0:T(8,128)(2,1)S(1)}, bf16[272,128]{1,0:T(8,128)(2,1)S(1)}, u32[]{:S(2)}, u32[]{:S(2)}) collective-permute-start(bf16[272,128]{1,0:T(8,128)(2,1)S(1)} %second_pack.1.refs_2_), channel_id=1, source_target_pairs={{0,16},{2,18},{4,20},{6,22},{8,24},{10,26},{12,28},{14,30},{16,32}... | collective-permute-start | bytes 208904 | tf_op jit(solution)/shard_map/ppermute | solution.py:250
  44.5 2.5 %collective-permute-start.2 = (bf16[272,128]{1,0:T(8,128)(2,1)S(1)}, bf16[272,128]{1,0:T(8,128)(2,1)S(1)}, u32[]{:S(2)}, u32[]{:S(2)}) collective-permute-start(bf16[272,128]{1,0:T(8,128)(2,1)S(1)} %second_pack.1.refs_2_), channel_id=1, source_target_pairs={{0,8},{2,10},{4,12},{6,14},{8,16},{9,1},{10,18},{11,3},{12,20},{13... | collective-permute-start | bytes 208904 | tf_op jit(solution)/shard_map/ppermute | solution.py:250
  47.1 4.9 %update.2.refs_4_ = bf16[256,1536]{1,0:T(8,128)(2,1)S(1)} custom-call(s32[1]{0:T(128)} %bitcast.refs_0_, s32[2,96,20]{2,1,0:T(8,128)S(1)} %copy.18.mask_ref.refs_1_, bf16[272,128]{1,0:T(8,128)(2,1)S(1)} %first_pack.1.own_ref.refs_2_, bf16[2,2,272,128]{3,2,1,0:T(8,128)(2,1)S(1)} %bitcast.15, bf16[256,1536]{1,0:T(8,128)(2,1)S(1)} %bitcast.12), custom_call_target="tpu_custom_call" | custom-call | tf_op jit(solution)/shard_map/update/pallas_call | solution.py:224
  51.9 0.0 collective-permute-done.3
  52.0 0.9 %collective-permute-done.2 = bf16[272,128]{1,0:T(8,128)(2,1)S(1)} collective-permute-done((bf16[272,128]{1,0:T(8,128)(2,1)S(1)}, bf16[272,128]{1,0:T(8,128)(2,1)S(1)}, u32[]{:S(2)}, u32[]{:S(2)}) %collective-permute-start.2) | collective-permute-done | bytes 69664 | tf_op jit(solution)/shard_map/ppermute | solution.py:250
  52.9 4.1 %all-gather.1 = bf16[4,272,128]{2,1,0:T(8,128)(2,1)S(1)} all-gather(bf16[2,272,128]{2,1,0:T(8,128)(2,1)S(1)} %pad_maximum_fusion.1), channel_id=3, replica_groups={{0,1},{2,3},{4,5},{6,7},{8,9},{10,11},{12,13},{14,15},{16,17},{18,19},{..., dimensions={0}, use_global_device_ids=true | all-gather | bytes 417792 | tf_op jit(solution)/shard_map/all_gather | solution.py:257
  57.0 4.9 %update.3 = bf16[256,1536]{1,0:T(8,128)(2,1)S(1)} custom-call(s32[1]{0:T(128)} %bitcast.refs_0_, s32[2,96,20]{2,1,0:T(8,128)S(1)} %copy.18.mask_ref.refs_1_, bf16[272,128]{1,0:T(8,128)(2,1)S(1)} %second_pack.1.refs_2_, bf16[2,2,272,128]{3,2,1,0:T(8,128)(2,1)S(1)} %bitcast.16, bf16[256,1536]{1,0:T(8,128)(2,1)S(1)} %update.2.refs_4_), custom_call_target="tpu_custom_call" | custom-call | tf_op jit(solution)/shard_map/update/pallas_call | solution.py:224
  61.9 16.9 %all_to_all.15 = bf16[8,32,1536]{2,1,0:T(8,128)(2,1)S(1)} all-to-all(bf16[8,32,1536]{2,1,0:T(8,128)(2,1)S(1)} %bitcast.13), channel_id=1, replica_groups=mesh['space'=64,'mem'=8] {'mem'}, dimensions={0} | all-to-all | bytes 1572864 | tf_op jit(solution)/shard_map/all_to_all | solution.py:281
  78.8 0.9 %copy.20 = bf16[8,4,8,1536]{3,2,0,1:T(8,128)(2,1)} copy(bf16[8,4,8,1536]{3,2,1,0:T(8,128)(2,1)S(1)} %bitcast.17) | data formatting | bytes 1572864 | tf_op jit(solution)/shard_map/reshape | solution.py:284
  (2 shorter events, 0.0 us)
Async XLA Ops:
  0.0 1.1 %copy-start = (bf16[32,12288]{1,0:T(8,128)(2,1)S(1)}, bf16[32,12288]{1,0:T(8,128)(2,1)}, u32[]{:S(2)}) copy-start(bf16[32,12288]{1,0:T(8,128)(2,1)} %state_ref.1) | copy-start | bytes 2359300
  1.1 0.9 %copy-start.1 = (f32[2,4,32,128]{3,2,1,0:T(8,128)S(1)}, f32[2,4,32,128]{3,2,1,0:T(8,128)}, u32[]{:S(2)}) copy-start(f32[2,4,32,128]{3,2,1,0:T(8,128)} %gate_ref.1) | copy-start | bytes 393220
  2.0 0.7 copy-start.4
  4.4 4.4 %copy-start.7 = (s32[2,1]{0,1:T(1,128)S(1)}, s32[2,1]{0,1:T(1,128)}, u32[]{:S(2)}) copy-start(s32[2,1]{0,1:T(1,128)} %param.8) | copy-start | bytes 28
  4.4 11.3 %copy-start.3 = (f32[2,128]{1,0:T(2,128)S(1)}, f32[2,128]{1,0:T(2,128)}, u32[]{:S(2)}) copy-start(f32[2,128]{1,0:T(2,128)} %error_ref.3) | copy-start | bytes 3076
  4.4 11.3 %all-to-all-start = ((bf16[8,48,256]{2,1,0:T(8,128)(2,1)}), bf16[8,48,256]{2,1,0:T(8,128)(2,1)S(1)}, u32[]{:S(2)}, u32[]{:S(2)}) async-start(bf16[8,48,256]{2,1,0:T(8,128)(2,1)} %get-tuple-element.13), calls=%async_computation | async-start | bytes 393216 | tf_op jit(solution)/shard_map/all_to_all | solution.py:265
  8.9 6.8 %copy-start.2 = (f32[2,128]{1,0:T(2,128)S(1)}, f32[2,128]{1,0:T(2,128)}, u32[]{:S(2)}) copy-start(f32[2,128]{1,0:T(2,128)} %observed_ref.3) | copy-start | bytes 3076
  15.9 12.6 %copy-start.6 = (s32[2,96,20]{1,0,2:T(2,128)S(1)}, s32[2,96,20]{1,0,2:T(2,128)}, u32[]{:S(2)}) copy-start(s32[2,96,20]{1,0,2:T(2,128)} %param.13) | copy-start | bytes 46084
  15.9 22.4 %all-to-all-start.1 = ((bf16[8,32,1536]{2,1,0:T(8,128)(2,1)}), bf16[8,32,1536]{2,1,0:T(8,128)(2,1)S(1)}, u32[]{:S(2)}, u32[]{:S(2)}) async-start(bf16[8,32,1536]{2,1,0:T(8,128)(2,1)} %get-tuple-element.16), calls=%async_computation.1 | async-start | bytes 1572864 | tf_op jit(solution)/shard_map/all_to_all | solution.py:269
  19.4 14.4 %collective-permute-start.1 = (bf16[272,128]{1,0:T(8,128)(2,1)S(1)}, bf16[272,128]{1,0:T(8,128)(2,1)S(1)}, u32[]{:S(2)}, u32[]{:S(2)}) collective-permute-start(bf16[272,128]{1,0:T(8,128)(2,1)S(1)} %first_pack.1.own_ref.refs_2_), channel_id=1, source_target_pairs={{0,16},{2,18},{4,20},{6,22},{8,24},{10,26},{12,28},{14,30},{16,32}... | collective-permute-start | bytes 208904 | tf_op jit(solution)/shard_map/ppermute | solution.py:250
  24.6 10.6 %collective-permute-start = (bf16[272,128]{1,0:T(8,128)(2,1)S(1)}, bf16[272,128]{1,0:T(8,128)(2,1)S(1)}, u32[]{:S(2)}, u32[]{:S(2)}) collective-permute-start(bf16[272,128]{1,0:T(8,128)(2,1)S(1)} %first_pack.1.own_ref.refs_2_), channel_id=1, source_target_pairs={{0,8},{2,10},{4,12},{6,14},{8,16},{9,1},{10,18},{11,3},{12,20},{13... | collective-permute-start | bytes 208904 | tf_op jit(solution)/shard_map/ppermute | solution.py:250
  38.3 0.7 copy-start.5
  42.2 9.7 %collective-permute-start.3 = (bf16[272,128]{1,0:T(8,128)(2,1)S(1)}, bf16[272,128]{1,0:T(8,128)(2,1)S(1)}, u32[]{:S(2)}, u32[]{:S(2)}) collective-permute-start(bf16[272,128]{1,0:T(8,128)(2,1)S(1)} %second_pack.1.refs_2_), channel_id=1, source_target_pairs={{0,16},{2,18},{4,20},{6,22},{8,24},{10,26},{12,28},{14,30},{16,32}... | collective-permute-start | bytes 208904 | tf_op jit(solution)/shard_map/ppermute | solution.py:250
  44.5 8.4 %collective-permute-start.2 = (bf16[272,128]{1,0:T(8,128)(2,1)S(1)}, bf16[272,128]{1,0:T(8,128)(2,1)S(1)}, u32[]{:S(2)}, u32[]{:S(2)}) collective-permute-start(bf16[272,128]{1,0:T(8,128)(2,1)S(1)} %second_pack.1.refs_2_), channel_id=1, source_target_pairs={{0,8},{2,10},{4,12},{6,14},{8,16},{9,1},{10,18},{11,3},{12,20},{13... | collective-permute-start | bytes 208904 | tf_op jit(solution)/shard_map/ppermute | solution.py:250

commit v3 on v2

--- a/solution.py
+++ b/solution.py
@@ -27,15 +27,28 @@
     return lax.dot_general(a, b, (dims, ((), ())), preferred_element_type=F32)
 
 
-def observe_kernel(index_ref, gate_ref, state_ref, out_ref, moved_ref):
-    groups, mem_dev, width = moved_ref.shape
-    high, low = two_parts(gate_ref[...].reshape(BATCHES * CAPB * OB, BLK))
-    picks = []
+def observe_kernel(index_hbm, gate_ref, state_ref, out_ref, index_ref, gate, picks, index_sem, gate_sem, sems):
+    mem_dev = state_ref.shape[0]
+    index_copy = pltpu.make_async_copy(index_hbm, index_ref, index_sem)
+    index_copy.start()
+    gate_copy = pltpu.make_async_copy(gate_ref, gate, gate_sem)
+    gate_copy.start()
+    index_copy.wait()
+    copies = []
     for k in range(BATCHES):
         for c in range(CAPB):
+            n = k * CAPB + c
             start = pl.multiple_of(index_ref[k, c] * BLK, BLK)
-            picks.append(state_ref[:, pl.ds(start, BLK)])
-    rows = jnp.concatenate(picks, 0)
+            copies.append(
+                pltpu.make_async_copy(state_ref.at[:, pl.ds(start, BLK)], picks.at[n], sems.at[n])
+            )
+    for copy in copies:
+        copy.start()
+    gate_copy.wait()
+    high, low = two_parts(gate[...].reshape(BATCHES * CAPB * OB, BLK))
+    for copy in copies:
+        copy.wait()
+    rows = picks[...].reshape(BATCHES * CAPB * mem_dev, BLK)
     each = dot(rows, high.astype(BF16), ((1,), (1,))) + dot(rows, low.astype(BF16), ((1,), (1,)))
     lane_block = lax.broadcasted_iota(jnp.int32, (mem_dev, BATCHES * SLOTS), 1) // OB
     prior = jnp.zeros((mem_dev, BATCHES * SLOTS), F32)
@@ -43,13 +56,30 @@
         prior = jnp.where(lane_block == n, each[n * mem_dev : (n + 1) * mem_dev], prior)
     mean = jnp.sum(prior, 0, keepdims=True) / mem_dev
     mean_high, mean_low = two_parts(mean)
-    spare = ROWS - mem_dev
-    row = lax.broadcasted_iota(jnp.int32, (spare, BATCHES * SLOTS), 0)
+    row = lax.broadcasted_iota(jnp.int32, (ROWS - mem_dev, BATCHES * SLOTS), 0)
     tail = jnp.where(row == 0, mean_high, jnp.where(row == 1, mean_low, 0.0))
     block = jnp.concatenate([prior - mean, tail], 0).astype(BF16)
-    for g in range(groups):
+    for g in range(out_ref.shape[0]):
         out_ref[g] = block
-        moved_ref[g] = state_ref[:, g * width : (g + 1) * width]
+
+
+def gather_small_kernel(place_ref, counts_ref, index_ref, mask_ref, observed_ref, error_ref, between_ref, own_ref, slots_ref):
+    columns, _, blocks = mask_ref.shape
+    lane_block = lax.broadcasted_iota(jnp.int32, (1, SLOTS), 1) // OB
+    wanted = jnp.zeros((1, SLOTS), jnp.int32)
+    for b in range(CAPB):
+        wanted = jnp.where(lane_block == b, index_ref[1, b], wanted)
+    chosen = (lax.broadcasted_iota(jnp.int32, (blocks, SLOTS), 0) == wanted).astype(F32).astype(BF16)
+    mask = mask_ref[...].astype(F32).astype(BF16)
+    between_ref[...] = dot(mask[:, 0], chosen, ((1,), (0,)))
+    rows = own_ref.shape[1]
+    row = lax.broadcasted_iota(jnp.int32, (rows, blocks), 0) + place_ref[0] * rows
+    mine = (lax.broadcasted_iota(jnp.int32, (rows, blocks), 1) == row).astype(F32).astype(BF16)
+    for k in range(BATCHES):
+        own_ref[k] = dot(mine, mask[:, k], ((1,), (1,)))
+        slots_ref[3 * k : 3 * k + 1] = observed_ref[k : k + 1]
+        slots_ref[3 * k + 1 : 3 * k + 2] = error_ref[k : k + 1]
+        slots_ref[3 * k + 2 : 3 * k + 3] = (lane_block < counts_ref[k, 0]).astype(F32)
 
 
 def members_of(shared_ref, batch_id):
@@ -63,13 +93,13 @@
     return jnp.concatenate(parts, 0)
 
 
-def store_packed(out_ref, prior, observed, error_now, live_count):
+def store_packed(out_ref, prior, slots):
+    observed, error_now, live = slots[0:1], slots[1:2], slots[2:3] > 0.5
     mean_obs = jnp.sum(prior, 0, keepdims=True) / MEMBERS
     spread = prior - mean_obs
     variance = jnp.sum(spread * spread, 0, keepdims=True) / (MEMBERS - 1)
     gain = 1.0 / (variance + error_now)
     shrink = gain / (1.0 + jnp.sqrt(error_now * gain))
-    live = lax.broadcasted_iota(jnp.int32, (1, SLOTS), 1) // OB < live_count
     scale = jnp.sqrt(shrink / (MEMBERS - 1))
     level = jnp.where(live, gain * (observed - mean_obs) / (scale * (MEMBERS - 1)), 0.0)
     scaled = (spread * jnp.where(live, scale, 0.0)).astype(BF16)
@@ -86,10 +116,8 @@
     out_ref[MEMBERS:] = tail.astype(BF16)
 
 
-def first_pack_kernel(counts_ref, shared_ref, observed_ref, error_ref, out_ref):
-    store_packed(
-        out_ref, members_of(shared_ref, 0), observed_ref[0:1], error_ref[0:1], counts_ref[0:1, 0:1]
-    )
+def first_pack_kernel(shared_ref, slots_ref, out_ref):
+    store_packed(out_ref, members_of(shared_ref, 0), slots_ref[0:3])
 
 
 def window(own_ref, around_ref):
@@ -115,13 +143,10 @@
     return (change[MEMBERS : MEMBERS + 1] + change[MEMBERS + 1 : MEMBERS + 2]) - change[:MEMBERS]
 
 
-def second_pack_kernel(
-    counts_ref, index_ref, mask_ref, shared_ref, own_ref, around_ref, observed_ref, error_ref, out_ref
-):
+def second_pack_kernel(flags_ref, shared_ref, own_ref, around_ref, slots_ref, out_ref):
     prior = members_of(shared_ref, 1)
     high, low = two_parts(prior - jnp.sum(prior, 0, keepdims=True) / MEMBERS)
     deviation = jnp.concatenate([high, low], 1).astype(BF16)
-    lane_block = lax.broadcasted_iota(jnp.int32, (1, SLOTS), 1) // OB
     change = jnp.zeros((PACK, 2 * SLOTS), F32)
     for offset, pack_ref in window(own_ref, around_ref):
         pack = pack_ref[...]
@@ -130,19 +155,15 @@
         kept = []
         for c in range(CAPB):
             column = (offset + 2) * CAPB + c
-            keep = jnp.zeros((1, SLOTS), F32)
-            for b in range(CAPB):
-                flag = mask_ref[0, index_ref[1, b], column].astype(F32)
-                keep = jnp.where(lane_block == b, flag, keep)
-            kept.append(covariance[c * OB : (c + 1) * OB] * keep)
+            kept.append(covariance[c * OB : (c + 1) * OB] * flags_ref[column : column + 1])
         high, low = two_parts(jnp.concatenate(kept, 0))
         change = change + dot(pack, jnp.concatenate([high, low], 1).astype(BF16), ((1,), (0,)))
     prior = prior + applied(change[:, :SLOTS] + change[:, SLOTS:])
-    store_packed(out_ref, prior, observed_ref[1:2], error_ref[1:2], counts_ref[1:2, 0:1])
+    store_packed(out_ref, prior, slots_ref[3:6])
 
 
 def update_kernel(
-    batch_id, place_ref, mask_ref, own_ref, around_ref, state_ref, out_ref,
+    batch_id, flags_ref, own_ref, around_ref, state_ref, out_ref,
     turned_ref, packs_ref, total_ref, kept_ref,
 ):
     tiles = window(own_ref, around_ref)
@@ -154,7 +175,6 @@
         packs_ref[:, (2 * n + 1) * SLOTS : (2 * n + 2) * SLOTS] = pack
         total_ref[span] = column_of(pack, MEMBERS + 2)
     cells = state_ref.shape[1]
-    first = place_ref[0] * (cells // BLK)
     step = 2 * BLK
     for at in range(0, cells, step):
         buffer = at // step % 2
@@ -168,8 +188,7 @@
                 row = 2 * n * SLOTS + c * OB
                 for h in range(2):
                     lanes = slice(h * BLK, (h + 1) * BLK)
-                    block = first + (at // BLK + h)
-                    flag = mask_ref[batch_id, block, (offset + 2) * CAPB + c].astype(F32)
+                    flag = flags_ref[batch_id, at // BLK + h, (offset + 2) * CAPB + c]
                     kept = (covariance[span, lanes] - total * mean[:, lanes]) * flag
                     high, low = two_parts(kept)
                     kept_ref[buffer, row : row + OB, lanes] = high.astype(BF16)
@@ -184,46 +203,68 @@
 
 
 def observe(block_index, gate_operator, prior_state, groups):
-    mem_dev, cells = prior_state.shape
+    mem_dev = prior_state.shape[0]
+    anywhere = pl.BlockSpec(memory_space=pltpu.HBM)
     return pl.pallas_call(
         observe_kernel,
-        in_specs=[SM, VM, VM],
-        out_specs=[VM, VM],
+        in_specs=[anywhere, anywhere, anywhere],
+        out_specs=VM,
+        out_shape=jax.ShapeDtypeStruct((groups, ROWS, BATCHES * SLOTS), BF16),
+        scratch_shapes=[
+            pltpu.SMEM(block_index.shape, jnp.int32),
+            pltpu.VMEM(gate_operator.shape, F32),
+            pltpu.VMEM((BATCHES * CAPB, mem_dev, BLK), BF16),
+            pltpu.SemaphoreType.DMA(()),
+            pltpu.SemaphoreType.DMA(()),
+            pltpu.SemaphoreType.DMA((BATCHES * CAPB,)),
+        ],
+        compiler_params=pltpu.CompilerParams(vmem_limit_bytes=64 * 1024 * 1024 - 65536),
+        name="observe",
+    )(block_index, gate_operator, prior_state)
+
+
+def gather_small(place, counts, index, local_mask, observed, errors, blocks):
+    columns = local_mask.shape[2]
+    return pl.pallas_call(
+        gather_small_kernel,
+        in_specs=[SM, SM, SM, VM, VM, VM],
+        out_specs=[VM, VM, VM],
         out_shape=[
-            jax.ShapeDtypeStruct((groups, ROWS, BATCHES * SLOTS), BF16),
-            jax.ShapeDtypeStruct((groups, mem_dev, cells // groups), BF16),
+            jax.ShapeDtypeStruct((columns, SLOTS), F32),
+            jax.ShapeDtypeStruct((BATCHES, blocks, columns), F32),
+            jax.ShapeDtypeStruct((3 * BATCHES, SLOTS), F32),
         ],
         compiler_params=PARAMS,
-        name="observe",
-    )(block_index, gate_operator, prior_state)
-
-
-def first_pack(counts, shared, observed, errors):
+        name="gather_small",
+    )(place, counts, index, local_mask.transpose(2, 0, 1), observed, errors)
+
+
+def first_pack(shared, slots):
     return pl.pallas_call(
         first_pack_kernel,
-        in_specs=[VM, VM, VM, VM],
+        in_specs=[VM, VM],
         out_specs=VM,
         out_shape=jax.ShapeDtypeStruct((PACK, SLOTS), BF16),
         compiler_params=PARAMS,
         name="first_pack",
-    )(counts, shared, observed, errors)
-
-
-def second_pack(counts, index, mask, shared, own, around, observed, errors):
+    )(shared, slots)
+
+
+def second_pack(flags, shared, own, around, slots):
     return pl.pallas_call(
         second_pack_kernel,
-        in_specs=[VM, SM, SM, VM, VM, VM, VM, VM],
+        in_specs=[VM, VM, VM, VM, VM],
         out_specs=VM,
         out_shape=jax.ShapeDtypeStruct((PACK, SLOTS), BF16),
         compiler_params=PARAMS,
         name="second_pack",
-    )(counts, index, mask, shared, own, around, observed, errors)
-
-
-def update(batch_id, place, mask, own, around, state):
+    )(flags, shared, own, around, slots)
+
+
+def update(batch_id, flags, own, around, state):
     return pl.pallas_call(
         lambda *refs: update_kernel(batch_id, *refs),
-        in_specs=[SM, SM, VM, VM, VM],
+        in_specs=[SM, VM, VM, VM],
         out_specs=VM,
         out_shape=jax.ShapeDtypeStruct(state.shape, BF16),
         scratch_shapes=[
@@ -234,7 +275,7 @@
         ],
         compiler_params=PARAMS,
         name="update",
-    )(place, mask, own, around, state)
+    )(flags, own, around, state)
 
 
 def passed_around(pack):
@@ -260,24 +301,26 @@
 def per_device(prior_state, block_counts, block_index, gate_operator, observed, obs_error, local_mask):
     groups = lax.axis_size("mem")
     mem_dev, cells = prior_state.shape
+    own_block = observe(block_index, gate_operator, prior_state, groups)
+    shared = lax.all_to_all(own_block, "mem", split_axis=0, concat_axis=0, tiled=True)
+    prior_state, local_mask, own_block = lax.optimization_barrier((prior_state, local_mask, own_block))
+    moved = prior_state.reshape(mem_dev, groups, cells // groups).transpose(1, 0, 2)
     place = lax.axis_index("mem").astype(jnp.int32).reshape(1)
-    own_block, moved = observe(block_index, gate_operator, prior_state, groups)
-    shared = lax.all_to_all(own_block, "mem", split_axis=0, concat_axis=0, tiled=True)
-    pack = first_pack(block_counts, shared, observed, obs_error)
-    received = passed_around(pack)
-    moved, pack = lax.optimization_barrier((moved, pack))
+    between, flags, slots = gather_small(
+        place, block_counts, block_index, local_mask, observed, obs_error, SB // groups
+    )
+    moved, between, flags, slots = lax.optimization_barrier((moved, between, flags, slots))
     state = lax.all_to_all(moved, "mem", split_axis=0, concat_axis=0, tiled=True)
     state = state.reshape(MEMBERS, cells // groups)
-    around = chip_shared(received)
-    around, state = lax.optimization_barrier((around, state))
-    next_pack = second_pack(
-        block_counts, block_index, local_mask, shared, pack, around, observed, obs_error
-    )
+    pack = first_pack(shared, slots)
+    around = chip_shared(passed_around(pack))
+    next_pack = second_pack(between, shared, pack, around, slots)
+    next_pack, state = lax.optimization_barrier((next_pack, state))
     received = passed_around(next_pack)
-    state = update(0, place, local_mask, pack, around, state)
+    state = update(0, flags, pack, around, state)
     received, state = lax.optimization_barrier((received, state))
     next_around = chip_shared(received)
-    state = update(1, place, local_mask, next_pack, next_around, state)
+    state = update(1, flags, next_pack, next_around, state)
     parts = lax.all_to_all(
         state.reshape(groups, mem_dev, cells // groups), "mem", split_axis=0, concat_axis=0, tiled=True
     )

time: 80.2 us -> 72.6 us (0.905)
  Pallas kernels: 14.8 us -> 11.4 us
  waiting for transfers between devices: 14.3 us -> 11.7 us
  blocking collectives: 24 us -> 22.7 us
    all_to_all x1, waiting for transfers between devices: 6.73 us -> 2.58 us  [per_device(): lax.all_to_all(own_block, 'mem', split_axis=0, concat_axis=0, tiled=True)]
    pallas_call x2, Pallas kernels: 9.73 us -> 6.99 us  [update(): pl.pallas_call(lambda *refs: update_kernel(batch_id, *refs), in_specs=[SM...]
    unnamed x18 -> x11, local copies, waits for them, and re-layouts: 3.61 us -> 1.42 us
    reshape x0 -> x1, local copies, waits for them, and re-layouts: none -> 2.12 us  [per_device(): prior_state.reshape(mem_dev, groups, cells // groups).transpose(1, 0, 2)]
    all_gather x2, blocking collectives: 7.15 us -> 5.06 us  [chip_shared(): return lax.all_gather(received, 'mem', axis=0, axis_index_groups=chips)]
    ppermute x4, waiting for transfers between devices: 7.6 us -> 9.1 us  [passed_around(): received.append(lax.ppermute(pack, ('space', 'mem'), pairs))]
    pallas_call x3 -> x4, Pallas kernels: 5.08 us -> 4.46 us  [the longest x1 2.53 us: observe(): pl.pallas_call(observe_kernel, in_specs=[anywhere, anywhere, anywhere], o...]
  transfers between devices with their start and end apart: 6 -> 6, of which waited for: 4 -> 5; matrix products, arithmetic and copies ran while one was open for 0% -> 3% of each run, Pallas kernels for 6% -> 8%
where the time goes in v3:
time: 72.6 us; the launch traced here: 72.1 us
  blocking collectives  22.7 us (31%)
  starting transfers between devices  21.7 us (30%)
  waiting for transfers between devices  11.7 us (16%)
  Pallas kernels  11.4 us (16%)
  local copies, waits for them, and re-layouts  4.48 us (6%)
    all_to_all x1, blocking collectives, per_device(): lax.all_to_all(state.reshape(groups, mem_dev, cells // groups), 'mem', sp...  17.6 us
    ppermute x4, starting transfers between devices, passed_around(): received.append(lax.ppermute(pack, ('space', 'mem'), pairs))  13.9 us
    ppermute x4, waiting for transfers between devices, passed_around(): received.append(lax.ppermute(pack, ('space', 'mem'), pairs))  9.1 us
    pallas_call x2, Pallas kernels, update(): pl.pallas_call(lambda *refs: update_kernel(batch_id, *refs), in_specs=[SM...  6.99 us
    all_gather x2, blocking collectives, chip_shared(): return lax.all_gather(received, 'mem', axis=0, axis_index_groups=chips)  5.06 us
    all_to_all x1, starting transfers between devices, per_device(): lax.all_to_all(own_block, 'mem', split_axis=0, concat_axis=0, tiled=True)  4.31 us
    all_to_all x1, starting transfers between devices, per_device(): lax.all_to_all(moved, 'mem', split_axis=0, concat_axis=0, tiled=True)  3.55 us
    all_to_all x1, waiting for transfers between devices, per_device(): lax.all_to_all(own_block, 'mem', split_axis=0, concat_axis=0, tiled=True)  2.58 us
  transfers between devices with their start and end apart: 6, of which 5 were waited for; matrix products, arithmetic and copies ran while one was open for 3% of the time, Pallas kernels for 8%

profile of v3, /device:TPU:24, one launch (start us, length us, event | category | flops | bytes accessed | tf_op | source)
XLA Modules:
  0.0 72.1 jit_solution(14723919148306396725)
XLA Ops:
  0.0 2.5 %observe.1 = bf16[8,48,256]{2,1,0:T(8,128)(2,1)} custom-call(s32[2,4]{1,0:T(2,128)} %index_ref.1, f32[2,4,32,128]{3,2,1,0:T(8,128)} %gate_ref.1, bf16[32,12288]{1,0:T(8,128)(2,1)} %state_ref.1), custom_call_target="tpu_custom_call" | custom-call | tf_op jit(solution)/shard_map/observe/pallas_call | solution.py:208
  2.5 4.3 %all-to-all-start = ((bf16[8,48,256]{2,1,0:T(8,128)(2,1)}), bf16[8,48,256]{2,1,0:T(8,128)(2,1)S(1)}, u32[]{:S(2)}, u32[]{:S(2)}) async-start(bf16[8,48,256]{2,1,0:T(8,128)(2,1)} %observe.1), calls=%async_computation | async-start | bytes 393216 | tf_op jit(solution)/shard_map/all_to_all | solution.py:305
  6.9 0.0 copy-start.4
  6.9 0.7 copy-done.4
  7.5 0.1 copy.12.counts_ref
  7.6 0.0 copy-start
  7.6 0.0 copy-start.2
  7.6 0.0 copy-start.3
  7.6 2.1 %copy.17 = bf16[4,8,8,1536]{3,2,0,1:T(8,128)(2,1)} copy(bf16[4,8,8,1536]{3,2,1,0:T(8,128)(2,1)} %bitcast.26) | data formatting | bytes 1572864 | tf_op jit(solution)/shard_map/reshape | solution.py:307
  9.7 0.0 copy-start.1
  9.7 0.0 copy-done
  9.7 0.0 copy-done.2
  9.7 0.0 copy-done.3
  9.7 0.7 copy-done.1
  10.4 0.7 gather_small.1
  11.1 2.6 %all-to-all-done.shared_ref = bf16[8,48,256]{2,1,0:T(8,128)(2,1)S(1)} async-done(((bf16[8,48,256]{2,1,0:T(8,128)(2,1)}), bf16[8,48,256]{2,1,0:T(8,128)(2,1)S(1)}, u32[]{:S(2)}, u32[]{:S(2)}) %all-to-all-start) | async-done | bytes 196640 | tf_op jit(solution)/shard_map/all_to_all | solution.py:305
  13.7 3.5 %all-to-all-start.1 = ((bf16[8,32,1536]{2,1,0:T(8,128)(2,1)}), bf16[8,32,1536]{2,1,0:T(8,128)(2,1)S(1)}, u32[]{:S(2)}, u32[]{:S(2)}) async-start(bf16[8,32,1536]{2,1,0:T(8,128)(2,1)} %bitcast.19), calls=%async_computation.1 | async-start | bytes 1572864 | tf_op jit(solution)/shard_map/all_to_all | solution.py:313
  17.2 0.2 first_pack.1.own_ref.refs_1_
  17.4 5.2 %collective-permute-start.1 = (bf16[272,128]{1,0:T(8,128)(2,1)S(1)}, bf16[272,128]{1,0:T(8,128)(2,1)S(1)}, u32[]{:S(2)}, u32[]{:S(2)}) collective-permute-start(bf16[272,128]{1,0:T(8,128)(2,1)S(1)} %first_pack.1.own_ref.refs_1_), channel_id=1, source_target_pairs={{0,16},{2,18},{4,20},{6,22},{8,24},{10,26},{12,28},{14,30},{16,32}... | collective-permute-start | bytes 208904 | tf_op jit(solution)/shard_map/ppermute | solution.py:291
  22.6 3.8 %collective-permute-start = (bf16[272,128]{1,0:T(8,128)(2,1)S(1)}, bf16[272,128]{1,0:T(8,128)(2,1)S(1)}, u32[]{:S(2)}, u32[]{:S(2)}) collective-permute-start(bf16[272,128]{1,0:T(8,128)(2,1)S(1)} %first_pack.1.own_ref.refs_1_), channel_id=1, source_target_pairs={{0,8},{2,10},{4,12},{6,14},{8,16},{9,1},{10,18},{11,3},{12,20},{13... | collective-permute-start | bytes 208904 | tf_op jit(solution)/shard_map/ppermute | solution.py:291
  26.4 5.4 %collective-permute-done.1 = bf16[272,128]{1,0:T(8,128)(2,1)S(1)} collective-permute-done((bf16[272,128]{1,0:T(8,128)(2,1)S(1)}, bf16[272,128]{1,0:T(8,128)(2,1)S(1)}, u32[]{:S(2)}, u32[]{:S(2)}) %collective-permute-start.1) | collective-permute-done | bytes 69664 | tf_op jit(solution)/shard_map/ppermute | solution.py:291
  31.8 1.4 %collective-permute-done = bf16[272,128]{1,0:T(8,128)(2,1)S(1)} collective-permute-done((bf16[272,128]{1,0:T(8,128)(2,1)S(1)}, bf16[272,128]{1,0:T(8,128)(2,1)S(1)}, u32[]{:S(2)}, u32[]{:S(2)}) %collective-permute-start) | collective-permute-done | bytes 69664 | tf_op jit(solution)/shard_map/ppermute | solution.py:291
  33.2 3.1 %all-gather = bf16[4,272,128]{2,1,0:T(8,128)(2,1)S(1)} all-gather(bf16[2,272,128]{2,1,0:T(8,128)(2,1)S(1)} %pad_maximum_fusion), channel_id=2, replica_groups={{0,1},{2,3},{4,5},{6,7},{8,9},{10,11},{12,13},{14,15},{16,17},{18,19},{..., dimensions={0}, use_global_device_ids=true | all-gather | bytes 417792 | tf_op jit(solution)/shard_map/all_gather | solution.py:298
  36.3 1.1 %second_pack.1.refs_1_ = bf16[272,128]{1,0:T(8,128)(2,1)S(1)} custom-call(f32[20,128]{1,0:T(8,128)S(1)} %get-tuple-element.24.flags_ref, bf16[8,48,256]{2,1,0:T(8,128)(2,1)S(1)} %all-to-all-done.shared_ref, bf16[272,128]{1,0:T(8,128)(2,1)S(1)} %first_pack.1.own_ref.refs_1_, bf16[2,2,272,128]{3,2,1,0:T(8,128)(2,1)S(1)} %bitcast.22, ...), custom_call_target="tpu_custom_call" | custom-call | tf_op jit(solution)/shard_map/second_pack/pallas_call | solution.py:254
  37.3 0.0 all-to-all-done.1
  37.4 2.3 %collective-permute-start.3 = (bf16[272,128]{1,0:T(8,128)(2,1)S(1)}, bf16[272,128]{1,0:T(8,128)(2,1)S(1)}, u32[]{:S(2)}, u32[]{:S(2)}) collective-permute-start(bf16[272,128]{1,0:T(8,128)(2,1)S(1)} %second_pack.1.refs_1_), channel_id=1, source_target_pairs={{0,16},{2,18},{4,20},{6,22},{8,24},{10,26},{12,28},{14,30},{16,32}... | collective-permute-start | bytes 208904 | tf_op jit(solution)/shard_map/ppermute | solution.py:291
  39.7 2.5 %collective-permute-start.2 = (bf16[272,128]{1,0:T(8,128)(2,1)S(1)}, bf16[272,128]{1,0:T(8,128)(2,1)S(1)}, u32[]{:S(2)}, u32[]{:S(2)}) collective-permute-start(bf16[272,128]{1,0:T(8,128)(2,1)S(1)} %second_pack.1.refs_1_), channel_id=1, source_target_pairs={{0,8},{2,10},{4,12},{6,14},{8,16},{9,1},{10,18},{11,3},{12,20},{13... | collective-permute-start | bytes 208904 | tf_op jit(solution)/shard_map/ppermute | solution.py:291
  42.2 3.5 %update.2.refs_3_ = bf16[256,1536]{1,0:T(8,128)(2,1)S(1)} custom-call(f32[2,12,20]{2,1,0:T(8,128)S(1)} %get-tuple-element.23.refs_0_, bf16[272,128]{1,0:T(8,128)(2,1)S(1)} %first_pack.1.own_ref.refs_1_, bf16[2,2,272,128]{3,2,1,0:T(8,128)(2,1)S(1)} %bitcast.23, bf16[256,1536]{1,0:T(8,128)(2,1)S(1)} %bitcast.20), custom_call_target="tpu_custom_call" | custom-call | tf_op jit(solution)/shard_map/update/pallas_call | solution.py:265
  45.7 0.9 %collective-permute-done.3 = bf16[272,128]{1,0:T(8,128)(2,1)S(1)} collective-permute-done((bf16[272,128]{1,0:T(8,128)(2,1)S(1)}, bf16[272,128]{1,0:T(8,128)(2,1)S(1)}, u32[]{:S(2)}, u32[]{:S(2)}) %collective-permute-start.3) | collective-permute-done | bytes 69664 | tf_op jit(solution)/shard_map/ppermute | solution.py:291
  46.7 1.4 %collective-permute-done.2 = bf16[272,128]{1,0:T(8,128)(2,1)S(1)} collective-permute-done((bf16[272,128]{1,0:T(8,128)(2,1)S(1)}, bf16[272,128]{1,0:T(8,128)(2,1)S(1)}, u32[]{:S(2)}, u32[]{:S(2)}) %collective-permute-start.2) | collective-permute-done | bytes 69664 | tf_op jit(solution)/shard_map/ppermute | solution.py:291
  48.1 2.0 %all-gather.1 = bf16[4,272,128]{2,1,0:T(8,128)(2,1)S(1)} all-gather(bf16[2,272,128]{2,1,0:T(8,128)(2,1)S(1)} %pad_maximum_fusion.1), channel_id=3, replica_groups={{0,1},{2,3},{4,5},{6,7},{8,9},{10,11},{12,13},{14,15},{16,17},{18,19},{..., dimensions={0}, use_global_device_ids=true | all-gather | bytes 417792 | tf_op jit(solution)/shard_map/all_gather | solution.py:298
  50.1 3.5 %update.3 = bf16[256,1536]{1,0:T(8,128)(2,1)S(1)} custom-call(f32[2,12,20]{2,1,0:T(8,128)S(1)} %get-tuple-element.23.refs_0_, bf16[272,128]{1,0:T(8,128)(2,1)S(1)} %second_pack.1.refs_1_, bf16[2,2,272,128]{3,2,1,0:T(8,128)(2,1)S(1)} %bitcast.24, bf16[256,1536]{1,0:T(8,128)(2,1)S(1)} %update.2.refs_3_), custom_call_target="tpu_custom_call" | custom-call | tf_op jit(solution)/shard_map/update/pallas_call | solution.py:265
  53.6 17.6 %all_to_all.15 = bf16[8,32,1536]{2,1,0:T(8,128)(2,1)S(1)} all-to-all(bf16[8,32,1536]{2,1,0:T(8,128)(2,1)S(1)} %bitcast.21), channel_id=1, replica_groups=mesh['space'=64,'mem'=8] {'mem'}, dimensions={0} | all-to-all | bytes 1572864 | tf_op jit(solution)/shard_map/all_to_all | solution.py:324
  71.2 0.9 %copy.15 = bf16[8,4,8,1536]{3,2,0,1:T(8,128)(2,1)} copy(bf16[8,4,8,1536]{3,2,1,0:T(8,128)(2,1)S(1)} %bitcast.27) | data formatting | bytes 1572864 | tf_op jit(solution)/shard_map/reshape | solution.py:327
  (2 shorter events, 0.0 us)
Async XLA Ops:
  2.5 11.2 %all-to-all-start = ((bf16[8,48,256]{2,1,0:T(8,128)(2,1)}), bf16[8,48,256]{2,1,0:T(8,128)(2,1)S(1)}, u32[]{:S(2)}, u32[]{:S(2)}) async-start(bf16[8,48,256]{2,1,0:T(8,128)(2,1)} %observe.1), calls=%async_computation | async-start | bytes 393216 | tf_op jit(solution)/shard_map/all_to_all | solution.py:305
  6.9 0.7 copy-start.4
  7.6 2.1 %copy-start = (s32[2,96,20]{1,0,2:T(2,128)S(1)}, s32[2,96,20]{1,0,2:T(2,128)}, u32[]{:S(2)}) copy-start(s32[2,96,20]{1,0,2:T(2,128)} %param.13) | copy-start | bytes 46084
  7.6 2.1 %copy-start.2 = (f32[2,128]{1,0:T(2,128)S(1)}, f32[2,128]{1,0:T(2,128)}, u32[]{:S(2)}) copy-start(f32[2,128]{1,0:T(2,128)} %observed_ref.1) | copy-start | bytes 3076
  7.6 2.1 %copy-start.3 = (f32[2,128]{1,0:T(2,128)S(1)}, f32[2,128]{1,0:T(2,128)}, u32[]{:S(2)}) copy-start(f32[2,128]{1,0:T(2,128)} %error_ref.1) | copy-start | bytes 3076
  9.7 0.7 copy-start.1
  13.7 23.7 %all-to-all-start.1 = ((bf16[8,32,1536]{2,1,0:T(8,128)(2,1)}), bf16[8,32,1536]{2,1,0:T(8,128)(2,1)S(1)}, u32[]{:S(2)}, u32[]{:S(2)}) async-start(bf16[8,32,1536]{2,1,0:T(8,128)(2,1)} %bitcast.19), calls=%async_computation.1 | async-start | bytes 1572864 | tf_op jit(solution)/shard_map/all_to_all | solution.py:313
  17.4 14.4 %collective-permute-start.1 = (bf16[272,128]{1,0:T(8,128)(2,1)S(1)}, bf16[272,128]{1,0:T(8,128)(2,1)S(1)}, u32[]{:S(2)}, u32[]{:S(2)}) collective-permute-start(bf16[272,128]{1,0:T(8,128)(2,1)S(1)} %first_pack.1.own_ref.refs_1_), channel_id=1, source_target_pairs={{0,16},{2,18},{4,20},{6,22},{8,24},{10,26},{12,28},{14,30},{16,32}... | collective-permute-start | bytes 208904 | tf_op jit(solution)/shard_map/ppermute | solution.py:291
  22.6 10.6 %collective-permute-start = (bf16[272,128]{1,0:T(8,128)(2,1)S(1)}, bf16[272,128]{1,0:T(8,128)(2,1)S(1)}, u32[]{:S(2)}, u32[]{:S(2)}) collective-permute-start(bf16[272,128]{1,0:T(8,128)(2,1)S(1)} %first_pack.1.own_ref.refs_1_), channel_id=1, source_target_pairs={{0,8},{2,10},{4,12},{6,14},{8,16},{9,1},{10,18},{11,3},{12,20},{13... | collective-permute-start | bytes 208904 | tf_op jit(solution)/shard_map/ppermute | solution.py:291
  37.4 9.3 %collective-permute-start.3 = (bf16[272,128]{1,0:T(8,128)(2,1)S(1)}, bf16[272,128]{1,0:T(8,128)(2,1)S(1)}, u32[]{:S(2)}, u32[]{:S(2)}) collective-permute-start(bf16[272,128]{1,0:T(8,128)(2,1)S(1)} %second_pack.1.refs_1_), channel_id=1, source_target_pairs={{0,16},{2,18},{4,20},{6,22},{8,24},{10,26},{12,28},{14,30},{16,32}... | collective-permute-start | bytes 208904 | tf_op jit(solution)/shard_map/ppermute | solution.py:291
  39.7 8.4 %collective-permute-start.2 = (bf16[272,128]{1,0:T(8,128)(2,1)S(1)}, bf16[272,128]{1,0:T(8,128)(2,1)S(1)}, u32[]{:S(2)}, u32[]{:S(2)}) collective-permute-start(bf16[272,128]{1,0:T(8,128)(2,1)S(1)} %second_pack.1.refs_1_), channel_id=1, source_target_pairs={{0,8},{2,10},{4,12},{6,14},{8,16},{9,1},{10,18},{11,3},{12,20},{13... | collective-permute-start | bytes 208904 | tf_op jit(solution)/shard_map/ppermute | solution.py:291

commit v4 on v3

--- a/solution.py
+++ b/solution.py
@@ -63,7 +63,7 @@
         out_ref[g] = block
 
 
-def gather_small_kernel(place_ref, counts_ref, index_ref, mask_ref, observed_ref, error_ref, between_ref, own_ref, slots_ref):
+def gather_small_kernel(counts_ref, index_ref, mask_ref, observed_ref, error_ref, between_ref, own_ref, slots_ref):
     columns, _, blocks = mask_ref.shape
     lane_block = lax.broadcasted_iota(jnp.int32, (1, SLOTS), 1) // OB
     wanted = jnp.zeros((1, SLOTS), jnp.int32)
@@ -72,11 +72,11 @@
     chosen = (lax.broadcasted_iota(jnp.int32, (blocks, SLOTS), 0) == wanted).astype(F32).astype(BF16)
     mask = mask_ref[...].astype(F32).astype(BF16)
     between_ref[...] = dot(mask[:, 0], chosen, ((1,), (0,)))
-    rows = own_ref.shape[1]
-    row = lax.broadcasted_iota(jnp.int32, (rows, blocks), 0) + place_ref[0] * rows
-    mine = (lax.broadcasted_iota(jnp.int32, (rows, blocks), 1) == row).astype(F32).astype(BF16)
+    cells = own_ref.shape[2]
+    block = lax.broadcasted_iota(jnp.int32, (blocks, cells), 1) // BLK + lax.axis_index("mem") * (cells // BLK)
+    mine = (lax.broadcasted_iota(jnp.int32, (blocks, cells), 0) == block).astype(F32).astype(BF16)
     for k in range(BATCHES):
-        own_ref[k] = dot(mine, mask[:, k], ((1,), (1,)))
+        own_ref[k] = dot(mask[:, k], mine, ((1,), (0,)))
         slots_ref[3 * k : 3 * k + 1] = observed_ref[k : k + 1]
         slots_ref[3 * k + 1 : 3 * k + 2] = error_ref[k : k + 1]
         slots_ref[3 * k + 2 : 3 * k + 3] = (lane_block < counts_ref[k, 0]).astype(F32)
@@ -121,22 +121,19 @@
 
 
 def window(own_ref, around_ref):
+    tile = lax.axis_index("space")
+    below, below_two = 1 - tile % 2, 1 - tile // 2 % 2
     return [
         (0, own_ref),
-        (-1, around_ref.at[0, 0]),
-        (-2, around_ref.at[0, 1]),
-        (1, around_ref.at[1, 0]),
-        (2, around_ref.at[1, 1]),
+        (-1, around_ref.at[below, 0]),
+        (-2, around_ref.at[below_two, 1]),
+        (1, around_ref.at[1 - below, 0]),
+        (2, around_ref.at[1 - below_two, 1]),
     ]
 
 
 def turned(pack):
-    return jnp.transpose(pack[:MEMBERS].astype(F32)).astype(BF16)
-
-
-def column_of(pack, row):
-    value = pack[row : row + 1].astype(F32) + pack[row + 1 : row + 2].astype(F32)
-    return jnp.transpose(jnp.broadcast_to(value, (SLOTS, SLOTS)))
+    return jnp.transpose(pack[:MEMBERS])
 
 
 def applied(change):
@@ -163,38 +160,52 @@
 
 
 def update_kernel(
-    batch_id, flags_ref, own_ref, around_ref, state_ref, out_ref,
-    turned_ref, packs_ref, total_ref, kept_ref,
+    batch_id, flags_ref, own_ref, around_ref, state_ref, out_ref, turned_ref, packs_ref, total_ref, kept_ref
 ):
     tiles = window(own_ref, around_ref)
     for n, (_, pack_ref) in enumerate(tiles):
         span = slice(n * SLOTS, (n + 1) * SLOTS)
-        pack = pack_ref[...]
-        turned_ref[span] = turned(pack)
-        packs_ref[:, 2 * n * SLOTS : (2 * n + 1) * SLOTS] = pack
-        packs_ref[:, (2 * n + 1) * SLOTS : (2 * n + 2) * SLOTS] = pack
-        total_ref[span] = column_of(pack, MEMBERS + 2)
+        turned_ref[span] = turned(pack_ref[...])
+        packs_ref[:, span] = pack_ref[...]
+    packs_ref[:, 5 * SLOTS :] = tiles[4][1][...]
+    total_ref[...] = dot(turned_ref[...], jnp.ones((MEMBERS, BLK), BF16), ((1,), (0,)))
     cells = state_ref.shape[1]
     step = 2 * BLK
-    for at in range(0, cells, step):
+    last = 4 * SLOTS
+
+    def covariances(at):
         buffer = at // step % 2
         values = state_ref[:, at : at + step]
         mean = jnp.sum(values.astype(F32), 0, keepdims=True) / MEMBERS
         covariance = dot(turned_ref[...], values, ((1,), (0,)))
         for n, (offset, _) in enumerate(tiles):
             for c in range(CAPB):
-                span = slice(n * SLOTS + c * OB, n * SLOTS + (c + 1) * OB)
-                total = total_ref[span]
-                row = 2 * n * SLOTS + c * OB
-                for h in range(2):
-                    lanes = slice(h * BLK, (h + 1) * BLK)
-                    flag = flags_ref[batch_id, at // BLK + h, (offset + 2) * CAPB + c]
-                    kept = (covariance[span, lanes] - total * mean[:, lanes]) * flag
-                    high, low = two_parts(kept)
-                    kept_ref[buffer, row : row + OB, lanes] = high.astype(BF16)
-                    kept_ref[buffer, row + SLOTS : row + SLOTS + OB, lanes] = low.astype(BF16)
-        change = dot(packs_ref[...], kept_ref[buffer], ((1,), (0,)))
-        out_ref[:, at : at + step] = (values.astype(F32) + applied(change)).astype(BF16)
+                row = n * SLOTS + c * OB
+                column = (offset + 2) * CAPB + c
+                flags = flags_ref[batch_id, column : column + 1, at : at + step]
+                total = total_ref[row : row + OB]
+                total = jnp.concatenate([total, total], 1)
+                kept = (covariance[row : row + OB] - total * mean) * flags
+                high, low = two_parts(kept)
+                kept_ref[buffer, row : row + OB] = high.astype(BF16)
+                low_row = row + (SLOTS if n == 4 else 6 * SLOTS)
+                kept_ref[buffer, low_row : low_row + OB] = low.astype(BF16)
+
+    def apply(at):
+        buffer = at // step % 2
+        change = (
+            dot(packs_ref[:, :last], kept_ref[buffer, :last], ((1,), (0,)))
+            + dot(packs_ref[:, last:], kept_ref[buffer, last : 6 * SLOTS], ((1,), (0,)))
+            + dot(packs_ref[:, :last], kept_ref[buffer, 6 * SLOTS :], ((1,), (0,)))
+        )
+        values = state_ref[:, at : at + step].astype(F32)
+        out_ref[:, at : at + step] = (values + applied(change)).astype(BF16)
+
+    covariances(0)
+    for at in range(0, cells, step):
+        if at + step < cells:
+            covariances(at + step)
+        apply(at)
 
 
 PARAMS = pltpu.CompilerParams(vmem_limit_bytes=32 * 1024 * 1024)
@@ -223,20 +234,20 @@
     )(block_index, gate_operator, prior_state)
 
 
-def gather_small(place, counts, index, local_mask, observed, errors, blocks):
+def gather_small(counts, index, local_mask, observed, errors, cells):
     columns = local_mask.shape[2]
     return pl.pallas_call(
         gather_small_kernel,
-        in_specs=[SM, SM, SM, VM, VM, VM],
+        in_specs=[SM, SM, VM, VM, VM],
         out_specs=[VM, VM, VM],
         out_shape=[
             jax.ShapeDtypeStruct((columns, SLOTS), F32),
-            jax.ShapeDtypeStruct((BATCHES, blocks, columns), F32),
+            jax.ShapeDtypeStruct((BATCHES, columns, cells), F32),
             jax.ShapeDtypeStruct((3 * BATCHES, SLOTS), F32),
         ],
         compiler_params=PARAMS,
         name="gather_small",
-    )(place, counts, index, local_mask.transpose(2, 0, 1), observed, errors)
+    )(counts, index, local_mask.transpose(2, 0, 1), observed, errors)
 
 
 def first_pack(shared, slots):
@@ -264,12 +275,12 @@
 def update(batch_id, flags, own, around, state):
     return pl.pallas_call(
         lambda *refs: update_kernel(batch_id, *refs),
-        in_specs=[SM, VM, VM, VM],
+        in_specs=[VM, VM, VM, VM],
         out_specs=VM,
         out_shape=jax.ShapeDtypeStruct(state.shape, BF16),
         scratch_shapes=[
             pltpu.VMEM((5 * SLOTS, MEMBERS), BF16),
-            pltpu.VMEM((PACK, 10 * SLOTS), BF16),
+            pltpu.VMEM((PACK, 6 * SLOTS), BF16),
             pltpu.VMEM((5 * SLOTS, BLK), F32),
             pltpu.VMEM((2, 10 * SLOTS, 2 * BLK), BF16),
         ],
@@ -285,9 +296,10 @@
         pairs = []
         for tile in range(tiles):
             for m in range(groups):
-                target = tile + offset if m % 2 == 0 else tile - offset
-                if 0 <= target < tiles:
-                    pairs.append((tile * groups + m, target * groups + m))
+                above = (tile // offset + m) % 2 == 0
+                partner = tile + offset if above else tile - offset
+                if 0 <= partner < tiles:
+                    pairs.append((tile * groups + m, partner * groups + m))
         received.append(lax.ppermute(pack, ("space", "mem"), pairs))
     return jnp.stack(received)
 
@@ -305,9 +317,8 @@
     shared = lax.all_to_all(own_block, "mem", split_axis=0, concat_axis=0, tiled=True)
     prior_state, local_mask, own_block = lax.optimization_barrier((prior_state, local_mask, own_block))
     moved = prior_state.reshape(mem_dev, groups, cells // groups).transpose(1, 0, 2)
-    place = lax.axis_index("mem").astype(jnp.int32).reshape(1)
     between, flags, slots = gather_small(
-        place, block_counts, block_index, local_mask, observed, obs_error, SB // groups
+        block_counts, block_index, local_mask, observed, obs_error, cells // groups
     )
     moved, between, flags, slots = lax.optimization_barrier((moved, between, flags, slots))
     state = lax.all_to_all(moved, "mem", split_axis=0, concat_axis=0, tiled=True)

time: 72.6 us -> 72.6 us (level)
  blocking collectives: 22.7 us -> 30.5 us
  waiting for transfers between devices: 11.7 us -> 7.25 us
  Pallas kernels: 11.4 us -> 9.59 us
  starting transfers between devices: 21.7 us -> 20.7 us
    all_gather x2, blocking collectives: 5.06 us -> 12.8 us  [chip_shared(): return lax.all_gather(received, 'mem', axis=0, axis_index_groups=chips)]
    ppermute x4, waiting for transfers between devices: 9.1 us -> 4.14 us  [passed_around(): received.append(lax.ppermute(pack, ('space', 'mem'), pairs))]
    pallas_call x3, Pallas kernels: 7.69 us -> 5.84 us  [the longest x2 5.02 us: update(): pl.pallas_call(lambda *refs: update_kernel(batch_id, *refs), in_specs=[VM...]
    ppermute x4, starting transfers between devices: 13.9 us -> 12.8 us  [passed_around(): received.append(lax.ppermute(pack, ('space', 'mem'), pairs))]
  transfers between devices with their start and end apart: 6 -> 6, of which waited for: 5 -> 4; matrix products, arithmetic and copies ran while one was open for 3% -> 3% of each run, Pallas kernels for 8% -> 6%
where the time goes in v4:
time: 72.6 us; the launch traced here: 72.1 us
  blocking collectives  30.5 us (42%)
  starting transfers between devices  20.7 us (29%)
  Pallas kernels  9.59 us (13%)
  waiting for transfers between devices  7.25 us (10%)
  local copies, waits for them, and re-layouts  3.84 us (5%)
    all_to_all x1, blocking collectives, per_device(): lax.all_to_all(state.reshape(groups, mem_dev, cells // groups), 'mem', sp...  17.8 us
    ppermute x4, starting transfers between devices, passed_around(): received.append(lax.ppermute(pack, ('space', 'mem'), pairs))  12.8 us
    all_gather x2, blocking collectives, chip_shared(): return lax.all_gather(received, 'mem', axis=0, axis_index_groups=chips)  12.8 us
    pallas_call x2, Pallas kernels, update(): pl.pallas_call(lambda *refs: update_kernel(batch_id, *refs), in_specs=[VM...  5.02 us
    all_to_all x1, starting transfers between devices, per_device(): lax.all_to_all(own_block, 'mem', split_axis=0, concat_axis=0, tiled=True)  4.31 us
    ppermute x4, waiting for transfers between devices, passed_around(): received.append(lax.ppermute(pack, ('space', 'mem'), pairs))  4.14 us
    all_to_all x1, starting transfers between devices, per_device(): lax.all_to_all(moved, 'mem', split_axis=0, concat_axis=0, tiled=True)  3.55 us
    all_to_all x1, waiting for transfers between devices, per_device(): lax.all_to_all(own_block, 'mem', split_axis=0, concat_axis=0, tiled=True)  3.11 us
  transfers between devices with their start and end apart: 6, of which 4 were waited for; matrix products, arithmetic and copies ran while one was open for 3% of the time, Pallas kernels for 6%

profile of v4, /device:TPU:24, one launch (start us, length us, event | category | flops | bytes accessed | tf_op | source)
XLA Modules:
  0.0 72.1 jit_solution(9496572479650528428)
XLA Ops:
  0.0 2.5 %observe.1 = bf16[8,48,256]{2,1,0:T(8,128)(2,1)} custom-call(s32[2,4]{1,0:T(2,128)} %index_ref.1, f32[2,4,32,128]{3,2,1,0:T(8,128)} %gate_ref.1, bf16[32,12288]{1,0:T(8,128)(2,1)} %state_ref.1), custom_call_target="tpu_custom_call" | custom-call | tf_op jit(solution)/shard_map/observe/pallas_call | solution.py:219
  2.5 0.0 copy-start.4
  2.5 4.3 %all-to-all-start = ((bf16[8,48,256]{2,1,0:T(8,128)(2,1)}), bf16[8,48,256]{2,1,0:T(8,128)(2,1)S(1)}, u32[]{:S(2)}, u32[]{:S(2)}) async-start(bf16[8,48,256]{2,1,0:T(8,128)(2,1)} %observe.1), calls=%async_computation | async-start | bytes 393216 | tf_op jit(solution)/shard_map/all_to_all | solution.py:317
  6.9 0.0 copy-done.4
  6.9 0.1 copy.12.counts_ref
  7.0 0.0 copy-start
  7.0 0.0 copy-start.2
  7.0 0.0 copy-start.3
  7.0 2.1 %copy.17 = bf16[4,8,8,1536]{3,2,0,1:T(8,128)(2,1)} copy(bf16[4,8,8,1536]{3,2,1,0:T(8,128)(2,1)} %bitcast.25) | data formatting | bytes 1572864 | tf_op jit(solution)/shard_map/reshape | solution.py:319
  9.1 0.0 copy-start.1
  9.1 0.0 copy-done
  9.1 0.0 copy-done.2
  9.1 0.0 copy-done.3
  9.1 0.7 copy-done.1
  9.8 0.8 %gather_small.1 = (f32[20,128]{1,0:T(8,128)S(1)}, f32[2,20,1536]{2,1,0:T(8,128)S(1)}, f32[6,128]{1,0:T(8,128)S(1)}) custom-call(s32[2,1]{1,0:T(2,128)S(1)} %copy.12.counts_ref, s32[2,4]{1,0:T(2,128)S(1)} %copy-done.1, s32[20,2,96]{2,1,0:T(2,128)S(1)} %bitcast.24, f32[2,128]{1,0:T(2,128)S(1)} %copy-done.2, f32[2,128]{1,0:T(2,128)S(1)} %copy-done.3), custom_call_target="tpu_custom_call" | custom-call | tf_op jit(solution)/shard_map/gather_small/pallas_call | solution.py:239
  10.6 3.1 %all-to-all-done.shared_ref = bf16[8,48,256]{2,1,0:T(8,128)(2,1)S(1)} async-done(((bf16[8,48,256]{2,1,0:T(8,128)(2,1)}), bf16[8,48,256]{2,1,0:T(8,128)(2,1)S(1)}, u32[]{:S(2)}, u32[]{:S(2)}) %all-to-all-start) | async-done | bytes 196640 | tf_op jit(solution)/shard_map/all_to_all | solution.py:317
  13.7 3.5 %all-to-all-start.1 = ((bf16[8,32,1536]{2,1,0:T(8,128)(2,1)}), bf16[8,32,1536]{2,1,0:T(8,128)(2,1)S(1)}, u32[]{:S(2)}, u32[]{:S(2)}) async-start(bf16[8,32,1536]{2,1,0:T(8,128)(2,1)} %bitcast.18), calls=%async_computation.1 | async-start | bytes 1572864 | tf_op jit(solution)/shard_map/all_to_all | solution.py:324
  17.3 0.2 first_pack.1.own_ref.refs_1_
  17.4 5.2 %collective-permute-start.1 = (bf16[272,128]{1,0:T(8,128)(2,1)S(1)}, bf16[272,128]{1,0:T(8,128)(2,1)S(1)}, u32[]{:S(2)}, u32[]{:S(2)}) collective-permute-start(bf16[272,128]{1,0:T(8,128)(2,1)S(1)} %first_pack.1.own_ref.refs_1_), channel_id=1, source_target_pairs={{0,16},{2,18},{4,20},{6,22},{8,24},{10,26},{12,28},{14,30},{16,0},... | collective-permute-start | bytes 208904 | tf_op jit(solution)/shard_map/ppermute | solution.py:303
  22.6 3.8 %collective-permute-start = (bf16[272,128]{1,0:T(8,128)(2,1)S(1)}, bf16[272,128]{1,0:T(8,128)(2,1)S(1)}, u32[]{:S(2)}, u32[]{:S(2)}) collective-permute-start(bf16[272,128]{1,0:T(8,128)(2,1)S(1)} %first_pack.1.own_ref.refs_1_), channel_id=1, source_target_pairs={{0,8},{2,10},{4,12},{6,14},{8,0},{9,17},{10,2},{11,19},{12,4},{13,... | collective-permute-start | bytes 208904 | tf_op jit(solution)/shard_map/ppermute | solution.py:303
  26.4 0.0 collective-permute-done.1
  26.5 2.4 %collective-permute-done = bf16[272,128]{1,0:T(8,128)(2,1)S(1)} collective-permute-done((bf16[272,128]{1,0:T(8,128)(2,1)S(1)}, bf16[272,128]{1,0:T(8,128)(2,1)S(1)}, u32[]{:S(2)}, u32[]{:S(2)}) %collective-permute-start) | collective-permute-done | bytes 69664 | tf_op jit(solution)/shard_map/ppermute | solution.py:303
  28.8 9.6 %all-gather = bf16[4,272,128]{2,1,0:T(8,128)(2,1)S(1)} all-gather(bf16[2,272,128]{2,1,0:T(8,128)(2,1)S(1)} %pad_maximum_fusion), channel_id=2, replica_groups={{0,1},{2,3},{4,5},{6,7},{8,9},{10,11},{12,13},{14,15},{16,17},{18,19},{..., dimensions={0}, use_global_device_ids=true | all-gather | bytes 417792 | tf_op jit(solution)/shard_map/all_gather | solution.py:310
  38.4 1.0 %second_pack.1.refs_1_ = bf16[272,128]{1,0:T(8,128)(2,1)S(1)} custom-call(f32[20,128]{1,0:T(8,128)S(1)} %get-tuple-element.24.flags_ref, bf16[8,48,256]{2,1,0:T(8,128)(2,1)S(1)} %all-to-all-done.shared_ref, bf16[272,128]{1,0:T(8,128)(2,1)S(1)} %first_pack.1.own_ref.refs_1_, bf16[2,2,272,128]{3,2,1,0:T(8,128)(2,1)S(1)} %bitcast.21, ...), custom_call_target="tpu_custom_call" | custom-call | tf_op jit(solution)/shard_map/second_pack/pallas_call | solution.py:265
  39.5 0.0 all-to-all-done.1
  39.5 1.9 %collective-permute-start.3 = (bf16[272,128]{1,0:T(8,128)(2,1)S(1)}, bf16[272,128]{1,0:T(8,128)(2,1)S(1)}, u32[]{:S(2)}, u32[]{:S(2)}) collective-permute-start(bf16[272,128]{1,0:T(8,128)(2,1)S(1)} %second_pack.1.refs_1_), channel_id=1, source_target_pairs={{0,16},{2,18},{4,20},{6,22},{8,24},{10,26},{12,28},{14,30},{16,0},... | collective-permute-start | bytes 208904 | tf_op jit(solution)/shard_map/ppermute | solution.py:303
  41.4 1.9 %collective-permute-start.2 = (bf16[272,128]{1,0:T(8,128)(2,1)S(1)}, bf16[272,128]{1,0:T(8,128)(2,1)S(1)}, u32[]{:S(2)}, u32[]{:S(2)}) collective-permute-start(bf16[272,128]{1,0:T(8,128)(2,1)S(1)} %second_pack.1.refs_1_), channel_id=1, source_target_pairs={{0,8},{2,10},{4,12},{6,14},{8,0},{9,17},{10,2},{11,19},{12,4},{13,... | collective-permute-start | bytes 208904 | tf_op jit(solution)/shard_map/ppermute | solution.py:303
  43.3 2.5 %update.2.refs_3_ = bf16[256,1536]{1,0:T(8,128)(2,1)S(1)} custom-call(f32[2,20,1536]{2,1,0:T(8,128)S(1)} %get-tuple-element.23.refs_0_, bf16[272,128]{1,0:T(8,128)(2,1)S(1)} %first_pack.1.own_ref.refs_1_, bf16[2,2,272,128]{3,2,1,0:T(8,128)(2,1)S(1)} %bitcast.22, bf16[256,1536]{1,0:T(8,128)(2,1)S(1)} %bitcast.19), custom_call_target="tpu_custom_call" | custom-call | tf_op jit(solution)/shard_map/update/pallas_call | solution.py:276
  45.8 0.8 %collective-permute-done.3 = bf16[272,128]{1,0:T(8,128)(2,1)S(1)} collective-permute-done((bf16[272,128]{1,0:T(8,128)(2,1)S(1)}, bf16[272,128]{1,0:T(8,128)(2,1)S(1)}, u32[]{:S(2)}, u32[]{:S(2)}) %collective-permute-start.3) | collective-permute-done | bytes 69664 | tf_op jit(solution)/shard_map/ppermute | solution.py:303
  46.6 1.0 %collective-permute-done.2 = bf16[272,128]{1,0:T(8,128)(2,1)S(1)} collective-permute-done((bf16[272,128]{1,0:T(8,128)(2,1)S(1)}, bf16[272,128]{1,0:T(8,128)(2,1)S(1)}, u32[]{:S(2)}, u32[]{:S(2)}) %collective-permute-start.2) | collective-permute-done | bytes 69664 | tf_op jit(solution)/shard_map/ppermute | solution.py:303
  47.6 3.2 %all-gather.1 = bf16[4,272,128]{2,1,0:T(8,128)(2,1)S(1)} all-gather(bf16[2,272,128]{2,1,0:T(8,128)(2,1)S(1)} %pad_maximum_fusion.1), channel_id=3, replica_groups={{0,1},{2,3},{4,5},{6,7},{8,9},{10,11},{12,13},{14,15},{16,17},{18,19},{..., dimensions={0}, use_global_device_ids=true | all-gather | bytes 417792 | tf_op jit(solution)/shard_map/all_gather | solution.py:310
  50.8 2.5 %update.3 = bf16[256,1536]{1,0:T(8,128)(2,1)S(1)} custom-call(f32[2,20,1536]{2,1,0:T(8,128)S(1)} %get-tuple-element.23.refs_0_, bf16[272,128]{1,0:T(8,128)(2,1)S(1)} %second_pack.1.refs_1_, bf16[2,2,272,128]{3,2,1,0:T(8,128)(2,1)S(1)} %bitcast.23, bf16[256,1536]{1,0:T(8,128)(2,1)S(1)} %update.2.refs_3_), custom_call_target="tpu_custom_call" | custom-call | tf_op jit(solution)/shard_map/update/pallas_call | solution.py:276
  53.3 17.8 %all_to_all.15 = bf16[8,32,1536]{2,1,0:T(8,128)(2,1)S(1)} all-to-all(bf16[8,32,1536]{2,1,0:T(8,128)(2,1)S(1)} %bitcast.20), channel_id=1, replica_groups=mesh['space'=64,'mem'=8] {'mem'}, dimensions={0} | all-to-all | bytes 1572864 | tf_op jit(solution)/shard_map/all_to_all | solution.py:335
  71.1 0.9 %copy.15 = bf16[8,4,8,1536]{3,2,0,1:T(8,128)(2,1)} copy(bf16[8,4,8,1536]{3,2,1,0:T(8,128)(2,1)S(1)} %bitcast.26) | data formatting | bytes 1572864 | tf_op jit(solution)/shard_map/reshape | solution.py:338
  (2 shorter events, 0.0 us)
Async XLA Ops:
  2.5 4.3 %copy-start.4 = (s32[2,1]{0,1:T(1,128)S(1)}, s32[2,1]{0,1:T(1,128)}, u32[]{:S(2)}) copy-start(s32[2,1]{0,1:T(1,128)} %param.8) | copy-start | bytes 28
  2.5 11.2 %all-to-all-start = ((bf16[8,48,256]{2,1,0:T(8,128)(2,1)}), bf16[8,48,256]{2,1,0:T(8,128)(2,1)S(1)}, u32[]{:S(2)}, u32[]{:S(2)}) async-start(bf16[8,48,256]{2,1,0:T(8,128)(2,1)} %observe.1), calls=%async_computation | async-start | bytes 393216 | tf_op jit(solution)/shard_map/all_to_all | solution.py:317
  7.0 2.1 %copy-start = (s32[2,96,20]{1,0,2:T(2,128)S(1)}, s32[2,96,20]{1,0,2:T(2,128)}, u32[]{:S(2)}) copy-start(s32[2,96,20]{1,0,2:T(2,128)} %param.13) | copy-start | bytes 46084
  7.0 2.1 %copy-start.2 = (f32[2,128]{1,0:T(2,128)S(1)}, f32[2,128]{1,0:T(2,128)}, u32[]{:S(2)}) copy-start(f32[2,128]{1,0:T(2,128)} %observed_ref.1) | copy-start | bytes 3076
  7.0 2.1 %copy-start.3 = (f32[2,128]{1,0:T(2,128)S(1)}, f32[2,128]{1,0:T(2,128)}, u32[]{:S(2)}) copy-start(f32[2,128]{1,0:T(2,128)} %error_ref.1) | copy-start | bytes 3076
  9.1 0.7 copy-start.1
  13.7 25.8 %all-to-all-start.1 = ((bf16[8,32,1536]{2,1,0:T(8,128)(2,1)}), bf16[8,32,1536]{2,1,0:T(8,128)(2,1)S(1)}, u32[]{:S(2)}, u32[]{:S(2)}) async-start(bf16[8,32,1536]{2,1,0:T(8,128)(2,1)} %bitcast.18), calls=%async_computation.1 | async-start | bytes 1572864 | tf_op jit(solution)/shard_map/all_to_all | solution.py:324
  17.4 9.0 %collective-permute-start.1 = (bf16[272,128]{1,0:T(8,128)(2,1)S(1)}, bf16[272,128]{1,0:T(8,128)(2,1)S(1)}, u32[]{:S(2)}, u32[]{:S(2)}) collective-permute-start(bf16[272,128]{1,0:T(8,128)(2,1)S(1)} %first_pack.1.own_ref.refs_1_), channel_id=1, source_target_pairs={{0,16},{2,18},{4,20},{6,22},{8,24},{10,26},{12,28},{14,30},{16,0},... | collective-permute-start | bytes 208904 | tf_op jit(solution)/shard_map/ppermute | solution.py:303
  22.6 6.2 %collective-permute-start = (bf16[272,128]{1,0:T(8,128)(2,1)S(1)}, bf16[272,128]{1,0:T(8,128)(2,1)S(1)}, u32[]{:S(2)}, u32[]{:S(2)}) collective-permute-start(bf16[272,128]{1,0:T(8,128)(2,1)S(1)} %first_pack.1.own_ref.refs_1_), channel_id=1, source_target_pairs={{0,8},{2,10},{4,12},{6,14},{8,0},{9,17},{10,2},{11,19},{12,4},{13,... | collective-permute-start | bytes 208904 | tf_op jit(solution)/shard_map/ppermute | solution.py:303
  39.5 7.1 %collective-permute-start.3 = (bf16[272,128]{1,0:T(8,128)(2,1)S(1)}, bf16[272,128]{1,0:T(8,128)(2,1)S(1)}, u32[]{:S(2)}, u32[]{:S(2)}) collective-permute-start(bf16[272,128]{1,0:T(8,128)(2,1)S(1)} %second_pack.1.refs_1_), channel_id=1, source_target_pairs={{0,16},{2,18},{4,20},{6,22},{8,24},{10,26},{12,28},{14,30},{16,0},... | collective-permute-start | bytes 208904 | tf_op jit(solution)/shard_map/ppermute | solution.py:303
  41.4 6.2 %collective-permute-start.2 = (bf16[272,128]{1,0:T(8,128)(2,1)S(1)}, bf16[272,128]{1,0:T(8,128)(2,1)S(1)}, u32[]{:S(2)}, u32[]{:S(2)}) collective-permute-start(bf16[272,128]{1,0:T(8,128)(2,1)S(1)} %second_pack.1.refs_1_), channel_id=1, source_target_pairs={{0,8},{2,10},{4,12},{6,14},{8,0},{9,17},{10,2},{11,19},{12,4},{13,... | collective-permute-start | bytes 208904 | tf_op jit(solution)/shard_map/ppermute | solution.py:303

commit v5 on v4

--- a/solution.py
+++ b/solution.py
@@ -27,28 +27,23 @@
     return lax.dot_general(a, b, (dims, ((), ())), preferred_element_type=F32)
 
 
-def observe_kernel(index_hbm, gate_ref, state_ref, out_ref, index_ref, gate, picks, index_sem, gate_sem, sems):
-    mem_dev = state_ref.shape[0]
+def observe_kernel(index_hbm, gate_hbm, state_hbm, out_ref, index_ref, gate, state, index_sem, gate_sem, state_sem):
     index_copy = pltpu.make_async_copy(index_hbm, index_ref, index_sem)
-    index_copy.start()
-    gate_copy = pltpu.make_async_copy(gate_ref, gate, gate_sem)
-    gate_copy.start()
-    index_copy.wait()
-    copies = []
+    gate_copy = pltpu.make_async_copy(gate_hbm, gate, gate_sem)
+    state_copy = pltpu.make_async_copy(state_hbm, state, state_sem)
+    copies = [index_copy, state_copy, gate_copy]
+    for copy in copies:
+        copy.start()
+    for copy in copies:
+        copy.wait()
+    mem_dev = state.shape[0]
+    high, low = two_parts(gate[...].reshape(BATCHES * CAPB * OB, BLK))
+    picks = []
     for k in range(BATCHES):
         for c in range(CAPB):
-            n = k * CAPB + c
             start = pl.multiple_of(index_ref[k, c] * BLK, BLK)
-            copies.append(
-                pltpu.make_async_copy(state_ref.at[:, pl.ds(start, BLK)], picks.at[n], sems.at[n])
-            )
-    for copy in copies:
-        copy.start()
-    gate_copy.wait()
-    high, low = two_parts(gate[...].reshape(BATCHES * CAPB * OB, BLK))
-    for copy in copies:
-        copy.wait()
-    rows = picks[...].reshape(BATCHES * CAPB * mem_dev, BLK)
+            picks.append(state[:, pl.ds(start, BLK)])
+    rows = jnp.concatenate(picks, 0)
     each = dot(rows, high.astype(BF16), ((1,), (1,))) + dot(rows, low.astype(BF16), ((1,), (1,)))
     lane_block = lax.broadcasted_iota(jnp.int32, (mem_dev, BATCHES * SLOTS), 1) // OB
     prior = jnp.zeros((mem_dev, BATCHES * SLOTS), F32)
@@ -122,13 +117,13 @@
 
 def window(own_ref, around_ref):
     tile = lax.axis_index("space")
-    below, below_two = 1 - tile % 2, 1 - tile // 2 % 2
+    odd, upper = tile % 2, tile // 2 % 2
     return [
         (0, own_ref),
-        (-1, around_ref.at[below, 0]),
-        (-2, around_ref.at[below_two, 1]),
-        (1, around_ref.at[1 - below, 0]),
-        (2, around_ref.at[1 - below_two, 1]),
+        (-1, around_ref.at[3 - 3 * odd]),
+        (-2, around_ref.at[1 + upper]),
+        (1, around_ref.at[3 * odd]),
+        (2, around_ref.at[2 - upper]),
     ]
 
 
@@ -224,10 +219,10 @@
         scratch_shapes=[
             pltpu.SMEM(block_index.shape, jnp.int32),
             pltpu.VMEM(gate_operator.shape, F32),
-            pltpu.VMEM((BATCHES * CAPB, mem_dev, BLK), BF16),
+            pltpu.VMEM(prior_state.shape, BF16),
             pltpu.SemaphoreType.DMA(()),
             pltpu.SemaphoreType.DMA(()),
-            pltpu.SemaphoreType.DMA((BATCHES * CAPB,)),
+            pltpu.SemaphoreType.DMA(()),
         ],
         compiler_params=pltpu.CompilerParams(vmem_limit_bytes=64 * 1024 * 1024 - 65536),
         name="observe",
@@ -289,25 +284,27 @@
     )(flags, own, around, state)
 
 
+def swapped(pack, across):
+    tiles, groups = lax.axis_size("space"), lax.axis_size("mem")
+    pairs = []
+    for tile in range(tiles):
+        for m in range(groups):
+            offset = 1 if m % 2 == across else 2
+            above = tile // offset % 2 == across
+            partner = tile + offset if above else tile - offset
+            if 0 <= partner < tiles:
+                pairs.append((tile * groups + m, partner * groups + m))
+    return lax.ppermute(pack, ("space", "mem"), pairs)
+
+
 def passed_around(pack):
-    tiles, groups = lax.axis_size("space"), lax.axis_size("mem")
-    received = []
-    for offset in (1, 2):
-        pairs = []
-        for tile in range(tiles):
-            for m in range(groups):
-                above = (tile // offset + m) % 2 == 0
-                partner = tile + offset if above else tile - offset
-                if 0 <= partner < tiles:
-                    pairs.append((tile * groups + m, partner * groups + m))
-        received.append(lax.ppermute(pack, ("space", "mem"), pairs))
-    return jnp.stack(received)
+    return jnp.stack([swapped(pack, 0), swapped(pack, 1)])
 
 
 def chip_shared(received):
     groups = lax.axis_size("mem")
     chips = [[2 * chip, 2 * chip + 1] for chip in range(groups // 2)]
-    return lax.all_gather(received, "mem", axis=0, axis_index_groups=chips)
+    return lax.all_gather(received, "mem", axis=0, axis_index_groups=chips, tiled=True)
 
 
 def per_device(prior_state, block_counts, block_index, gate_operator, observed, obs_error, local_mask):

time: 72.6 us -> 72.2 us (level)
  blocking collectives: 30.5 us -> 21.9 us
  starting transfers between devices: 20.7 us -> 29 us
    all_gather x2, blocking collectives: 12.8 us -> 4.01 us  [chip_shared(): lax.all_gather(received, 'mem', axis=0, axis_index_groups=chips, tiled=True)]
    ppermute x4, starting transfers between devices: 12.8 us -> 21.1 us  [swapped(): return lax.ppermute(pack, ('space', 'mem'), pairs)]
where the time goes in v5:
time: 72.2 us; the launch traced here: 71.8 us
  starting transfers between devices  29 us (40%)
  blocking collectives  21.9 us (30%)
  Pallas kernels  9.15 us (13%)
  waiting for transfers between devices  7.78 us (11%)
  local copies, waits for them, and re-layouts  3.84 us (5%)
    ppermute x4, starting transfers between devices, swapped(): return lax.ppermute(pack, ('space', 'mem'), pairs)  21.1 us
    all_to_all x1, blocking collectives, per_device(): lax.all_to_all(state.reshape(groups, mem_dev, cells // groups), 'mem', sp...  17.8 us
    pallas_call x2, Pallas kernels, update(): pl.pallas_call(lambda *refs: update_kernel(batch_id, *refs), in_specs=[VM...  5.01 us
    ppermute x4, waiting for transfers between devices, swapped(): return lax.ppermute(pack, ('space', 'mem'), pairs)  4.67 us
    all_to_all x1, starting transfers between devices, per_device(): lax.all_to_all(own_block, 'mem', split_axis=0, concat_axis=0, tiled=True)  4.31 us
    all_gather x2, blocking collectives, chip_shared(): lax.all_gather(received, 'mem', axis=0, axis_index_groups=chips, tiled=True)  4.01 us
    all_to_all x1, starting transfers between devices, per_device(): lax.all_to_all(moved, 'mem', split_axis=0, concat_axis=0, tiled=True)  3.55 us
    all_to_all x1, waiting for transfers between devices, per_device(): lax.all_to_all(own_block, 'mem', split_axis=0, concat_axis=0, tiled=True)  3.11 us
  transfers between devices with their start and end apart: 6, of which 4 were waited for; matrix products, arithmetic and copies ran while one was open for 3% of the time, Pallas kernels for 6%

profile of v5, /device:TPU:24, one launch (start us, length us, event | category | flops | bytes accessed | tf_op | source)
XLA Modules:
  0.0 71.8 jit_solution(15833999527865423276)
XLA Ops:
  0.0 2.1 %observe.1 = bf16[8,48,256]{2,1,0:T(8,128)(2,1)} custom-call(s32[2,4]{1,0:T(2,128)} %index_ref.1, f32[2,4,32,128]{3,2,1,0:T(8,128)} %gate_hbm.1, bf16[32,12288]{1,0:T(8,128)(2,1)} %state_hbm.1), custom_call_target="tpu_custom_call" | custom-call | tf_op jit(solution)/shard_map/observe/pallas_call | solution.py:214
  2.1 0.0 copy-start.4
  2.1 4.3 %all-to-all-start = ((bf16[8,48,256]{2,1,0:T(8,128)(2,1)}), bf16[8,48,256]{2,1,0:T(8,128)(2,1)S(1)}, u32[]{:S(2)}, u32[]{:S(2)}) async-start(bf16[8,48,256]{2,1,0:T(8,128)(2,1)} %observe.1), calls=%async_computation | async-start | bytes 393216 | tf_op jit(solution)/shard_map/all_to_all | solution.py:314
  6.4 0.0 copy-done.4
  6.4 0.1 copy.12.counts_ref
  6.5 0.0 copy-start
  6.5 0.0 copy-start.2
  6.5 0.0 copy-start.3
  6.5 2.1 %copy.17 = bf16[4,8,8,1536]{3,2,0,1:T(8,128)(2,1)} copy(bf16[4,8,8,1536]{3,2,1,0:T(8,128)(2,1)} %bitcast.20) | data formatting | bytes 1572864 | tf_op jit(solution)/shard_map/reshape | solution.py:316
  8.7 0.0 copy-start.1
  8.7 0.0 copy-done
  8.7 0.0 copy-done.2
  8.7 0.0 copy-done.3
  8.7 0.7 copy-done.1
  9.3 0.8 %gather_small.1 = (f32[20,128]{1,0:T(8,128)S(1)}, f32[2,20,1536]{2,1,0:T(8,128)S(1)}, f32[6,128]{1,0:T(8,128)S(1)}) custom-call(s32[2,1]{1,0:T(2,128)S(1)} %copy.12.counts_ref, s32[2,4]{1,0:T(2,128)S(1)} %copy-done.1, s32[20,2,96]{2,1,0:T(2,128)S(1)} %bitcast.19, f32[2,128]{1,0:T(2,128)S(1)} %copy-done.2, f32[2,128]{1,0:T(2,128)S(1)} %copy-done.3), custom_call_target="tpu_custom_call" | custom-call | tf_op jit(solution)/shard_map/gather_small/pallas_call | solution.py:234
  10.2 3.1 %all-to-all-done.shared_ref = bf16[8,48,256]{2,1,0:T(8,128)(2,1)S(1)} async-done(((bf16[8,48,256]{2,1,0:T(8,128)(2,1)}), bf16[8,48,256]{2,1,0:T(8,128)(2,1)S(1)}, u32[]{:S(2)}, u32[]{:S(2)}) %all-to-all-start) | async-done | bytes 196640 | tf_op jit(solution)/shard_map/all_to_all | solution.py:314
  13.3 3.5 %all-to-all-start.1 = ((bf16[8,32,1536]{2,1,0:T(8,128)(2,1)}), bf16[8,32,1536]{2,1,0:T(8,128)(2,1)S(1)}, u32[]{:S(2)}, u32[]{:S(2)}) async-start(bf16[8,32,1536]{2,1,0:T(8,128)(2,1)} %bitcast.16), calls=%async_computation.1 | async-start | bytes 1572864 | tf_op jit(solution)/shard_map/all_to_all | solution.py:321
  16.8 0.2 first_pack.1.own_ref.refs_1_
  17.0 12.0 %collective-permute-start.1 = (bf16[272,128]{1,0:T(8,128)(2,1)S(1)}, bf16[272,128]{1,0:T(8,128)(2,1)S(1)}, u32[]{:S(2)}, u32[]{:S(2)}) collective-permute-start(bf16[272,128]{1,0:T(8,128)(2,1)S(1)} %first_pack.1.own_ref.refs_1_), channel_id=1, source_target_pairs={{9,17},{11,19},{13,21},{15,23},{16,32},{17,9},{18,34},{19,11},{20,... | collective-permute-start | bytes 208904 | tf_op jit(solution)/shard_map/ppermute | solution.py:297
  29.0 2.9 %collective-permute-start = (bf16[272,128]{1,0:T(8,128)(2,1)S(1)}, bf16[272,128]{1,0:T(8,128)(2,1)S(1)}, u32[]{:S(2)}, u32[]{:S(2)}) collective-permute-start(bf16[272,128]{1,0:T(8,128)(2,1)S(1)} %first_pack.1.own_ref.refs_1_), channel_id=1, source_target_pairs={{0,8},{1,17},{2,10},{3,19},{4,12},{5,21},{6,14},{7,23},{8,0},{9,25... | collective-permute-start | bytes 208904 | tf_op jit(solution)/shard_map/ppermute | solution.py:297
  32.0 0.0 collective-permute-done.1
  32.0 3.6 %collective-permute-done = bf16[272,128]{1,0:T(8,128)(2,1)S(1)} collective-permute-done((bf16[272,128]{1,0:T(8,128)(2,1)S(1)}, bf16[272,128]{1,0:T(8,128)(2,1)S(1)}, u32[]{:S(2)}, u32[]{:S(2)}) %collective-permute-start) | collective-permute-done | bytes 69664 | tf_op jit(solution)/shard_map/ppermute | solution.py:297
  35.6 2.0 %all_gather.6.around_ref.refs_2_ = bf16[4,272,128]{2,1,0:T(8,128)(2,1)S(1)} all-gather(bf16[2,272,128]{2,1,0:T(8,128)(2,1)S(1)} %pad_maximum_fusion), channel_id=1, replica_groups={{0,1},{2,3},{4,5},{6,7},{8,9},{10,11},{12,13},{14,15},{16,17},{18,19},{..., dimensions={0}, use_global_device_ids=true | all-gather | bytes 417792 | tf_op jit(solution)/shard_map/all_gather | solution.py:307
  37.6 1.1 %second_pack.1.refs_1_ = bf16[272,128]{1,0:T(8,128)(2,1)S(1)} custom-call(f32[20,128]{1,0:T(8,128)S(1)} %get-tuple-element.24.flags_ref, bf16[8,48,256]{2,1,0:T(8,128)(2,1)S(1)} %all-to-all-done.shared_ref, bf16[272,128]{1,0:T(8,128)(2,1)S(1)} %first_pack.1.own_ref.refs_1_, bf16[4,272,128]{2,1,0:T(8,128)(2,1)S(1)} %all_gather.6.around_ref.refs_2_, ...), custom_call_target="tpu_custom_call" | custom-call | tf_op jit(solution)/shard_map/second_pack/pallas_call | solution.py:260
  38.7 0.0 all-to-all-done.1
  38.7 3.4 %collective-permute-start.3 = (bf16[272,128]{1,0:T(8,128)(2,1)S(1)}, bf16[272,128]{1,0:T(8,128)(2,1)S(1)}, u32[]{:S(2)}, u32[]{:S(2)}) collective-permute-start(bf16[272,128]{1,0:T(8,128)(2,1)S(1)} %second_pack.1.refs_1_), channel_id=1, source_target_pairs={{9,17},{11,19},{13,21},{15,23},{16,32},{17,9},{18,34},{19,11},{20,... | collective-permute-start | bytes 208904 | tf_op jit(solution)/shard_map/ppermute | solution.py:297
  42.1 2.8 %collective-permute-start.2 = (bf16[272,128]{1,0:T(8,128)(2,1)S(1)}, bf16[272,128]{1,0:T(8,128)(2,1)S(1)}, u32[]{:S(2)}, u32[]{:S(2)}) collective-permute-start(bf16[272,128]{1,0:T(8,128)(2,1)S(1)} %second_pack.1.refs_1_), channel_id=1, source_target_pairs={{0,8},{1,17},{2,10},{3,19},{4,12},{5,21},{6,14},{7,23},{8,0},{9,25... | collective-permute-start | bytes 208904 | tf_op jit(solution)/shard_map/ppermute | solution.py:297
  44.9 2.5 %update.2.refs_3_ = bf16[256,1536]{1,0:T(8,128)(2,1)S(1)} custom-call(f32[2,20,1536]{2,1,0:T(8,128)S(1)} %get-tuple-element.23.refs_0_, bf16[272,128]{1,0:T(8,128)(2,1)S(1)} %first_pack.1.own_ref.refs_1_, bf16[4,272,128]{2,1,0:T(8,128)(2,1)S(1)} %all_gather.6.around_ref.refs_2_, bf16[256,1536]{1,0:T(8,128)(2,1)S(1)} %bitcast.17), custom_call_target="tpu_custom_call" | custom-call | tf_op jit(solution)/shard_map/update/pallas_call | solution.py:271
  47.3 0.5 collective-permute-done.3
  47.9 0.5 collective-permute-done.2
  48.4 2.0 %all_gather.7.refs_2_ = bf16[4,272,128]{2,1,0:T(8,128)(2,1)S(1)} all-gather(bf16[2,272,128]{2,1,0:T(8,128)(2,1)S(1)} %pad_maximum_fusion.1), channel_id=1, replica_groups={{0,1},{2,3},{4,5},{6,7},{8,9},{10,11},{12,13},{14,15},{16,17},{18,19},{..., dimensions={0}, use_global_device_ids=true | all-gather | bytes 417792 | tf_op jit(solution)/shard_map/all_gather | solution.py:307
  50.4 2.5 %update.3 = bf16[256,1536]{1,0:T(8,128)(2,1)S(1)} custom-call(f32[2,20,1536]{2,1,0:T(8,128)S(1)} %get-tuple-element.23.refs_0_, bf16[272,128]{1,0:T(8,128)(2,1)S(1)} %second_pack.1.refs_1_, bf16[4,272,128]{2,1,0:T(8,128)(2,1)S(1)} %all_gather.7.refs_2_, bf16[256,1536]{1,0:T(8,128)(2,1)S(1)} %update.2.refs_3_), custom_call_target="tpu_custom_call" | custom-call | tf_op jit(solution)/shard_map/update/pallas_call | solution.py:271
  53.0 17.8 %all_to_all.15 = bf16[8,32,1536]{2,1,0:T(8,128)(2,1)S(1)} all-to-all(bf16[8,32,1536]{2,1,0:T(8,128)(2,1)S(1)} %bitcast.18), channel_id=1, replica_groups=mesh['space'=64,'mem'=8] {'mem'}, dimensions={0} | all-to-all | bytes 1572864 | tf_op jit(solution)/shard_map/all_to_all | solution.py:332
  70.8 0.9 %copy.15 = bf16[8,4,8,1536]{3,2,0,1:T(8,128)(2,1)} copy(bf16[8,4,8,1536]{3,2,1,0:T(8,128)(2,1)S(1)} %bitcast.21) | data formatting | bytes 1572864 | tf_op jit(solution)/shard_map/reshape | solution.py:335
  (2 shorter events, 0.0 us)
Async XLA Ops:
  2.1 4.3 %copy-start.4 = (s32[2,1]{0,1:T(1,128)S(1)}, s32[2,1]{0,1:T(1,128)}, u32[]{:S(2)}) copy-start(s32[2,1]{0,1:T(1,128)} %param.8) | copy-start | bytes 28
  2.1 11.2 %all-to-all-start = ((bf16[8,48,256]{2,1,0:T(8,128)(2,1)}), bf16[8,48,256]{2,1,0:T(8,128)(2,1)S(1)}, u32[]{:S(2)}, u32[]{:S(2)}) async-start(bf16[8,48,256]{2,1,0:T(8,128)(2,1)} %observe.1), calls=%async_computation | async-start | bytes 393216 | tf_op jit(solution)/shard_map/all_to_all | solution.py:314
  6.5 2.1 %copy-start = (s32[2,96,20]{1,0,2:T(2,128)S(1)}, s32[2,96,20]{1,0,2:T(2,128)}, u32[]{:S(2)}) copy-start(s32[2,96,20]{1,0,2:T(2,128)} %param.13) | copy-start | bytes 46084
  6.5 2.1 %copy-start.2 = (f32[2,128]{1,0:T(2,128)S(1)}, f32[2,128]{1,0:T(2,128)}, u32[]{:S(2)}) copy-start(f32[2,128]{1,0:T(2,128)} %observed_ref.1) | copy-start | bytes 3076
  6.5 2.1 %copy-start.3 = (f32[2,128]{1,0:T(2,128)S(1)}, f32[2,128]{1,0:T(2,128)}, u32[]{:S(2)}) copy-start(f32[2,128]{1,0:T(2,128)} %error_ref.1) | copy-start | bytes 3076
  8.7 0.7 copy-start.1
  13.3 25.4 %all-to-all-start.1 = ((bf16[8,32,1536]{2,1,0:T(8,128)(2,1)}), bf16[8,32,1536]{2,1,0:T(8,128)(2,1)S(1)}, u32[]{:S(2)}, u32[]{:S(2)}) async-start(bf16[8,32,1536]{2,1,0:T(8,128)(2,1)} %bitcast.16), calls=%async_computation.1 | async-start | bytes 1572864 | tf_op jit(solution)/shard_map/all_to_all | solution.py:321
  17.0 15.0 %collective-permute-start.1 = (bf16[272,128]{1,0:T(8,128)(2,1)S(1)}, bf16[272,128]{1,0:T(8,128)(2,1)S(1)}, u32[]{:S(2)}, u32[]{:S(2)}) collective-permute-start(bf16[272,128]{1,0:T(8,128)(2,1)S(1)} %first_pack.1.own_ref.refs_1_), channel_id=1, source_target_pairs={{9,17},{11,19},{13,21},{15,23},{16,32},{17,9},{18,34},{19,11},{20,... | collective-permute-start | bytes 208904 | tf_op jit(solution)/shard_map/ppermute | solution.py:297
  29.0 6.6 %collective-permute-start = (bf16[272,128]{1,0:T(8,128)(2,1)S(1)}, bf16[272,128]{1,0:T(8,128)(2,1)S(1)}, u32[]{:S(2)}, u32[]{:S(2)}) collective-permute-start(bf16[272,128]{1,0:T(8,128)(2,1)S(1)} %first_pack.1.own_ref.refs_1_), channel_id=1, source_target_pairs={{0,8},{1,17},{2,10},{3,19},{4,12},{5,21},{6,14},{7,23},{8,0},{9,25... | collective-permute-start | bytes 208904 | tf_op jit(solution)/shard_map/ppermute | solution.py:297
  38.7 9.2 %collective-permute-start.3 = (bf16[272,128]{1,0:T(8,128)(2,1)S(1)}, bf16[272,128]{1,0:T(8,128)(2,1)S(1)}, u32[]{:S(2)}, u32[]{:S(2)}) collective-permute-start(bf16[272,128]{1,0:T(8,128)(2,1)S(1)} %second_pack.1.refs_1_), channel_id=1, source_target_pairs={{9,17},{11,19},{13,21},{15,23},{16,32},{17,9},{18,34},{19,11},{20,... | collective-permute-start | bytes 208904 | tf_op jit(solution)/shard_map/ppermute | solution.py:297
  42.1 6.3 %collective-permute-start.2 = (bf16[272,128]{1,0:T(8,128)(2,1)S(1)}, bf16[272,128]{1,0:T(8,128)(2,1)S(1)}, u32[]{:S(2)}, u32[]{:S(2)}) collective-permute-start(bf16[272,128]{1,0:T(8,128)(2,1)S(1)} %second_pack.1.refs_1_), channel_id=1, source_target_pairs={{0,8},{1,17},{2,10},{3,19},{4,12},{5,21},{6,14},{7,23},{8,0},{9,25... | collective-permute-start | bytes 208904 | tf_op jit(solution)/shard_map/ppermute | solution.py:297

commit v6 on v5

--- a/solution.py
+++ b/solution.py
@@ -6,13 +6,12 @@
 from jax.sharding import PartitionSpec as P
 
 MEMBERS = 256
+ROW = 16
 BLK = 128
 OB = 32
 CAPB = 4
-SB = 96
 SLOTS = 128
 BATCHES = 2
-ROWS = 48
 PACK = 272
 F32 = jnp.float32
 BF16 = jnp.bfloat16
@@ -49,13 +48,8 @@
     prior = jnp.zeros((mem_dev, BATCHES * SLOTS), F32)
     for n in range(BATCHES * CAPB):
         prior = jnp.where(lane_block == n, each[n * mem_dev : (n + 1) * mem_dev], prior)
-    mean = jnp.sum(prior, 0, keepdims=True) / mem_dev
-    mean_high, mean_low = two_parts(mean)
-    row = lax.broadcasted_iota(jnp.int32, (ROWS - mem_dev, BATCHES * SLOTS), 0)
-    tail = jnp.where(row == 0, mean_high, jnp.where(row == 1, mean_low, 0.0))
-    block = jnp.concatenate([prior - mean, tail], 0).astype(BF16)
     for g in range(out_ref.shape[0]):
-        out_ref[g] = block
+        out_ref[g] = prior
 
 
 def gather_small_kernel(counts_ref, index_ref, mask_ref, observed_ref, error_ref, between_ref, own_ref, slots_ref):
@@ -78,14 +72,9 @@
 
 
 def members_of(shared_ref, batch_id):
-    groups = shared_ref.shape[0]
-    mem_dev = MEMBERS // groups
+    groups, mem_dev, _ = shared_ref.shape
     lanes = slice(batch_id * SLOTS, (batch_id + 1) * SLOTS)
-    parts = []
-    for g in range(groups):
-        block = shared_ref[g, :, lanes].astype(F32)
-        parts.append(block[:mem_dev] + (block[mem_dev : mem_dev + 1] + block[mem_dev + 1 : mem_dev + 2]))
-    return jnp.concatenate(parts, 0)
+    return shared_ref[:, :, lanes].reshape(groups * mem_dev, SLOTS)
 
 
 def store_packed(out_ref, prior, slots):
@@ -215,7 +204,7 @@
         observe_kernel,
         in_specs=[anywhere, anywhere, anywhere],
         out_specs=VM,
-        out_shape=jax.ShapeDtypeStruct((groups, ROWS, BATCHES * SLOTS), BF16),
+        out_shape=jax.ShapeDtypeStruct((groups, mem_dev, BATCHES * SLOTS), F32),
         scratch_shapes=[
             pltpu.SMEM(block_index.shape, jnp.int32),
             pltpu.VMEM(gate_operator.shape, F32),
@@ -284,21 +273,28 @@
     )(flags, own, around, state)
 
 
-def swapped(pack, across):
+def partner_of(tile, m, across):
+    offset = 1 if m % 2 == across else 2
+    return tile + offset if tile // offset % 2 == across else tile - offset
+
+
+def swapped(pack, across, wanted):
     tiles, groups = lax.axis_size("space"), lax.axis_size("mem")
     pairs = []
     for tile in range(tiles):
         for m in range(groups):
-            offset = 1 if m % 2 == across else 2
-            above = tile // offset % 2 == across
-            partner = tile + offset if above else tile - offset
-            if 0 <= partner < tiles:
+            partner = partner_of(tile, m, across)
+            if 0 <= partner < tiles and wanted(tile):
                 pairs.append((tile * groups + m, partner * groups + m))
     return lax.ppermute(pack, ("space", "mem"), pairs)
 
 
 def passed_around(pack):
-    return jnp.stack([swapped(pack, 0), swapped(pack, 1)])
+    starts = swapped(pack, 0, lambda tile: tile % ROW < ROW // 2)
+    across = swapped(pack, 1, lambda tile: True)
+    ends = swapped(pack, 0, lambda tile: tile % ROW >= ROW // 2)
+    first = lax.optimization_barrier(jnp.stack([across, starts]))
+    return jnp.stack([first[1] + ends, first[0]])
 
 
 def chip_shared(received):

time: 72.2 us -> 72.7 us (level)
  starting transfers between devices: 29 us -> 29.9 us
    ppermute x4 -> x6, waiting for transfers between devices: 4.67 us -> 3.73 us  [swapped(): return lax.ppermute(pack, ('space', 'mem'), pairs)]
    ppermute x4 -> x6, starting transfers between devices: 21.1 us -> 22.1 us  [swapped(): return lax.ppermute(pack, ('space', 'mem'), pairs)]
  transfers between devices with their start and end apart: 6 -> 8, of which waited for: 4 -> 3; matrix products, arithmetic and copies ran while one was open for 3% -> 3% of each run, Pallas kernels for 6% -> 6%
where the time goes in v6:
time: 72.7 us; the launch traced here: 72.2 us
  starting transfers between devices  29.9 us (41%)
  blocking collectives  21.5 us (30%)
  Pallas kernels  9.1 us (13%)
  waiting for transfers between devices  7.54 us (10%)
  local copies, waits for them, and re-layouts  3.85 us (5%)
    ppermute x6, starting transfers between devices, swapped(): return lax.ppermute(pack, ('space', 'mem'), pairs)  22.1 us
    all_to_all x1, blocking collectives, per_device(): lax.all_to_all(state.reshape(groups, mem_dev, cells // groups), 'mem', sp...  17.5 us
    pallas_call x2, Pallas kernels, update(): pl.pallas_call(lambda *refs: update_kernel(batch_id, *refs), in_specs=[VM...  4.97 us
    all_to_all x1, starting transfers between devices, per_device(): lax.all_to_all(own_block, 'mem', split_axis=0, concat_axis=0, tiled=True)  4.31 us
    all_gather x2, blocking collectives, chip_shared(): lax.all_gather(received, 'mem', axis=0, axis_index_groups=chips, tiled=True)  4.01 us
    all_to_all x1, waiting for transfers between devices, per_device(): lax.all_to_all(own_block, 'mem', split_axis=0, concat_axis=0, tiled=True)  3.81 us
    ppermute x6, waiting for transfers between devices, swapped(): return lax.ppermute(pack, ('space', 'mem'), pairs)  3.73 us
    all_to_all x1, starting transfers between devices, per_device(): lax.all_to_all(moved, 'mem', split_axis=0, concat_axis=0, tiled=True)  3.55 us
  transfers between devices with their start and end apart: 8, of which 3 were waited for; matrix products, arithmetic and copies ran while one was open for 3% of the time, Pallas kernels for 6%

profile of v6, /device:TPU:24, one launch (start us, length us, event | category | flops | bytes accessed | tf_op | source)
XLA Modules:
  0.0 72.2 jit_solution(5889333844942393575)
XLA Ops:
  0.0 2.1 %observe.1 = f32[8,32,256]{2,1,0:T(8,128)} custom-call(s32[2,4]{1,0:T(2,128)} %index_ref.1, f32[2,4,32,128]{3,2,1,0:T(8,128)} %gate_hbm.1, bf16[32,12288]{1,0:T(8,128)(2,1)} %state_hbm.1), custom_call_target="tpu_custom_call" | custom-call | tf_op jit(solution)/shard_map/observe/pallas_call | solution.py:203
  2.1 0.0 copy-start.4
  2.1 4.3 %all-to-all-start = ((f32[8,32,256]{2,1,0:T(8,128)}), f32[8,32,256]{2,1,0:T(8,128)S(1)}, u32[]{:S(2)}, u32[]{:S(2)}) async-start(f32[8,32,256]{2,1,0:T(8,128)} %observe.1), calls=%async_computation | async-start | bytes 524288 | tf_op jit(solution)/shard_map/all_to_all | solution.py:310
  6.4 0.0 copy-done.4
  6.4 0.1 copy.12.counts_ref
  6.5 0.0 copy-start
  6.5 0.0 copy-start.2
  6.5 0.0 copy-start.3
  6.5 2.1 %copy.17 = bf16[4,8,8,1536]{3,2,0,1:T(8,128)(2,1)} copy(bf16[4,8,8,1536]{3,2,1,0:T(8,128)(2,1)} %bitcast.37) | data formatting | bytes 1572864 | tf_op jit(solution)/shard_map/reshape | solution.py:312
  8.7 0.0 copy-start.1
  8.7 0.0 copy-done
  8.7 0.0 copy-done.2
  8.7 0.0 copy-done.3
  8.7 0.7 copy-done.1
  9.3 0.8 %gather_small.1 = (f32[20,128]{1,0:T(8,128)S(1)}, f32[2,20,1536]{2,1,0:T(8,128)S(1)}, f32[6,128]{1,0:T(8,128)S(1)}) custom-call(s32[2,1]{1,0:T(2,128)S(1)} %copy.12.counts_ref, s32[2,4]{1,0:T(2,128)S(1)} %copy-done.1, s32[20,2,96]{2,1,0:T(2,128)S(1)} %bitcast.35, f32[2,128]{1,0:T(2,128)S(1)} %copy-done.2, f32[2,128]{1,0:T(2,128)S(1)} %copy-done.3), custom_call_target="tpu_custom_call" | custom-call | tf_op jit(solution)/shard_map/gather_small/pallas_call | solution.py:223
  10.2 3.8 %all-to-all-done.shared_ref = f32[8,32,256]{2,1,0:T(8,128)S(1)} async-done(((f32[8,32,256]{2,1,0:T(8,128)}), f32[8,32,256]{2,1,0:T(8,128)S(1)}, u32[]{:S(2)}, u32[]{:S(2)}) %all-to-all-start) | async-done | bytes 262176 | tf_op jit(solution)/shard_map/all_to_all | solution.py:310
  14.0 3.5 %all-to-all-start.1 = ((bf16[8,32,1536]{2,1,0:T(8,128)(2,1)}), bf16[8,32,1536]{2,1,0:T(8,128)(2,1)S(1)}, u32[]{:S(2)}, u32[]{:S(2)}) async-start(bf16[8,32,1536]{2,1,0:T(8,128)(2,1)} %bitcast.32), calls=%async_computation.1 | async-start | bytes 1572864 | tf_op jit(solution)/shard_map/all_to_all | solution.py:317
  17.5 0.2 first_pack.1.own_ref.refs_1_
  17.7 3.8 %collective-permute-start.1 = (bf16[272,128]{1,0:T(8,128)(2,1)S(1)}, bf16[272,128]{1,0:T(8,128)(2,1)S(1)}, u32[]{:S(2)}, u32[]{:S(2)}) collective-permute-start(bf16[272,128]{1,0:T(8,128)(2,1)S(1)} %first_pack.1.own_ref.refs_1_), channel_id=1, source_target_pairs={{0,8},{1,17},{2,10},{3,19},{4,12},{5,21},{6,14},{7,23},{8,0},{9,25... | collective-permute-start | bytes 208904 | tf_op jit(solution)/shard_map/ppermute | solution.py:289
  21.5 8.9 %collective-permute-start = (bf16[272,128]{1,0:T(8,128)(2,1)S(1)}, bf16[272,128]{1,0:T(8,128)(2,1)S(1)}, u32[]{:S(2)}, u32[]{:S(2)}) collective-permute-start(bf16[272,128]{1,0:T(8,128)(2,1)S(1)} %first_pack.1.own_ref.refs_1_), channel_id=1, source_target_pairs={{9,17},{11,19},{13,21},{15,23},{16,32},{17,9},{18,34},{19,11},{20,... | collective-permute-start | bytes 208904 | tf_op jit(solution)/shard_map/ppermute | solution.py:289
  30.4 0.7 collective-permute-start.2
  31.1 0.0 collective-permute-done.1
  31.1 1.9 %collective-permute-done = bf16[272,128]{1,0:T(8,128)(2,1)S(1)} collective-permute-done((bf16[272,128]{1,0:T(8,128)(2,1)S(1)}, bf16[272,128]{1,0:T(8,128)(2,1)S(1)}, u32[]{:S(2)}, u32[]{:S(2)}) %collective-permute-start) | collective-permute-done | bytes 69664 | tf_op jit(solution)/shard_map/ppermute | solution.py:289
  33.0 0.0 collective-permute-done.2
  33.1 2.0 %all_gather.6.around_ref.refs_2_ = bf16[4,272,128]{2,1,0:T(8,128)(2,1)S(1)} all-gather(bf16[2,272,128]{2,1,0:T(8,128)(2,1)S(1)} %pad_maximum_fusion.1), channel_id=1, replica_groups={{0,1},{2,3},{4,5},{6,7},{8,9},{10,11},{12,13},{14,15},{16,17},{18,19},{..., dimensions={0}, use_global_device_ids=true | all-gather | bytes 417792 | tf_op jit(solution)/shard_map/all_gather | solution.py:303
  35.1 1.0 %second_pack.1.refs_1_ = bf16[272,128]{1,0:T(8,128)(2,1)S(1)} custom-call(f32[20,128]{1,0:T(8,128)S(1)} %get-tuple-element.24.flags_ref, f32[8,32,256]{2,1,0:T(8,128)S(1)} %all-to-all-done.shared_ref, bf16[272,128]{1,0:T(8,128)(2,1)S(1)} %first_pack.1.own_ref.refs_1_, bf16[4,272,128]{2,1,0:T(8,128)(2,1)S(1)} %all_gather.6.around_ref.refs_2_, ...), custom_call_target="tpu_custom_call" | custom-call | tf_op jit(solution)/shard_map/second_pack/pallas_call | solution.py:249
  36.1 0.0 all-to-all-done.1
  36.1 3.8 %collective-permute-start.4 = (bf16[272,128]{1,0:T(8,128)(2,1)S(1)}, bf16[272,128]{1,0:T(8,128)(2,1)S(1)}, u32[]{:S(2)}, u32[]{:S(2)}) collective-permute-start(bf16[272,128]{1,0:T(8,128)(2,1)S(1)} %second_pack.1.refs_1_), channel_id=1, source_target_pairs={{0,8},{1,17},{2,10},{3,19},{4,12},{5,21},{6,14},{7,23},{8,0},{9,25... | collective-permute-start | bytes 208904 | tf_op jit(solution)/shard_map/ppermute | solution.py:289
  40.0 4.2 %collective-permute-start.3 = (bf16[272,128]{1,0:T(8,128)(2,1)S(1)}, bf16[272,128]{1,0:T(8,128)(2,1)S(1)}, u32[]{:S(2)}, u32[]{:S(2)}) collective-permute-start(bf16[272,128]{1,0:T(8,128)(2,1)S(1)} %second_pack.1.refs_1_), channel_id=1, source_target_pairs={{9,17},{11,19},{13,21},{15,23},{16,32},{17,9},{18,34},{19,11},{20,... | collective-permute-start | bytes 208904 | tf_op jit(solution)/shard_map/ppermute | solution.py:289
  44.2 0.7 collective-permute-start.5
  44.9 2.5 %update.2.refs_3_ = bf16[256,1536]{1,0:T(8,128)(2,1)S(1)} custom-call(f32[2,20,1536]{2,1,0:T(8,128)S(1)} %get-tuple-element.23.refs_0_, bf16[272,128]{1,0:T(8,128)(2,1)S(1)} %first_pack.1.own_ref.refs_1_, bf16[4,272,128]{2,1,0:T(8,128)(2,1)S(1)} %all_gather.6.around_ref.refs_2_, bf16[256,1536]{1,0:T(8,128)(2,1)S(1)} %bitcast.33), custom_call_target="tpu_custom_call" | custom-call | tf_op jit(solution)/shard_map/update/pallas_call | solution.py:260
  47.3 0.0 collective-permute-done.4
  47.4 1.8 %collective-permute-done.3 = bf16[272,128]{1,0:T(8,128)(2,1)S(1)} collective-permute-done((bf16[272,128]{1,0:T(8,128)(2,1)S(1)}, bf16[272,128]{1,0:T(8,128)(2,1)S(1)}, u32[]{:S(2)}, u32[]{:S(2)}) %collective-permute-start.3) | collective-permute-done | bytes 69664 | tf_op jit(solution)/shard_map/ppermute | solution.py:289
  49.2 0.0 collective-permute-done.5
  49.3 2.0 %all_gather.7.refs_2_ = bf16[4,272,128]{2,1,0:T(8,128)(2,1)S(1)} all-gather(bf16[2,272,128]{2,1,0:T(8,128)(2,1)S(1)} %pad_maximum_fusion.3), channel_id=1, replica_groups={{0,1},{2,3},{4,5},{6,7},{8,9},{10,11},{12,13},{14,15},{16,17},{18,19},{..., dimensions={0}, use_global_device_ids=true | all-gather | bytes 417792 | tf_op jit(solution)/shard_map/all_gather | solution.py:303
  51.3 2.5 %update.3 = bf16[256,1536]{1,0:T(8,128)(2,1)S(1)} custom-call(f32[2,20,1536]{2,1,0:T(8,128)S(1)} %get-tuple-element.23.refs_0_, bf16[272,128]{1,0:T(8,128)(2,1)S(1)} %second_pack.1.refs_1_, bf16[4,272,128]{2,1,0:T(8,128)(2,1)S(1)} %all_gather.7.refs_2_, bf16[256,1536]{1,0:T(8,128)(2,1)S(1)} %update.2.refs_3_), custom_call_target="tpu_custom_call" | custom-call | tf_op jit(solution)/shard_map/update/pallas_call | solution.py:260
  53.8 17.5 %all_to_all.15 = bf16[8,32,1536]{2,1,0:T(8,128)(2,1)S(1)} all-to-all(bf16[8,32,1536]{2,1,0:T(8,128)(2,1)S(1)} %bitcast.34), channel_id=1, replica_groups=mesh['space'=64,'mem'=8] {'mem'}, dimensions={0} | all-to-all | bytes 1572864 | tf_op jit(solution)/shard_map/all_to_all | solution.py:328
  71.3 0.9 %copy.15 = bf16[8,4,8,1536]{3,2,0,1:T(8,128)(2,1)} copy(bf16[8,4,8,1536]{3,2,1,0:T(8,128)(2,1)S(1)} %bitcast.36) | data formatting | bytes 1572864 | tf_op jit(solution)/shard_map/reshape | solution.py:331
  (8 shorter events, 0.1 us)
Async XLA Ops:
  2.1 4.3 %copy-start.4 = (s32[2,1]{0,1:T(1,128)S(1)}, s32[2,1]{0,1:T(1,128)}, u32[]{:S(2)}) copy-start(s32[2,1]{0,1:T(1,128)} %param.8) | copy-start | bytes 28
  2.1 11.9 %all-to-all-start = ((f32[8,32,256]{2,1,0:T(8,128)}), f32[8,32,256]{2,1,0:T(8,128)S(1)}, u32[]{:S(2)}, u32[]{:S(2)}) async-start(f32[8,32,256]{2,1,0:T(8,128)} %observe.1), calls=%async_computation | async-start | bytes 524288 | tf_op jit(solution)/shard_map/all_to_all | solution.py:310
  6.5 2.1 %copy-start = (s32[2,96,20]{1,0,2:T(2,128)S(1)}, s32[2,96,20]{1,0,2:T(2,128)}, u32[]{:S(2)}) copy-start(s32[2,96,20]{1,0,2:T(2,128)} %param.13) | copy-start | bytes 46084
  6.5 2.1 %copy-start.2 = (f32[2,128]{1,0:T(2,128)S(1)}, f32[2,128]{1,0:T(2,128)}, u32[]{:S(2)}) copy-start(f32[2,128]{1,0:T(2,128)} %observed_ref.1) | copy-start | bytes 3076
  6.5 2.1 %copy-start.3 = (f32[2,128]{1,0:T(2,128)S(1)}, f32[2,128]{1,0:T(2,128)}, u32[]{:S(2)}) copy-start(f32[2,128]{1,0:T(2,128)} %error_ref.1) | copy-start | bytes 3076
  8.7 0.7 copy-start.1
  14.0 22.1 %all-to-all-start.1 = ((bf16[8,32,1536]{2,1,0:T(8,128)(2,1)}), bf16[8,32,1536]{2,1,0:T(8,128)(2,1)S(1)}, u32[]{:S(2)}, u32[]{:S(2)}) async-start(bf16[8,32,1536]{2,1,0:T(8,128)(2,1)} %bitcast.32), calls=%async_computation.1 | async-start | bytes 1572864 | tf_op jit(solution)/shard_map/all_to_all | solution.py:317
  17.7 13.4 %collective-permute-start.1 = (bf16[272,128]{1,0:T(8,128)(2,1)S(1)}, bf16[272,128]{1,0:T(8,128)(2,1)S(1)}, u32[]{:S(2)}, u32[]{:S(2)}) collective-permute-start(bf16[272,128]{1,0:T(8,128)(2,1)S(1)} %first_pack.1.own_ref.refs_1_), channel_id=1, source_target_pairs={{0,8},{1,17},{2,10},{3,19},{4,12},{5,21},{6,14},{7,23},{8,0},{9,25... | collective-permute-start | bytes 208904 | tf_op jit(solution)/shard_map/ppermute | solution.py:289
  21.5 11.5 %collective-permute-start = (bf16[272,128]{1,0:T(8,128)(2,1)S(1)}, bf16[272,128]{1,0:T(8,128)(2,1)S(1)}, u32[]{:S(2)}, u32[]{:S(2)}) collective-permute-start(bf16[272,128]{1,0:T(8,128)(2,1)S(1)} %first_pack.1.own_ref.refs_1_), channel_id=1, source_target_pairs={{9,17},{11,19},{13,21},{15,23},{16,32},{17,9},{18,34},{19,11},{20,... | collective-permute-start | bytes 208904 | tf_op jit(solution)/shard_map/ppermute | solution.py:289
  30.4 2.6 %collective-permute-start.2 = (bf16[272,128]{1,0:T(8,128)(2,1)S(1)}, bf16[272,128]{1,0:T(8,128)(2,1)S(1)}, u32[]{:S(2)}, u32[]{:S(2)}) collective-permute-start(bf16[272,128]{1,0:T(8,128)(2,1)S(1)} %first_pack.1.own_ref.refs_1_), channel_id=1, source_target_pairs={{64,72},{65,81},{66,74},{67,83},{68,76},{69,85},{70,78},{71,87},{7... | collective-permute-start | bytes 208904 | tf_op jit(solution)/shard_map/ppermute | solution.py:289
  36.1 11.2 %collective-permute-start.4 = (bf16[272,128]{1,0:T(8,128)(2,1)S(1)}, bf16[272,128]{1,0:T(8,128)(2,1)S(1)}, u32[]{:S(2)}, u32[]{:S(2)}) collective-permute-start(bf16[272,128]{1,0:T(8,128)(2,1)S(1)} %second_pack.1.refs_1_), channel_id=1, source_target_pairs={{0,8},{1,17},{2,10},{3,19},{4,12},{5,21},{6,14},{7,23},{8,0},{9,25... | collective-permute-start | bytes 208904 | tf_op jit(solution)/shard_map/ppermute | solution.py:289
  40.0 9.2 %collective-permute-start.3 = (bf16[272,128]{1,0:T(8,128)(2,1)S(1)}, bf16[272,128]{1,0:T(8,128)(2,1)S(1)}, u32[]{:S(2)}, u32[]{:S(2)}) collective-permute-start(bf16[272,128]{1,0:T(8,128)(2,1)S(1)} %second_pack.1.refs_1_), channel_id=1, source_target_pairs={{9,17},{11,19},{13,21},{15,23},{16,32},{17,9},{18,34},{19,11},{20,... | collective-permute-start | bytes 208904 | tf_op jit(solution)/shard_map/ppermute | solution.py:289
  44.2 5.0 %collective-permute-start.5 = (bf16[272,128]{1,0:T(8,128)(2,1)S(1)}, bf16[272,128]{1,0:T(8,128)(2,1)S(1)}, u32[]{:S(2)}, u32[]{:S(2)}) collective-permute-start(bf16[272,128]{1,0:T(8,128)(2,1)S(1)} %second_pack.1.refs_1_), channel_id=1, source_target_pairs={{64,72},{65,81},{66,74},{67,83},{68,76},{69,85},{70,78},{71,87},{7... | collective-permute-start | bytes 208904 | tf_op jit(solution)/shard_map/ppermute | solution.py:289

commit v7 on v6

--- a/solution.py
+++ b/solution.py
@@ -128,17 +128,18 @@
     prior = members_of(shared_ref, 1)
     high, low = two_parts(prior - jnp.sum(prior, 0, keepdims=True) / MEMBERS)
     deviation = jnp.concatenate([high, low], 1).astype(BF16)
-    change = jnp.zeros((PACK, 2 * SLOTS), F32)
-    for offset, pack_ref in window(own_ref, around_ref):
-        pack = pack_ref[...]
-        covariance = dot(turned(pack), deviation, ((1,), (0,)))
-        covariance = covariance[:, :SLOTS] + covariance[:, SLOTS:]
-        kept = []
+    tiles = [(offset, pack_ref[...]) for offset, pack_ref in window(own_ref, around_ref)]
+    covariance = dot(jnp.concatenate([turned(pack) for _, pack in tiles], 0), deviation, ((1,), (0,)))
+    covariance = covariance[:, :SLOTS] + covariance[:, SLOTS:]
+    kept = []
+    for n, (offset, _) in enumerate(tiles):
         for c in range(CAPB):
             column = (offset + 2) * CAPB + c
-            kept.append(covariance[c * OB : (c + 1) * OB] * flags_ref[column : column + 1])
-        high, low = two_parts(jnp.concatenate(kept, 0))
-        change = change + dot(pack, jnp.concatenate([high, low], 1).astype(BF16), ((1,), (0,)))
+            row = n * SLOTS + c * OB
+            kept.append(covariance[row : row + OB] * flags_ref[column : column + 1])
+    high, low = two_parts(jnp.concatenate(kept, 0))
+    parts = jnp.concatenate([high, low], 1).astype(BF16)
+    change = dot(jnp.concatenate([pack for _, pack in tiles], 1), parts, ((1,), (0,)))
     prior = prior + applied(change[:, :SLOTS] + change[:, SLOTS:])
     store_packed(out_ref, prior, slots_ref[3:6])
 
@@ -161,17 +162,18 @@
         buffer = at // step % 2
         values = state_ref[:, at : at + step]
         mean = jnp.sum(values.astype(F32), 0, keepdims=True) / MEMBERS
-        covariance = dot(turned_ref[...], values, ((1,), (0,)))
         for n, (offset, _) in enumerate(tiles):
+            covariance = dot(turned_ref[n * SLOTS : (n + 1) * SLOTS], values, ((1,), (0,)))
             for c in range(CAPB):
                 row = n * SLOTS + c * OB
                 column = (offset + 2) * CAPB + c
                 flags = flags_ref[batch_id, column : column + 1, at : at + step]
                 total = total_ref[row : row + OB]
                 total = jnp.concatenate([total, total], 1)
-                kept = (covariance[row : row + OB] - total * mean) * flags
-                high, low = two_parts(kept)
-                kept_ref[buffer, row : row + OB] = high.astype(BF16)
+                kept = (covariance[c * OB : (c + 1) * OB] - total * mean) * flags
+                high = kept.astype(BF16)
+                low = kept - high.astype(F32)
+                kept_ref[buffer, row : row + OB] = high
                 low_row = row + (SLOTS if n == 4 else 6 * SLOTS)
                 kept_ref[buffer, low_row : low_row + OB] = low.astype(BF16)
 

time: 72.7 us -> 72.4 us (level)
  no operation moved by 1% of the time
where the time goes in v7:
time: 72.4 us; the launch traced here: 71.9 us
  starting transfers between devices  29.9 us (41%)
  blocking collectives  21.5 us (30%)
  Pallas kernels  8.71 us (12%)
  waiting for transfers between devices  7.61 us (11%)
  local copies, waits for them, and re-layouts  3.85 us (5%)
    ppermute x6, starting transfers between devices, swapped(): return lax.ppermute(pack, ('space', 'mem'), pairs)  22.1 us
    all_to_all x1, blocking collectives, per_device(): lax.all_to_all(state.reshape(groups, mem_dev, cells // groups), 'mem', sp...  17.5 us
    pallas_call x2, Pallas kernels, update(): pl.pallas_call(lambda *refs: update_kernel(batch_id, *refs), in_specs=[VM...  4.82 us
    all_to_all x1, starting transfers between devices, per_device(): lax.all_to_all(own_block, 'mem', split_axis=0, concat_axis=0, tiled=True)  4.31 us
    all_gather x2, blocking collectives, chip_shared(): lax.all_gather(received, 'mem', axis=0, axis_index_groups=chips, tiled=True)  4.01 us
    all_to_all x1, waiting for transfers between devices, per_device(): lax.all_to_all(own_block, 'mem', split_axis=0, concat_axis=0, tiled=True)  3.81 us
    ppermute x6, waiting for transfers between devices, swapped(): return lax.ppermute(pack, ('space', 'mem'), pairs)  3.8 us
    all_to_all x1, starting transfers between devices, per_device(): lax.all_to_all(moved, 'mem', split_axis=0, concat_axis=0, tiled=True)  3.55 us
  transfers between devices with their start and end apart: 8, of which 3 were waited for; matrix products, arithmetic and copies ran while one was open for 3% of the time, Pallas kernels for 6%

profile of v7, /device:TPU:24, one launch (start us, length us, event | category | flops | bytes accessed | tf_op | source)
XLA Modules:
  0.0 71.9 jit_solution(15332304225466152751)
XLA Ops:
  0.0 2.1 %observe.1 = f32[8,32,256]{2,1,0:T(8,128)} custom-call(s32[2,4]{1,0:T(2,128)} %index_ref.1, f32[2,4,32,128]{3,2,1,0:T(8,128)} %gate_hbm.1, bf16[32,12288]{1,0:T(8,128)(2,1)} %state_hbm.1), custom_call_target="tpu_custom_call" | custom-call | tf_op jit(solution)/shard_map/observe/pallas_call | solution.py:205
  2.1 0.0 copy-start.4
  2.1 4.3 %all-to-all-start = ((f32[8,32,256]{2,1,0:T(8,128)}), f32[8,32,256]{2,1,0:T(8,128)S(1)}, u32[]{:S(2)}, u32[]{:S(2)}) async-start(f32[8,32,256]{2,1,0:T(8,128)} %observe.1), calls=%async_computation | async-start | bytes 524288 | tf_op jit(solution)/shard_map/all_to_all | solution.py:312
  6.4 0.0 copy-done.4
  6.4 0.1 copy.12.counts_ref
  6.5 0.0 copy-start
  6.5 0.0 copy-start.2
  6.5 0.0 copy-start.3
  6.5 2.1 %copy.17 = bf16[4,8,8,1536]{3,2,0,1:T(8,128)(2,1)} copy(bf16[4,8,8,1536]{3,2,1,0:T(8,128)(2,1)} %bitcast.37) | data formatting | bytes 1572864 | tf_op jit(solution)/shard_map/reshape | solution.py:314
  8.7 0.0 copy-start.1
  8.7 0.0 copy-done
  8.7 0.0 copy-done.2
  8.7 0.0 copy-done.3
  8.7 0.7 copy-done.1
  9.3 0.8 %gather_small.1 = (f32[20,128]{1,0:T(8,128)S(1)}, f32[2,20,1536]{2,1,0:T(8,128)S(1)}, f32[6,128]{1,0:T(8,128)S(1)}) custom-call(s32[2,1]{1,0:T(2,128)S(1)} %copy.12.counts_ref, s32[2,4]{1,0:T(2,128)S(1)} %copy-done.1, s32[20,2,96]{2,1,0:T(2,128)S(1)} %bitcast.35, f32[2,128]{1,0:T(2,128)S(1)} %copy-done.2, f32[2,128]{1,0:T(2,128)S(1)} %copy-done.3), custom_call_target="tpu_custom_call" | custom-call | tf_op jit(solution)/shard_map/gather_small/pallas_call | solution.py:225
  10.2 3.8 %all-to-all-done.shared_ref = f32[8,32,256]{2,1,0:T(8,128)S(1)} async-done(((f32[8,32,256]{2,1,0:T(8,128)}), f32[8,32,256]{2,1,0:T(8,128)S(1)}, u32[]{:S(2)}, u32[]{:S(2)}) %all-to-all-start) | async-done | bytes 262176 | tf_op jit(solution)/shard_map/all_to_all | solution.py:312
  14.0 3.5 %all-to-all-start.1 = ((bf16[8,32,1536]{2,1,0:T(8,128)(2,1)}), bf16[8,32,1536]{2,1,0:T(8,128)(2,1)S(1)}, u32[]{:S(2)}, u32[]{:S(2)}) async-start(bf16[8,32,1536]{2,1,0:T(8,128)(2,1)} %bitcast.32), calls=%async_computation.1 | async-start | bytes 1572864 | tf_op jit(solution)/shard_map/all_to_all | solution.py:319
  17.5 0.2 first_pack.1.own_ref.refs_1_
  17.7 3.8 %collective-permute-start.1 = (bf16[272,128]{1,0:T(8,128)(2,1)S(1)}, bf16[272,128]{1,0:T(8,128)(2,1)S(1)}, u32[]{:S(2)}, u32[]{:S(2)}) collective-permute-start(bf16[272,128]{1,0:T(8,128)(2,1)S(1)} %first_pack.1.own_ref.refs_1_), channel_id=1, source_target_pairs={{0,8},{1,17},{2,10},{3,19},{4,12},{5,21},{6,14},{7,23},{8,0},{9,25... | collective-permute-start | bytes 208904 | tf_op jit(solution)/shard_map/ppermute | solution.py:291
  21.5 8.9 %collective-permute-start = (bf16[272,128]{1,0:T(8,128)(2,1)S(1)}, bf16[272,128]{1,0:T(8,128)(2,1)S(1)}, u32[]{:S(2)}, u32[]{:S(2)}) collective-permute-start(bf16[272,128]{1,0:T(8,128)(2,1)S(1)} %first_pack.1.own_ref.refs_1_), channel_id=1, source_target_pairs={{9,17},{11,19},{13,21},{15,23},{16,32},{17,9},{18,34},{19,11},{20,... | collective-permute-start | bytes 208904 | tf_op jit(solution)/shard_map/ppermute | solution.py:291
  30.4 0.7 collective-permute-start.2
  31.1 0.0 collective-permute-done.1
  31.1 1.9 %collective-permute-done = bf16[272,128]{1,0:T(8,128)(2,1)S(1)} collective-permute-done((bf16[272,128]{1,0:T(8,128)(2,1)S(1)}, bf16[272,128]{1,0:T(8,128)(2,1)S(1)}, u32[]{:S(2)}, u32[]{:S(2)}) %collective-permute-start) | collective-permute-done | bytes 69664 | tf_op jit(solution)/shard_map/ppermute | solution.py:291
  33.0 0.0 collective-permute-done.2
  33.1 2.0 %all_gather.6.around_ref.refs_2_ = bf16[4,272,128]{2,1,0:T(8,128)(2,1)S(1)} all-gather(bf16[2,272,128]{2,1,0:T(8,128)(2,1)S(1)} %pad_maximum_fusion.1), channel_id=1, replica_groups={{0,1},{2,3},{4,5},{6,7},{8,9},{10,11},{12,13},{14,15},{16,17},{18,19},{..., dimensions={0}, use_global_device_ids=true | all-gather | bytes 417792 | tf_op jit(solution)/shard_map/all_gather | solution.py:305
  35.1 0.8 %second_pack.1.refs_1_ = bf16[272,128]{1,0:T(8,128)(2,1)S(1)} custom-call(f32[20,128]{1,0:T(8,128)S(1)} %get-tuple-element.24.flags_ref, f32[8,32,256]{2,1,0:T(8,128)S(1)} %all-to-all-done.shared_ref, bf16[272,128]{1,0:T(8,128)(2,1)S(1)} %first_pack.1.own_ref.refs_1_, bf16[4,272,128]{2,1,0:T(8,128)(2,1)S(1)} %all_gather.6.around_ref.refs_2_, ...), custom_call_target="tpu_custom_call" | custom-call | tf_op jit(solution)/shard_map/second_pack/pallas_call | solution.py:251
  35.9 0.0 all-to-all-done.1
  35.9 3.8 %collective-permute-start.4 = (bf16[272,128]{1,0:T(8,128)(2,1)S(1)}, bf16[272,128]{1,0:T(8,128)(2,1)S(1)}, u32[]{:S(2)}, u32[]{:S(2)}) collective-permute-start(bf16[272,128]{1,0:T(8,128)(2,1)S(1)} %second_pack.1.refs_1_), channel_id=1, source_target_pairs={{0,8},{1,17},{2,10},{3,19},{4,12},{5,21},{6,14},{7,23},{8,0},{9,25... | collective-permute-start | bytes 208904 | tf_op jit(solution)/shard_map/ppermute | solution.py:291
  39.7 4.2 %collective-permute-start.3 = (bf16[272,128]{1,0:T(8,128)(2,1)S(1)}, bf16[272,128]{1,0:T(8,128)(2,1)S(1)}, u32[]{:S(2)}, u32[]{:S(2)}) collective-permute-start(bf16[272,128]{1,0:T(8,128)(2,1)S(1)} %second_pack.1.refs_1_), channel_id=1, source_target_pairs={{9,17},{11,19},{13,21},{15,23},{16,32},{17,9},{18,34},{19,11},{20,... | collective-permute-start | bytes 208904 | tf_op jit(solution)/shard_map/ppermute | solution.py:291
  43.9 0.7 collective-permute-start.5
  44.6 2.4 %update.2.refs_3_ = bf16[256,1536]{1,0:T(8,128)(2,1)S(1)} custom-call(f32[2,20,1536]{2,1,0:T(8,128)S(1)} %get-tuple-element.23.refs_0_, bf16[272,128]{1,0:T(8,128)(2,1)S(1)} %first_pack.1.own_ref.refs_1_, bf16[4,272,128]{2,1,0:T(8,128)(2,1)S(1)} %all_gather.6.around_ref.refs_2_, bf16[256,1536]{1,0:T(8,128)(2,1)S(1)} %bitcast.33), custom_call_target="tpu_custom_call" | custom-call | tf_op jit(solution)/shard_map/update/pallas_call | solution.py:262
  47.0 0.0 collective-permute-done.4
  47.0 1.9 %collective-permute-done.3 = bf16[272,128]{1,0:T(8,128)(2,1)S(1)} collective-permute-done((bf16[272,128]{1,0:T(8,128)(2,1)S(1)}, bf16[272,128]{1,0:T(8,128)(2,1)S(1)}, u32[]{:S(2)}, u32[]{:S(2)}) %collective-permute-start.3) | collective-permute-done | bytes 69664 | tf_op jit(solution)/shard_map/ppermute | solution.py:291
  49.0 0.0 collective-permute-done.5
  49.0 2.0 %all_gather.7.refs_2_ = bf16[4,272,128]{2,1,0:T(8,128)(2,1)S(1)} all-gather(bf16[2,272,128]{2,1,0:T(8,128)(2,1)S(1)} %pad_maximum_fusion.3), channel_id=1, replica_groups={{0,1},{2,3},{4,5},{6,7},{8,9},{10,11},{12,13},{14,15},{16,17},{18,19},{..., dimensions={0}, use_global_device_ids=true | all-gather | bytes 417792 | tf_op jit(solution)/shard_map/all_gather | solution.py:305
  51.0 2.4 %update.3 = bf16[256,1536]{1,0:T(8,128)(2,1)S(1)} custom-call(f32[2,20,1536]{2,1,0:T(8,128)S(1)} %get-tuple-element.23.refs_0_, bf16[272,128]{1,0:T(8,128)(2,1)S(1)} %second_pack.1.refs_1_, bf16[4,272,128]{2,1,0:T(8,128)(2,1)S(1)} %all_gather.7.refs_2_, bf16[256,1536]{1,0:T(8,128)(2,1)S(1)} %update.2.refs_3_), custom_call_target="tpu_custom_call" | custom-call | tf_op jit(solution)/shard_map/update/pallas_call | solution.py:262
  53.4 17.5 %all_to_all.15 = bf16[8,32,1536]{2,1,0:T(8,128)(2,1)S(1)} all-to-all(bf16[8,32,1536]{2,1,0:T(8,128)(2,1)S(1)} %bitcast.34), channel_id=1, replica_groups=mesh['space'=64,'mem'=8] {'mem'}, dimensions={0} | all-to-all | bytes 1572864 | tf_op jit(solution)/shard_map/all_to_all | solution.py:330
  70.9 0.9 %copy.15 = bf16[8,4,8,1536]{3,2,0,1:T(8,128)(2,1)} copy(bf16[8,4,8,1536]{3,2,1,0:T(8,128)(2,1)S(1)} %bitcast.36) | data formatting | bytes 1572864 | tf_op jit(solution)/shard_map/reshape | solution.py:333
  (8 shorter events, 0.1 us)
Async XLA Ops:
  2.1 4.3 %copy-start.4 = (s32[2,1]{0,1:T(1,128)S(1)}, s32[2,1]{0,1:T(1,128)}, u32[]{:S(2)}) copy-start(s32[2,1]{0,1:T(1,128)} %param.8) | copy-start | bytes 28
  2.1 11.9 %all-to-all-start = ((f32[8,32,256]{2,1,0:T(8,128)}), f32[8,32,256]{2,1,0:T(8,128)S(1)}, u32[]{:S(2)}, u32[]{:S(2)}) async-start(f32[8,32,256]{2,1,0:T(8,128)} %observe.1), calls=%async_computation | async-start | bytes 524288 | tf_op jit(solution)/shard_map/all_to_all | solution.py:312
  6.5 2.1 %copy-start = (s32[2,96,20]{1,0,2:T(2,128)S(1)}, s32[2,96,20]{1,0,2:T(2,128)}, u32[]{:S(2)}) copy-start(s32[2,96,20]{1,0,2:T(2,128)} %param.13) | copy-start | bytes 46084
  6.5 2.1 %copy-start.2 = (f32[2,128]{1,0:T(2,128)S(1)}, f32[2,128]{1,0:T(2,128)}, u32[]{:S(2)}) copy-start(f32[2,128]{1,0:T(2,128)} %observed_ref.1) | copy-start | bytes 3076
  6.5 2.1 %copy-start.3 = (f32[2,128]{1,0:T(2,128)S(1)}, f32[2,128]{1,0:T(2,128)}, u32[]{:S(2)}) copy-start(f32[2,128]{1,0:T(2,128)} %error_ref.1) | copy-start | bytes 3076
  8.7 0.7 copy-start.1
  14.0 21.9 %all-to-all-start.1 = ((bf16[8,32,1536]{2,1,0:T(8,128)(2,1)}), bf16[8,32,1536]{2,1,0:T(8,128)(2,1)S(1)}, u32[]{:S(2)}, u32[]{:S(2)}) async-start(bf16[8,32,1536]{2,1,0:T(8,128)(2,1)} %bitcast.32), calls=%async_computation.1 | async-start | bytes 1572864 | tf_op jit(solution)/shard_map/all_to_all | solution.py:319
  17.7 13.4 %collective-permute-start.1 = (bf16[272,128]{1,0:T(8,128)(2,1)S(1)}, bf16[272,128]{1,0:T(8,128)(2,1)S(1)}, u32[]{:S(2)}, u32[]{:S(2)}) collective-permute-start(bf16[272,128]{1,0:T(8,128)(2,1)S(1)} %first_pack.1.own_ref.refs_1_), channel_id=1, source_target_pairs={{0,8},{1,17},{2,10},{3,19},{4,12},{5,21},{6,14},{7,23},{8,0},{9,25... | collective-permute-start | bytes 208904 | tf_op jit(solution)/shard_map/ppermute | solution.py:291
  21.5 11.5 %collective-permute-start = (bf16[272,128]{1,0:T(8,128)(2,1)S(1)}, bf16[272,128]{1,0:T(8,128)(2,1)S(1)}, u32[]{:S(2)}, u32[]{:S(2)}) collective-permute-start(bf16[272,128]{1,0:T(8,128)(2,1)S(1)} %first_pack.1.own_ref.refs_1_), channel_id=1, source_target_pairs={{9,17},{11,19},{13,21},{15,23},{16,32},{17,9},{18,34},{19,11},{20,... | collective-permute-start | bytes 208904 | tf_op jit(solution)/shard_map/ppermute | solution.py:291
  30.4 2.6 %collective-permute-start.2 = (bf16[272,128]{1,0:T(8,128)(2,1)S(1)}, bf16[272,128]{1,0:T(8,128)(2,1)S(1)}, u32[]{:S(2)}, u32[]{:S(2)}) collective-permute-start(bf16[272,128]{1,0:T(8,128)(2,1)S(1)} %first_pack.1.own_ref.refs_1_), channel_id=1, source_target_pairs={{64,72},{65,81},{66,74},{67,83},{68,76},{69,85},{70,78},{71,87},{7... | collective-permute-start | bytes 208904 | tf_op jit(solution)/shard_map/ppermute | solution.py:291
  35.9 11.1 %collective-permute-start.4 = (bf16[272,128]{1,0:T(8,128)(2,1)S(1)}, bf16[272,128]{1,0:T(8,128)(2,1)S(1)}, u32[]{:S(2)}, u32[]{:S(2)}) collective-permute-start(bf16[272,128]{1,0:T(8,128)(2,1)S(1)} %second_pack.1.refs_1_), channel_id=1, source_target_pairs={{0,8},{1,17},{2,10},{3,19},{4,12},{5,21},{6,14},{7,23},{8,0},{9,25... | collective-permute-start | bytes 208904 | tf_op jit(solution)/shard_map/ppermute | solution.py:291
  39.7 9.2 %collective-permute-start.3 = (bf16[272,128]{1,0:T(8,128)(2,1)S(1)}, bf16[272,128]{1,0:T(8,128)(2,1)S(1)}, u32[]{:S(2)}, u32[]{:S(2)}) collective-permute-start(bf16[272,128]{1,0:T(8,128)(2,1)S(1)} %second_pack.1.refs_1_), channel_id=1, source_target_pairs={{9,17},{11,19},{13,21},{15,23},{16,32},{17,9},{18,34},{19,11},{20,... | collective-permute-start | bytes 208904 | tf_op jit(solution)/shard_map/ppermute | solution.py:291
  43.9 5.0 %collective-permute-start.5 = (bf16[272,128]{1,0:T(8,128)(2,1)S(1)}, bf16[272,128]{1,0:T(8,128)(2,1)S(1)}, u32[]{:S(2)}, u32[]{:S(2)}) collective-permute-start(bf16[272,128]{1,0:T(8,128)(2,1)S(1)} %second_pack.1.refs_1_), channel_id=1, source_target_pairs={{64,72},{65,81},{66,74},{67,83},{68,76},{69,85},{70,78},{71,87},{7... | collective-permute-start | bytes 208904 | tf_op jit(solution)/shard_map/ppermute | solution.py:291

commit v8 on v7

--- a/solution.py
+++ b/solution.py
@@ -12,6 +12,7 @@
 CAPB = 4
 SLOTS = 128
 BATCHES = 2
+ROWS = 48
 PACK = 272
 F32 = jnp.float32
 BF16 = jnp.bfloat16
@@ -48,8 +49,13 @@
     prior = jnp.zeros((mem_dev, BATCHES * SLOTS), F32)
     for n in range(BATCHES * CAPB):
         prior = jnp.where(lane_block == n, each[n * mem_dev : (n + 1) * mem_dev], prior)
+    mean = jnp.sum(prior, 0, keepdims=True) / mem_dev
+    mean_high, mean_low = two_parts(mean)
+    row = lax.broadcasted_iota(jnp.int32, (ROWS - mem_dev, BATCHES * SLOTS), 0)
+    tail = jnp.where(row == 0, mean_high, jnp.where(row == 1, mean_low, 0.0))
+    block = jnp.concatenate([prior - mean, tail], 0).astype(BF16)
     for g in range(out_ref.shape[0]):
-        out_ref[g] = prior
+        out_ref[g] = block
 
 
 def gather_small_kernel(counts_ref, index_ref, mask_ref, observed_ref, error_ref, between_ref, own_ref, slots_ref):
@@ -72,9 +78,14 @@
 
 
 def members_of(shared_ref, batch_id):
-    groups, mem_dev, _ = shared_ref.shape
+    groups = shared_ref.shape[0]
+    mem_dev = MEMBERS // groups
     lanes = slice(batch_id * SLOTS, (batch_id + 1) * SLOTS)
-    return shared_ref[:, :, lanes].reshape(groups * mem_dev, SLOTS)
+    parts = []
+    for g in range(groups):
+        block = shared_ref[g, :, lanes].astype(F32)
+        parts.append(block[:mem_dev] + (block[mem_dev : mem_dev + 1] + block[mem_dev + 1 : mem_dev + 2]))
+    return jnp.concatenate(parts, 0)
 
 
 def store_packed(out_ref, prior, slots):
@@ -206,7 +217,7 @@
         observe_kernel,
         in_specs=[anywhere, anywhere, anywhere],
         out_specs=VM,
-        out_shape=jax.ShapeDtypeStruct((groups, mem_dev, BATCHES * SLOTS), F32),
+        out_shape=jax.ShapeDtypeStruct((groups, ROWS, BATCHES * SLOTS), BF16),
         scratch_shapes=[
             pltpu.SMEM(block_index.shape, jnp.int32),
             pltpu.VMEM(gate_operator.shape, F32),

time: 72.4 us -> 71.7 us (level)
  no operation moved by 1% of the time
where the time goes in v8:
time: 71.7 us; the launch traced here: 71.2 us
  starting transfers between devices  29.9 us (42%)
  blocking collectives  21.5 us (30%)
  Pallas kernels  8.71 us (12%)
  waiting for transfers between devices  6.91 us (10%)
  local copies, waits for them, and re-layouts  3.85 us (5%)
    ppermute x6, starting transfers between devices, swapped(): return lax.ppermute(pack, ('space', 'mem'), pairs)  22.1 us
    all_to_all x1, blocking collectives, per_device(): lax.all_to_all(state.reshape(groups, mem_dev, cells // groups), 'mem', sp...  17.5 us
    pallas_call x2, Pallas kernels, update(): pl.pallas_call(lambda *refs: update_kernel(batch_id, *refs), in_specs=[VM...  4.82 us
    all_to_all x1, starting transfers between devices, per_device(): lax.all_to_all(own_block, 'mem', split_axis=0, concat_axis=0, tiled=True)  4.31 us
    all_gather x2, blocking collectives, chip_shared(): lax.all_gather(received, 'mem', axis=0, axis_index_groups=chips, tiled=True)  4.01 us
    ppermute x6, waiting for transfers between devices, swapped(): return lax.ppermute(pack, ('space', 'mem'), pairs)  3.8 us
    all_to_all x1, starting transfers between devices, per_device(): lax.all_to_all(moved, 'mem', split_axis=0, concat_axis=0, tiled=True)  3.55 us
    all_to_all x1, waiting for transfers between devices, per_device(): lax.all_to_all(own_block, 'mem', split_axis=0, concat_axis=0, tiled=True)  3.11 us
  transfers between devices with their start and end apart: 8, of which 3 were waited for; matrix products, arithmetic and copies ran while one was open for 3% of the time, Pallas kernels for 6%

profile of v8, /device:TPU:24, one launch (start us, length us, event | category | flops | bytes accessed | tf_op | source)
XLA Modules:
  0.0 71.2 jit_solution(6654007496860452184)
XLA Ops:
  0.0 2.1 %observe.1 = bf16[8,48,256]{2,1,0:T(8,128)(2,1)} custom-call(s32[2,4]{1,0:T(2,128)} %index_ref.1, f32[2,4,32,128]{3,2,1,0:T(8,128)} %gate_hbm.1, bf16[32,12288]{1,0:T(8,128)(2,1)} %state_hbm.1), custom_call_target="tpu_custom_call" | custom-call | tf_op jit(solution)/shard_map/observe/pallas_call | solution.py:216
  2.1 0.0 copy-start.4
  2.1 4.3 %all-to-all-start = ((bf16[8,48,256]{2,1,0:T(8,128)(2,1)}), bf16[8,48,256]{2,1,0:T(8,128)(2,1)S(1)}, u32[]{:S(2)}, u32[]{:S(2)}) async-start(bf16[8,48,256]{2,1,0:T(8,128)(2,1)} %observe.1), calls=%async_computation | async-start | bytes 393216 | tf_op jit(solution)/shard_map/all_to_all | solution.py:323
  6.4 0.0 copy-done.4
  6.4 0.1 copy.12.counts_ref
  6.5 0.0 copy-start
  6.5 0.0 copy-start.2
  6.5 0.0 copy-start.3
  6.5 2.1 %copy.17 = bf16[4,8,8,1536]{3,2,0,1:T(8,128)(2,1)} copy(bf16[4,8,8,1536]{3,2,1,0:T(8,128)(2,1)} %bitcast.36) | data formatting | bytes 1572864 | tf_op jit(solution)/shard_map/reshape | solution.py:325
  8.7 0.0 copy-start.1
  8.7 0.0 copy-done
  8.7 0.0 copy-done.2
  8.7 0.0 copy-done.3
  8.7 0.7 copy-done.1
  9.3 0.8 %gather_small.1 = (f32[20,128]{1,0:T(8,128)S(1)}, f32[2,20,1536]{2,1,0:T(8,128)S(1)}, f32[6,128]{1,0:T(8,128)S(1)}) custom-call(s32[2,1]{1,0:T(2,128)S(1)} %copy.12.counts_ref, s32[2,4]{1,0:T(2,128)S(1)} %copy-done.1, s32[20,2,96]{2,1,0:T(2,128)S(1)} %bitcast.35, f32[2,128]{1,0:T(2,128)S(1)} %copy-done.2, f32[2,128]{1,0:T(2,128)S(1)} %copy-done.3), custom_call_target="tpu_custom_call" | custom-call | tf_op jit(solution)/shard_map/gather_small/pallas_call | solution.py:236
  10.2 3.1 %all-to-all-done.shared_ref = bf16[8,48,256]{2,1,0:T(8,128)(2,1)S(1)} async-done(((bf16[8,48,256]{2,1,0:T(8,128)(2,1)}), bf16[8,48,256]{2,1,0:T(8,128)(2,1)S(1)}, u32[]{:S(2)}, u32[]{:S(2)}) %all-to-all-start) | async-done | bytes 196640 | tf_op jit(solution)/shard_map/all_to_all | solution.py:323
  13.3 3.5 %all-to-all-start.1 = ((bf16[8,32,1536]{2,1,0:T(8,128)(2,1)}), bf16[8,32,1536]{2,1,0:T(8,128)(2,1)S(1)}, u32[]{:S(2)}, u32[]{:S(2)}) async-start(bf16[8,32,1536]{2,1,0:T(8,128)(2,1)} %bitcast.32), calls=%async_computation.1 | async-start | bytes 1572864 | tf_op jit(solution)/shard_map/all_to_all | solution.py:330
  16.8 0.2 first_pack.1.own_ref.refs_1_
  17.0 3.8 %collective-permute-start.1 = (bf16[272,128]{1,0:T(8,128)(2,1)S(1)}, bf16[272,128]{1,0:T(8,128)(2,1)S(1)}, u32[]{:S(2)}, u32[]{:S(2)}) collective-permute-start(bf16[272,128]{1,0:T(8,128)(2,1)S(1)} %first_pack.1.own_ref.refs_1_), channel_id=1, source_target_pairs={{0,8},{1,17},{2,10},{3,19},{4,12},{5,21},{6,14},{7,23},{8,0},{9,25... | collective-permute-start | bytes 208904 | tf_op jit(solution)/shard_map/ppermute | solution.py:302
  20.8 8.9 %collective-permute-start = (bf16[272,128]{1,0:T(8,128)(2,1)S(1)}, bf16[272,128]{1,0:T(8,128)(2,1)S(1)}, u32[]{:S(2)}, u32[]{:S(2)}) collective-permute-start(bf16[272,128]{1,0:T(8,128)(2,1)S(1)} %first_pack.1.own_ref.refs_1_), channel_id=1, source_target_pairs={{9,17},{11,19},{13,21},{15,23},{16,32},{17,9},{18,34},{19,11},{20,... | collective-permute-start | bytes 208904 | tf_op jit(solution)/shard_map/ppermute | solution.py:302
  29.7 0.7 collective-permute-start.2
  30.4 0.0 collective-permute-done.1
  30.4 1.9 %collective-permute-done = bf16[272,128]{1,0:T(8,128)(2,1)S(1)} collective-permute-done((bf16[272,128]{1,0:T(8,128)(2,1)S(1)}, bf16[272,128]{1,0:T(8,128)(2,1)S(1)}, u32[]{:S(2)}, u32[]{:S(2)}) %collective-permute-start) | collective-permute-done | bytes 69664 | tf_op jit(solution)/shard_map/ppermute | solution.py:302
  32.3 0.0 collective-permute-done.2
  32.4 2.0 %all_gather.6.around_ref.refs_2_ = bf16[4,272,128]{2,1,0:T(8,128)(2,1)S(1)} all-gather(bf16[2,272,128]{2,1,0:T(8,128)(2,1)S(1)} %pad_maximum_fusion.1), channel_id=1, replica_groups={{0,1},{2,3},{4,5},{6,7},{8,9},{10,11},{12,13},{14,15},{16,17},{18,19},{..., dimensions={0}, use_global_device_ids=true | all-gather | bytes 417792 | tf_op jit(solution)/shard_map/all_gather | solution.py:316
  34.4 0.8 %second_pack.1.refs_1_ = bf16[272,128]{1,0:T(8,128)(2,1)S(1)} custom-call(f32[20,128]{1,0:T(8,128)S(1)} %get-tuple-element.24.flags_ref, bf16[8,48,256]{2,1,0:T(8,128)(2,1)S(1)} %all-to-all-done.shared_ref, bf16[272,128]{1,0:T(8,128)(2,1)S(1)} %first_pack.1.own_ref.refs_1_, bf16[4,272,128]{2,1,0:T(8,128)(2,1)S(1)} %all_gather.6.around_ref.refs_2_, ...), custom_call_target="tpu_custom_call" | custom-call | tf_op jit(solution)/shard_map/second_pack/pallas_call | solution.py:262
  35.2 0.0 all-to-all-done.1
  35.2 3.8 %collective-permute-start.4 = (bf16[272,128]{1,0:T(8,128)(2,1)S(1)}, bf16[272,128]{1,0:T(8,128)(2,1)S(1)}, u32[]{:S(2)}, u32[]{:S(2)}) collective-permute-start(bf16[272,128]{1,0:T(8,128)(2,1)S(1)} %second_pack.1.refs_1_), channel_id=1, source_target_pairs={{0,8},{1,17},{2,10},{3,19},{4,12},{5,21},{6,14},{7,23},{8,0},{9,25... | collective-permute-start | bytes 208904 | tf_op jit(solution)/shard_map/ppermute | solution.py:302
  39.0 4.2 %collective-permute-start.3 = (bf16[272,128]{1,0:T(8,128)(2,1)S(1)}, bf16[272,128]{1,0:T(8,128)(2,1)S(1)}, u32[]{:S(2)}, u32[]{:S(2)}) collective-permute-start(bf16[272,128]{1,0:T(8,128)(2,1)S(1)} %second_pack.1.refs_1_), channel_id=1, source_target_pairs={{9,17},{11,19},{13,21},{15,23},{16,32},{17,9},{18,34},{19,11},{20,... | collective-permute-start | bytes 208904 | tf_op jit(solution)/shard_map/ppermute | solution.py:302
  43.2 0.7 collective-permute-start.5
  43.9 2.4 %update.2.refs_3_ = bf16[256,1536]{1,0:T(8,128)(2,1)S(1)} custom-call(f32[2,20,1536]{2,1,0:T(8,128)S(1)} %get-tuple-element.23.refs_0_, bf16[272,128]{1,0:T(8,128)(2,1)S(1)} %first_pack.1.own_ref.refs_1_, bf16[4,272,128]{2,1,0:T(8,128)(2,1)S(1)} %all_gather.6.around_ref.refs_2_, bf16[256,1536]{1,0:T(8,128)(2,1)S(1)} %bitcast.33), custom_call_target="tpu_custom_call" | custom-call | tf_op jit(solution)/shard_map/update/pallas_call | solution.py:273
  46.3 0.0 collective-permute-done.4
  46.3 1.9 %collective-permute-done.3 = bf16[272,128]{1,0:T(8,128)(2,1)S(1)} collective-permute-done((bf16[272,128]{1,0:T(8,128)(2,1)S(1)}, bf16[272,128]{1,0:T(8,128)(2,1)S(1)}, u32[]{:S(2)}, u32[]{:S(2)}) %collective-permute-start.3) | collective-permute-done | bytes 69664 | tf_op jit(solution)/shard_map/ppermute | solution.py:302
  48.3 0.0 collective-permute-done.5
  48.3 2.0 %all_gather.7.refs_2_ = bf16[4,272,128]{2,1,0:T(8,128)(2,1)S(1)} all-gather(bf16[2,272,128]{2,1,0:T(8,128)(2,1)S(1)} %pad_maximum_fusion.3), channel_id=1, replica_groups={{0,1},{2,3},{4,5},{6,7},{8,9},{10,11},{12,13},{14,15},{16,17},{18,19},{..., dimensions={0}, use_global_device_ids=true | all-gather | bytes 417792 | tf_op jit(solution)/shard_map/all_gather | solution.py:316
  50.3 2.4 %update.3 = bf16[256,1536]{1,0:T(8,128)(2,1)S(1)} custom-call(f32[2,20,1536]{2,1,0:T(8,128)S(1)} %get-tuple-element.23.refs_0_, bf16[272,128]{1,0:T(8,128)(2,1)S(1)} %second_pack.1.refs_1_, bf16[4,272,128]{2,1,0:T(8,128)(2,1)S(1)} %all_gather.7.refs_2_, bf16[256,1536]{1,0:T(8,128)(2,1)S(1)} %update.2.refs_3_), custom_call_target="tpu_custom_call" | custom-call | tf_op jit(solution)/shard_map/update/pallas_call | solution.py:273
  52.7 17.5 %all_to_all.15 = bf16[8,32,1536]{2,1,0:T(8,128)(2,1)S(1)} all-to-all(bf16[8,32,1536]{2,1,0:T(8,128)(2,1)S(1)} %bitcast.34), channel_id=1, replica_groups=mesh['space'=64,'mem'=8] {'mem'}, dimensions={0} | all-to-all | bytes 1572864 | tf_op jit(solution)/shard_map/all_to_all | solution.py:341
  70.2 0.9 %copy.15 = bf16[8,4,8,1536]{3,2,0,1:T(8,128)(2,1)} copy(bf16[8,4,8,1536]{3,2,1,0:T(8,128)(2,1)S(1)} %bitcast.37) | data formatting | bytes 1572864 | tf_op jit(solution)/shard_map/reshape | solution.py:344
  (8 shorter events, 0.1 us)
Async XLA Ops:
  2.1 4.3 %copy-start.4 = (s32[2,1]{0,1:T(1,128)S(1)}, s32[2,1]{0,1:T(1,128)}, u32[]{:S(2)}) copy-start(s32[2,1]{0,1:T(1,128)} %param.8) | copy-start | bytes 28
  2.1 11.2 %all-to-all-start = ((bf16[8,48,256]{2,1,0:T(8,128)(2,1)}), bf16[8,48,256]{2,1,0:T(8,128)(2,1)S(1)}, u32[]{:S(2)}, u32[]{:S(2)}) async-start(bf16[8,48,256]{2,1,0:T(8,128)(2,1)} %observe.1), calls=%async_computation | async-start | bytes 393216 | tf_op jit(solution)/shard_map/all_to_all | solution.py:323
  6.5 2.1 %copy-start = (s32[2,96,20]{1,0,2:T(2,128)S(1)}, s32[2,96,20]{1,0,2:T(2,128)}, u32[]{:S(2)}) copy-start(s32[2,96,20]{1,0,2:T(2,128)} %param.13) | copy-start | bytes 46084
  6.5 2.1 %copy-start.2 = (f32[2,128]{1,0:T(2,128)S(1)}, f32[2,128]{1,0:T(2,128)}, u32[]{:S(2)}) copy-start(f32[2,128]{1,0:T(2,128)} %observed_ref.1) | copy-start | bytes 3076
  6.5 2.1 %copy-start.3 = (f32[2,128]{1,0:T(2,128)S(1)}, f32[2,128]{1,0:T(2,128)}, u32[]{:S(2)}) copy-start(f32[2,128]{1,0:T(2,128)} %error_ref.1) | copy-start | bytes 3076
  8.7 0.7 copy-start.1
  13.3 21.9 %all-to-all-start.1 = ((bf16[8,32,1536]{2,1,0:T(8,128)(2,1)}), bf16[8,32,1536]{2,1,0:T(8,128)(2,1)S(1)}, u32[]{:S(2)}, u32[]{:S(2)}) async-start(bf16[8,32,1536]{2,1,0:T(8,128)(2,1)} %bitcast.32), calls=%async_computation.1 | async-start | bytes 1572864 | tf_op jit(solution)/shard_map/all_to_all | solution.py:330
  17.0 13.4 %collective-permute-start.1 = (bf16[272,128]{1,0:T(8,128)(2,1)S(1)}, bf16[272,128]{1,0:T(8,128)(2,1)S(1)}, u32[]{:S(2)}, u32[]{:S(2)}) collective-permute-start(bf16[272,128]{1,0:T(8,128)(2,1)S(1)} %first_pack.1.own_ref.refs_1_), channel_id=1, source_target_pairs={{0,8},{1,17},{2,10},{3,19},{4,12},{5,21},{6,14},{7,23},{8,0},{9,25... | collective-permute-start | bytes 208904 | tf_op jit(solution)/shard_map/ppermute | solution.py:302
  20.8 11.5 %collective-permute-start = (bf16[272,128]{1,0:T(8,128)(2,1)S(1)}, bf16[272,128]{1,0:T(8,128)(2,1)S(1)}, u32[]{:S(2)}, u32[]{:S(2)}) collective-permute-start(bf16[272,128]{1,0:T(8,128)(2,1)S(1)} %first_pack.1.own_ref.refs_1_), channel_id=1, source_target_pairs={{9,17},{11,19},{13,21},{15,23},{16,32},{17,9},{18,34},{19,11},{20,... | collective-permute-start | bytes 208904 | tf_op jit(solution)/shard_map/ppermute | solution.py:302
  29.7 2.6 %collective-permute-start.2 = (bf16[272,128]{1,0:T(8,128)(2,1)S(1)}, bf16[272,128]{1,0:T(8,128)(2,1)S(1)}, u32[]{:S(2)}, u32[]{:S(2)}) collective-permute-start(bf16[272,128]{1,0:T(8,128)(2,1)S(1)} %first_pack.1.own_ref.refs_1_), channel_id=1, source_target_pairs={{64,72},{65,81},{66,74},{67,83},{68,76},{69,85},{70,78},{71,87},{7... | collective-permute-start | bytes 208904 | tf_op jit(solution)/shard_map/ppermute | solution.py:302
  35.2 11.1 %collective-permute-start.4 = (bf16[272,128]{1,0:T(8,128)(2,1)S(1)}, bf16[272,128]{1,0:T(8,128)(2,1)S(1)}, u32[]{:S(2)}, u32[]{:S(2)}) collective-permute-start(bf16[272,128]{1,0:T(8,128)(2,1)S(1)} %second_pack.1.refs_1_), channel_id=1, source_target_pairs={{0,8},{1,17},{2,10},{3,19},{4,12},{5,21},{6,14},{7,23},{8,0},{9,25... | collective-permute-start | bytes 208904 | tf_op jit(solution)/shard_map/ppermute | solution.py:302
  39.0 9.2 %collective-permute-start.3 = (bf16[272,128]{1,0:T(8,128)(2,1)S(1)}, bf16[272,128]{1,0:T(8,128)(2,1)S(1)}, u32[]{:S(2)}, u32[]{:S(2)}) collective-permute-start(bf16[272,128]{1,0:T(8,128)(2,1)S(1)} %second_pack.1.refs_1_), channel_id=1, source_target_pairs={{9,17},{11,19},{13,21},{15,23},{16,32},{17,9},{18,34},{19,11},{20,... | collective-permute-start | bytes 208904 | tf_op jit(solution)/shard_map/ppermute | solution.py:302
  43.2 5.0 %collective-permute-start.5 = (bf16[272,128]{1,0:T(8,128)(2,1)S(1)}, bf16[272,128]{1,0:T(8,128)(2,1)S(1)}, u32[]{:S(2)}, u32[]{:S(2)}) collective-permute-start(bf16[272,128]{1,0:T(8,128)(2,1)S(1)} %second_pack.1.refs_1_), channel_id=1, source_target_pairs={{64,72},{65,81},{66,74},{67,83},{68,76},{69,85},{70,78},{71,87},{7... | collective-permute-start | bytes 208904 | tf_op jit(solution)/shard_map/ppermute | solution.py:302

commit v9 on v8

--- a/solution.py
+++ b/solution.py
@@ -156,7 +156,7 @@
 
 
 def update_kernel(
-    batch_id, flags_ref, own_ref, around_ref, state_ref, out_ref, turned_ref, packs_ref, total_ref, kept_ref
+    batch_id, flags_ref, own_ref, around_ref, state_ref, mean_ref, out_ref, turned_ref, packs_ref, total_ref, kept_ref
 ):
     tiles = window(own_ref, around_ref)
     for n, (_, pack_ref) in enumerate(tiles):
@@ -172,7 +172,10 @@
     def covariances(at):
         buffer = at // step % 2
         values = state_ref[:, at : at + step]
-        mean = jnp.sum(values.astype(F32), 0, keepdims=True) / MEMBERS
+        if batch_id == 0:
+            mean = jnp.sum(values.astype(F32), 0, keepdims=True) / MEMBERS
+        else:
+            mean = mean_ref[0:1, at : at + step]
         for n, (offset, _) in enumerate(tiles):
             covariance = dot(turned_ref[n * SLOTS : (n + 1) * SLOTS], values, ((1,), (0,)))
             for c in range(CAPB):
@@ -196,7 +199,10 @@
             + dot(packs_ref[:, :last], kept_ref[buffer, 6 * SLOTS :], ((1,), (0,)))
         )
         values = state_ref[:, at : at + step].astype(F32)
-        out_ref[:, at : at + step] = (values + applied(change)).astype(BF16)
+        values = (values + applied(change)).astype(BF16)
+        out_ref[:, at : at + step] = values
+        if batch_id == 0:
+            mean_ref[:, at : at + step] = jnp.sum(values.astype(F32), 0, keepdims=True) / MEMBERS
 
     covariances(0)
     for at in range(0, cells, step):
@@ -269,12 +275,22 @@
     )(flags, shared, own, around, slots)
 
 
-def update(batch_id, flags, own, around, state):
-    return pl.pallas_call(
-        lambda *refs: update_kernel(batch_id, *refs),
-        in_specs=[VM, VM, VM, VM],
-        out_specs=VM,
-        out_shape=jax.ShapeDtypeStruct(state.shape, BF16),
+def first_update_kernel(flags_ref, own_ref, around_ref, state_ref, out_ref, mean_ref, *scratch):
+    update_kernel(0, flags_ref, own_ref, around_ref, state_ref, mean_ref, out_ref, *scratch)
+
+
+def second_update_kernel(flags_ref, own_ref, around_ref, state_ref, mean_ref, out_ref, *scratch):
+    update_kernel(1, flags_ref, own_ref, around_ref, state_ref, mean_ref, out_ref, *scratch)
+
+
+def update(kernel, flags, own, around, state, *mean):
+    shape = jax.ShapeDtypeStruct(state.shape, BF16)
+    means = jax.ShapeDtypeStruct((1, state.shape[1]), F32)
+    return pl.pallas_call(
+        kernel,
+        in_specs=[VM] * (4 + len(mean)),
+        out_specs=VM if mean else [VM, VM],
+        out_shape=shape if mean else [shape, means],
         scratch_shapes=[
             pltpu.VMEM((5 * SLOTS, MEMBERS), BF16),
             pltpu.VMEM((PACK, 6 * SLOTS), BF16),
@@ -283,7 +299,7 @@
         ],
         compiler_params=PARAMS,
         name="update",
-    )(flags, own, around, state)
+    )(flags, own, around, state, *mean)
 
 
 def partner_of(tile, m, across):
@@ -334,10 +350,10 @@
     next_pack = second_pack(between, shared, pack, around, slots)
     next_pack, state = lax.optimization_barrier((next_pack, state))
     received = passed_around(next_pack)
-    state = update(0, flags, pack, around, state)
-    received, state = lax.optimization_barrier((received, state))
+    state, mean = update(first_update_kernel, flags, pack, around, state)
+    received, state, mean = lax.optimization_barrier((received, state, mean))
     next_around = chip_shared(received)
-    state = update(1, flags, next_pack, next_around, state)
+    state = update(second_update_kernel, flags, next_pack, next_around, state, mean)
     parts = lax.all_to_all(
         state.reshape(groups, mem_dev, cells // groups), "mem", split_axis=0, concat_axis=0, tiled=True
     )

time: 71.7 us -> 71.6 us (level)
  no operation moved by 1% of the time
where the time goes in v9:
time: 71.6 us; the launch traced here: 71.1 us
  starting transfers between devices  29.9 us (42%)
  blocking collectives  21.5 us (30%)
  Pallas kernels  8.77 us (12%)
  waiting for transfers between devices  6.78 us (9%)
  local copies, waits for them, and re-layouts  3.85 us (5%)
    ppermute x6, starting transfers between devices, swapped(): return lax.ppermute(pack, ('space', 'mem'), pairs)  22.1 us
    all_to_all x1, blocking collectives, per_device(): lax.all_to_all(state.reshape(groups, mem_dev, cells // groups), 'mem', sp...  17.5 us
    pallas_call x2, Pallas kernels, update(): pl.pallas_call(kernel, in_specs=[VM] * (4 + len(mean)), out_specs=VM if m...  4.89 us
    all_to_all x1, starting transfers between devices, per_device(): lax.all_to_all(own_block, 'mem', split_axis=0, concat_axis=0, tiled=True)  4.31 us
    all_gather x2, blocking collectives, chip_shared(): lax.all_gather(received, 'mem', axis=0, axis_index_groups=chips, tiled=True)  4.01 us
    ppermute x6, waiting for transfers between devices, swapped(): return lax.ppermute(pack, ('space', 'mem'), pairs)  3.67 us
    all_to_all x1, starting transfers between devices, per_device(): lax.all_to_all(moved, 'mem', split_axis=0, concat_axis=0, tiled=True)  3.55 us
    all_to_all x1, waiting for transfers between devices, per_device(): lax.all_to_all(own_block, 'mem', split_axis=0, concat_axis=0, tiled=True)  3.11 us
  transfers between devices with their start and end apart: 8, of which 3 were waited for; matrix products, arithmetic and copies ran while one was open for 3% of the time, Pallas kernels for 6%

profile of v9, /device:TPU:24, one launch (start us, length us, event | category | flops | bytes accessed | tf_op | source)
XLA Modules:
  0.0 71.1 jit_solution(8374429473792025799)
XLA Ops:
  0.0 2.1 %observe.1 = bf16[8,48,256]{2,1,0:T(8,128)(2,1)} custom-call(s32[2,4]{1,0:T(2,128)} %index_ref.1, f32[2,4,32,128]{3,2,1,0:T(8,128)} %gate_hbm.1, bf16[32,12288]{1,0:T(8,128)(2,1)} %state_hbm.1), custom_call_target="tpu_custom_call" | custom-call | tf_op jit(solution)/shard_map/observe/pallas_call | solution.py:222
  2.1 0.0 copy-start.4
  2.1 4.3 %all-to-all-start = ((bf16[8,48,256]{2,1,0:T(8,128)(2,1)}), bf16[8,48,256]{2,1,0:T(8,128)(2,1)S(1)}, u32[]{:S(2)}, u32[]{:S(2)}) async-start(bf16[8,48,256]{2,1,0:T(8,128)(2,1)} %observe.1), calls=%async_computation | async-start | bytes 393216 | tf_op jit(solution)/shard_map/all_to_all | solution.py:339
  6.4 0.0 copy-done.4
  6.4 0.1 copy.12.counts_ref
  6.5 0.0 copy-start
  6.5 0.0 copy-start.2
  6.5 0.0 copy-start.3
  6.5 2.1 %copy.17 = bf16[4,8,8,1536]{3,2,0,1:T(8,128)(2,1)} copy(bf16[4,8,8,1536]{3,2,1,0:T(8,128)(2,1)} %bitcast.36) | data formatting | bytes 1572864 | tf_op jit(solution)/shard_map/reshape | solution.py:341
  8.7 0.0 copy-start.1
  8.7 0.0 copy-done
  8.7 0.0 copy-done.2
  8.7 0.0 copy-done.3
  8.7 0.7 copy-done.1
  9.3 0.8 %gather_small.1 = (f32[20,128]{1,0:T(8,128)S(1)}, f32[2,20,1536]{2,1,0:T(8,128)S(1)}, f32[6,128]{1,0:T(8,128)S(1)}) custom-call(s32[2,1]{1,0:T(2,128)S(1)} %copy.12.counts_ref, s32[2,4]{1,0:T(2,128)S(1)} %copy-done.1, s32[20,2,96]{2,1,0:T(2,128)S(1)} %bitcast.35, f32[2,128]{1,0:T(2,128)S(1)} %copy-done.2, f32[2,128]{1,0:T(2,128)S(1)} %copy-done.3), custom_call_target="tpu_custom_call" | custom-call | tf_op jit(solution)/shard_map/gather_small/pallas_call | solution.py:242
  10.2 3.1 %all-to-all-done.shared_ref = bf16[8,48,256]{2,1,0:T(8,128)(2,1)S(1)} async-done(((bf16[8,48,256]{2,1,0:T(8,128)(2,1)}), bf16[8,48,256]{2,1,0:T(8,128)(2,1)S(1)}, u32[]{:S(2)}, u32[]{:S(2)}) %all-to-all-start) | async-done | bytes 196640 | tf_op jit(solution)/shard_map/all_to_all | solution.py:339
  13.3 3.5 %all-to-all-start.1 = ((bf16[8,32,1536]{2,1,0:T(8,128)(2,1)}), bf16[8,32,1536]{2,1,0:T(8,128)(2,1)S(1)}, u32[]{:S(2)}, u32[]{:S(2)}) async-start(bf16[8,32,1536]{2,1,0:T(8,128)(2,1)} %bitcast.32), calls=%async_computation.1 | async-start | bytes 1572864 | tf_op jit(solution)/shard_map/all_to_all | solution.py:346
  16.8 0.2 first_pack.1.own_ref
  17.0 3.8 %collective-permute-start.1 = (bf16[272,128]{1,0:T(8,128)(2,1)S(1)}, bf16[272,128]{1,0:T(8,128)(2,1)S(1)}, u32[]{:S(2)}, u32[]{:S(2)}) collective-permute-start(bf16[272,128]{1,0:T(8,128)(2,1)S(1)} %first_pack.1.own_ref), channel_id=1, source_target_pairs={{0,8},{1,17},{2,10},{3,19},{4,12},{5,21},{6,14},{7,23},{8,0},{9,25... | collective-permute-start | bytes 208904 | tf_op jit(solution)/shard_map/ppermute | solution.py:318
  20.8 8.9 %collective-permute-start = (bf16[272,128]{1,0:T(8,128)(2,1)S(1)}, bf16[272,128]{1,0:T(8,128)(2,1)S(1)}, u32[]{:S(2)}, u32[]{:S(2)}) collective-permute-start(bf16[272,128]{1,0:T(8,128)(2,1)S(1)} %first_pack.1.own_ref), channel_id=1, source_target_pairs={{9,17},{11,19},{13,21},{15,23},{16,32},{17,9},{18,34},{19,11},{20,... | collective-permute-start | bytes 208904 | tf_op jit(solution)/shard_map/ppermute | solution.py:318
  29.7 0.7 collective-permute-start.2
  30.4 0.0 collective-permute-done.1
  30.4 1.9 %collective-permute-done = bf16[272,128]{1,0:T(8,128)(2,1)S(1)} collective-permute-done((bf16[272,128]{1,0:T(8,128)(2,1)S(1)}, bf16[272,128]{1,0:T(8,128)(2,1)S(1)}, u32[]{:S(2)}, u32[]{:S(2)}) %collective-permute-start) | collective-permute-done | bytes 69664 | tf_op jit(solution)/shard_map/ppermute | solution.py:318
  32.3 0.0 collective-permute-done.2
  32.4 2.0 %all_gather.6.around_ref = bf16[4,272,128]{2,1,0:T(8,128)(2,1)S(1)} all-gather(bf16[2,272,128]{2,1,0:T(8,128)(2,1)S(1)} %pad_maximum_fusion.1), channel_id=1, replica_groups={{0,1},{2,3},{4,5},{6,7},{8,9},{10,11},{12,13},{14,15},{16,17},{18,19},{..., dimensions={0}, use_global_device_ids=true | all-gather | bytes 417792 | tf_op jit(solution)/shard_map/all_gather | solution.py:332
  34.4 0.8 %second_pack.1.own_ref = bf16[272,128]{1,0:T(8,128)(2,1)S(1)} custom-call(f32[20,128]{1,0:T(8,128)S(1)} %get-tuple-element.27.flags_ref, bf16[8,48,256]{2,1,0:T(8,128)(2,1)S(1)} %all-to-all-done.shared_ref, bf16[272,128]{1,0:T(8,128)(2,1)S(1)} %first_pack.1.own_ref, bf16[4,272,128]{2,1,0:T(8,128)(2,1)S(1)} %all_gather.6.around_ref, ...), custom_call_target="tpu_custom_call" | custom-call | tf_op jit(solution)/shard_map/second_pack/pallas_call | solution.py:268
  35.2 0.0 all-to-all-done.1
  35.2 3.8 %collective-permute-start.4 = (bf16[272,128]{1,0:T(8,128)(2,1)S(1)}, bf16[272,128]{1,0:T(8,128)(2,1)S(1)}, u32[]{:S(2)}, u32[]{:S(2)}) collective-permute-start(bf16[272,128]{1,0:T(8,128)(2,1)S(1)} %second_pack.1.own_ref), channel_id=1, source_target_pairs={{0,8},{1,17},{2,10},{3,19},{4,12},{5,21},{6,14},{7,23},{8,0},{9,25... | collective-permute-start | bytes 208904 | tf_op jit(solution)/shard_map/ppermute | solution.py:318
  39.0 4.2 %collective-permute-start.3 = (bf16[272,128]{1,0:T(8,128)(2,1)S(1)}, bf16[272,128]{1,0:T(8,128)(2,1)S(1)}, u32[]{:S(2)}, u32[]{:S(2)}) collective-permute-start(bf16[272,128]{1,0:T(8,128)(2,1)S(1)} %second_pack.1.own_ref), channel_id=1, source_target_pairs={{9,17},{11,19},{13,21},{15,23},{16,32},{17,9},{18,34},{19,11},{20,... | collective-permute-start | bytes 208904 | tf_op jit(solution)/shard_map/ppermute | solution.py:318
  43.2 0.7 collective-permute-start.5
  43.9 2.5 %update.2 = (bf16[256,1536]{1,0:T(8,128)(2,1)S(1)}, f32[1,1536]{1,0:T(1,128)S(1)}) custom-call(f32[2,20,1536]{2,1,0:T(8,128)S(1)} %get-tuple-element.26.flags_ref, bf16[272,128]{1,0:T(8,128)(2,1)S(1)} %first_pack.1.own_ref, bf16[4,272,128]{2,1,0:T(8,128)(2,1)S(1)} %all_gather.6.around_ref, bf16[256,1536]{1,0:T(8,128)(2,1)S(1)} %bitcast.34), custom_call_target="tpu_custom_call" | custom-call | tf_op jit(solution)/shard_map/update/pallas_call | solution.py:289
  46.5 0.0 collective-permute-done.4
  46.5 1.8 %collective-permute-done.3 = bf16[272,128]{1,0:T(8,128)(2,1)S(1)} collective-permute-done((bf16[272,128]{1,0:T(8,128)(2,1)S(1)}, bf16[272,128]{1,0:T(8,128)(2,1)S(1)}, u32[]{:S(2)}, u32[]{:S(2)}) %collective-permute-start.3) | collective-permute-done | bytes 69664 | tf_op jit(solution)/shard_map/ppermute | solution.py:318
  48.3 0.0 collective-permute-done.5
  48.3 2.0 %all_gather.7.around_ref = bf16[4,272,128]{2,1,0:T(8,128)(2,1)S(1)} all-gather(bf16[2,272,128]{2,1,0:T(8,128)(2,1)S(1)} %pad_maximum_fusion.3), channel_id=1, replica_groups={{0,1},{2,3},{4,5},{6,7},{8,9},{10,11},{12,13},{14,15},{16,17},{18,19},{..., dimensions={0}, use_global_device_ids=true | all-gather | bytes 417792 | tf_op jit(solution)/shard_map/all_gather | solution.py:332
  50.3 2.3 %update.3 = bf16[256,1536]{1,0:T(8,128)(2,1)S(1)} custom-call(f32[2,20,1536]{2,1,0:T(8,128)S(1)} %get-tuple-element.26.flags_ref, bf16[272,128]{1,0:T(8,128)(2,1)S(1)} %second_pack.1.own_ref, bf16[4,272,128]{2,1,0:T(8,128)(2,1)S(1)} %all_gather.7.around_ref, bf16[256,1536]{1,0:T(8,128)(2,1)S(1)} %get-tuple-element.35.state_ref, ...), custom_call_target="tpu_custom_call" | custom-call | tf_op jit(solution)/shard_map/update/pallas_call | solution.py:289
  52.7 17.5 %all_to_all.15 = bf16[8,32,1536]{2,1,0:T(8,128)(2,1)S(1)} all-to-all(bf16[8,32,1536]{2,1,0:T(8,128)(2,1)S(1)} %bitcast.33), channel_id=1, replica_groups=mesh['space'=64,'mem'=8] {'mem'}, dimensions={0} | all-to-all | bytes 1572864 | tf_op jit(solution)/shard_map/all_to_all | solution.py:357
  70.2 0.9 %copy.15 = bf16[8,4,8,1536]{3,2,0,1:T(8,128)(2,1)} copy(bf16[8,4,8,1536]{3,2,1,0:T(8,128)(2,1)S(1)} %bitcast.37) | data formatting | bytes 1572864 | tf_op jit(solution)/shard_map/reshape | solution.py:360
  (8 shorter events, 0.1 us)
Async XLA Ops:
  2.1 4.3 %copy-start.4 = (s32[2,1]{0,1:T(1,128)S(1)}, s32[2,1]{0,1:T(1,128)}, u32[]{:S(2)}) copy-start(s32[2,1]{0,1:T(1,128)} %param.8) | copy-start | bytes 28
  2.1 11.2 %all-to-all-start = ((bf16[8,48,256]{2,1,0:T(8,128)(2,1)}), bf16[8,48,256]{2,1,0:T(8,128)(2,1)S(1)}, u32[]{:S(2)}, u32[]{:S(2)}) async-start(bf16[8,48,256]{2,1,0:T(8,128)(2,1)} %observe.1), calls=%async_computation | async-start | bytes 393216 | tf_op jit(solution)/shard_map/all_to_all | solution.py:339
  6.5 2.1 %copy-start = (s32[2,96,20]{1,0,2:T(2,128)S(1)}, s32[2,96,20]{1,0,2:T(2,128)}, u32[]{:S(2)}) copy-start(s32[2,96,20]{1,0,2:T(2,128)} %param.13) | copy-start | bytes 46084
  6.5 2.1 %copy-start.2 = (f32[2,128]{1,0:T(2,128)S(1)}, f32[2,128]{1,0:T(2,128)}, u32[]{:S(2)}) copy-start(f32[2,128]{1,0:T(2,128)} %observed_ref.1) | copy-start | bytes 3076
  6.5 2.1 %copy-start.3 = (f32[2,128]{1,0:T(2,128)S(1)}, f32[2,128]{1,0:T(2,128)}, u32[]{:S(2)}) copy-start(f32[2,128]{1,0:T(2,128)} %error_ref.1) | copy-start | bytes 3076
  8.7 0.7 copy-start.1
  13.3 21.9 %all-to-all-start.1 = ((bf16[8,32,1536]{2,1,0:T(8,128)(2,1)}), bf16[8,32,1536]{2,1,0:T(8,128)(2,1)S(1)}, u32[]{:S(2)}, u32[]{:S(2)}) async-start(bf16[8,32,1536]{2,1,0:T(8,128)(2,1)} %bitcast.32), calls=%async_computation.1 | async-start | bytes 1572864 | tf_op jit(solution)/shard_map/all_to_all | solution.py:346
  17.0 13.4 %collective-permute-start.1 = (bf16[272,128]{1,0:T(8,128)(2,1)S(1)}, bf16[272,128]{1,0:T(8,128)(2,1)S(1)}, u32[]{:S(2)}, u32[]{:S(2)}) collective-permute-start(bf16[272,128]{1,0:T(8,128)(2,1)S(1)} %first_pack.1.own_ref), channel_id=1, source_target_pairs={{0,8},{1,17},{2,10},{3,19},{4,12},{5,21},{6,14},{7,23},{8,0},{9,25... | collective-permute-start | bytes 208904 | tf_op jit(solution)/shard_map/ppermute | solution.py:318
  20.8 11.5 %collective-permute-start = (bf16[272,128]{1,0:T(8,128)(2,1)S(1)}, bf16[272,128]{1,0:T(8,128)(2,1)S(1)}, u32[]{:S(2)}, u32[]{:S(2)}) collective-permute-start(bf16[272,128]{1,0:T(8,128)(2,1)S(1)} %first_pack.1.own_ref), channel_id=1, source_target_pairs={{9,17},{11,19},{13,21},{15,23},{16,32},{17,9},{18,34},{19,11},{20,... | collective-permute-start | bytes 208904 | tf_op jit(solution)/shard_map/ppermute | solution.py:318
  29.7 2.6 %collective-permute-start.2 = (bf16[272,128]{1,0:T(8,128)(2,1)S(1)}, bf16[272,128]{1,0:T(8,128)(2,1)S(1)}, u32[]{:S(2)}, u32[]{:S(2)}) collective-permute-start(bf16[272,128]{1,0:T(8,128)(2,1)S(1)} %first_pack.1.own_ref), channel_id=1, source_target_pairs={{64,72},{65,81},{66,74},{67,83},{68,76},{69,85},{70,78},{71,87},{7... | collective-permute-start | bytes 208904 | tf_op jit(solution)/shard_map/ppermute | solution.py:318
  35.2 11.3 %collective-permute-start.4 = (bf16[272,128]{1,0:T(8,128)(2,1)S(1)}, bf16[272,128]{1,0:T(8,128)(2,1)S(1)}, u32[]{:S(2)}, u32[]{:S(2)}) collective-permute-start(bf16[272,128]{1,0:T(8,128)(2,1)S(1)} %second_pack.1.own_ref), channel_id=1, source_target_pairs={{0,8},{1,17},{2,10},{3,19},{4,12},{5,21},{6,14},{7,23},{8,0},{9,25... | collective-permute-start | bytes 208904 | tf_op jit(solution)/shard_map/ppermute | solution.py:318
  39.0 9.2 %collective-permute-start.3 = (bf16[272,128]{1,0:T(8,128)(2,1)S(1)}, bf16[272,128]{1,0:T(8,128)(2,1)S(1)}, u32[]{:S(2)}, u32[]{:S(2)}) collective-permute-start(bf16[272,128]{1,0:T(8,128)(2,1)S(1)} %second_pack.1.own_ref), channel_id=1, source_target_pairs={{9,17},{11,19},{13,21},{15,23},{16,32},{17,9},{18,34},{19,11},{20,... | collective-permute-start | bytes 208904 | tf_op jit(solution)/shard_map/ppermute | solution.py:318
  43.2 5.0 %collective-permute-start.5 = (bf16[272,128]{1,0:T(8,128)(2,1)S(1)}, bf16[272,128]{1,0:T(8,128)(2,1)S(1)}, u32[]{:S(2)}, u32[]{:S(2)}) collective-permute-start(bf16[272,128]{1,0:T(8,128)(2,1)S(1)} %second_pack.1.own_ref), channel_id=1, source_target_pairs={{64,72},{65,81},{66,74},{67,83},{68,76},{69,85},{70,78},{71,87},{7... | collective-permute-start | bytes 208904 | tf_op jit(solution)/shard_map/ppermute | solution.py:318
